TPU v7x, 32 devices: a whole 2x2x4 slice. The times are simulated.
32 devices in a mesh: row: 16 (over z, x, core), col: 2 (over y).
Axes of the slice: x: 2, y: 2, z: 4, core: 2. Of those that a mesh axis runs over, the one named last changes fastest.
Arguments:
- tokens: bfloat16 [6144, 2560], P('row', 'col'), may hold values from -8 to 8
- dest_row: int32 [6144], P('row'), may hold values from 0 to 14335, as said below
- seq_lens: int32 [16, 4], P('row'), may hold values from 0 to 384, as said below
- cotangent: bfloat16 [14336, 2560], P('row', 'col'), may hold values from -8 to 8
- query_down: float32 [2560, 768], P('row'), may hold values from -0.125 to 0.125
- joint_down: float32 [2560, 288], P('row'), may hold values from -0.125 to 0.125
- query_up: float32 [768, 3840], P('row', 'col'), may hold values from -0.3125 to 0.3125
- joint_up: float32 [256, 5120], P('row', 'col'), may hold values from -0.375 to 0.375
- out_weight: float32 [2560, 2560], P('row', 'col'), may hold values from -2.5 to 2.5
- gate_weight: float32 [2560, 6400], P('row', 'col'), may hold values from -0.125 to 0.125
- up_weight: float32 [2560, 6400], P('row', 'col'), may hold values from -0.125 to 0.125
- down_weight: float32 [2560, 6400], P('row', 'col'), may hold values from -0.625 to 0.625
- norm_gains: float32 [6144], P('row'), may hold values from 0.5 to 1.5
- first_query_down: float32 [2560, 768], P('row'), may hold values from -112 to 112
- first_joint_down: float32 [2560, 288], P('row'), may hold values from -160 to 160
- first_query_up: float32 [768, 3840], P('row', 'col'), may hold values from -56 to 56
- first_joint_up: float32 [256, 5120], P('row', 'col'), may hold values from -56 to 56
- first_out_weight: float32 [2560, 2560], P('row', 'col'), may hold values from -4 to 4
- first_gate_weight: float32 [2560, 6400], P('row', 'col'), may hold values from -28 to 28
- first_up_weight: float32 [2560, 6400], P('row', 'col'), may hold values from -28 to 28
- first_down_weight: float32 [2560, 6400], P('row', 'col'), may hold values from -4 to 4
- first_norm_gains: float32 [6144], P('row'), may hold values from -80 to 80
- second_query_down: float32 [2560, 768], P('row'), may hold values from 1290.24 to 5160.96
- second_joint_down: float32 [2560, 288], P('row'), may hold values from 2887.68 to 11673.6
- second_query_up: float32 [768, 3840], P('row', 'col'), may hold values from 325.632 to 1290.24
- second_joint_up: float32 [256, 5120], P('row', 'col'), may hold values from 325.632 to 1290.24
- second_out_weight: float32 [2560, 2560], P('row', 'col'), may hold values from 0.811008 to 3.2256
- second_gate_weight: float32 [2560, 6400], P('row', 'col'), may hold values from 103.41581 to 412.8768
- second_up_weight: float32 [2560, 6400], P('row', 'col'), may hold values from 103.41581 to 412.8768
- second_down_weight: float32 [2560, 6400], P('row', 'col'), may hold values from 3.231744 to 12.9024
- second_norm_gains: float32 [6144], P('row'), may hold values from 724.992 to 2887.68
Outputs:
- outputs: bfloat16 [14336, 2560], P('row', 'col')
- grad_tokens: bfloat16 [6144, 2560], P('row', 'col')
- grad_query_down: float32 [2560, 768], P('row')
- grad_joint_down: float32 [2560, 288], P('row')
- grad_query_up: float32 [768, 3840], P('row', 'col')
- grad_joint_up: float32 [256, 5120], P('row', 'col')
- grad_out_weight: float32 [2560, 2560], P('row', 'col')
- grad_gate_weight: float32 [2560, 6400], P('row', 'col')
- grad_up_weight: float32 [2560, 6400], P('row', 'col')
- grad_down_weight: float32 [2560, 6400], P('row', 'col')
- grad_norm_gains: float32 [6144], P('row')
- second_query_down_next: float32 [2560, 768], P('row')
- second_joint_down_next: float32 [2560, 288], P('row')
- second_query_up_next: float32 [768, 3840], P('row', 'col')
- second_joint_up_next: float32 [256, 5120], P('row', 'col')
- second_out_weight_next: float32 [2560, 2560], P('row', 'col')
- second_gate_weight_next: float32 [2560, 6400], P('row', 'col')
- second_up_weight_next: float32 [2560, 6400], P('row', 'col')
- second_down_weight_next: float32 [2560, 6400], P('row', 'col')
- second_norm_gains_next: float32 [6144], P('row')
- query_down_next: float32 [2560, 768], P('row')
- joint_down_next: float32 [2560, 288], P('row')
- query_up_next: float32 [768, 3840], P('row', 'col')
- joint_up_next: float32 [256, 5120], P('row', 'col')
- out_weight_next: float32 [2560, 2560], P('row', 'col')
- gate_weight_next: float32 [2560, 6400], P('row', 'col')
- up_weight_next: float32 [2560, 6400], P('row', 'col')
- down_weight_next: float32 [2560, 6400], P('row', 'col')
- norm_gains_next: float32 [6144], P('row')
Inputs may be any that keep to these rules, and one draw needn't show every extreme that they name: `seq_lens`: row g lists the lengths of the sequences of group g in layout order and sums to 384; one row, drawn from the seed, is 384 followed by zeros. `dest_row`: group g owns rows g * 896 to (g + 1) * 896 - 1 of the balanced layout; its sequences stand there in the order of seq_lens row g, each preceded by the fewest empty rows that make its extent a multiple of 128, the last ending at the group's last row, the remaining empty rows before the first. Each token has a distinct row, every occupied row belongs to a token, and the 384 tokens of each device along row hold exactly 24 tokens of every group.
All inputs are finite; a program needn't handle non-finite values.
Results may differ from a plain program's by a relative error of at most 0.03.
Values may be sent and summed in bfloat16 or wider, within the bound.
No kernel may reach another device: no remote copies, remote signals or barrier semaphores. Data moves between devices by JAX's collectives and lax.ppermute only.
A program may use at most 320 MiB of HBM per device.

v0:
```python
import jax
import jax.numpy as jnp
from jax import lax
from jax.sharding import PartitionSpec as P

D = 2560
FF = 6400
HEADS = 40
NOPE = 64
ROPE = 32
VDIM = 64
Q_RANK = 768
KV_RANK = 256
SEQS = 4
BLK = 128
STEP = 10
CAP = 896


EPSILON = 1e-05
RESIDUAL_SCALE = 1.4 / 62**0.5
BETA_ONE = 0.9
BETA_TWO = 0.95
ADAM_EPSILON = 1e-08
DECAY_RATE = 0.1
MASKED = -1e30
FULL_TYPE = jnp.float32
HALF_TYPE = jnp.bfloat16


def layout(lengths):
    padded = (lengths + BLK - 1) // BLK * BLK
    endings = CAP - jnp.sum(padded) + jnp.cumsum(padded)
    starts = endings - lengths
    row_ids = jnp.arange(CAP, dtype=jnp.int32)
    inside = (row_ids[:, None] >= starts[None, :]) & (row_ids[:, None] < endings[None, :])
    labels = jnp.arange(SEQS, dtype=jnp.int32) + 1
    segment = jnp.sum(jnp.where(inside, labels[None, :], 0), axis=1) - 1
    position = jnp.sum(jnp.where(inside, row_ids[:, None] - starts[None, :], 0), axis=1)
    return (segment, position)


def rotary_tables(position):
    frequency = 10000.0 ** (-(jnp.arange(ROPE // 2, dtype=FULL_TYPE) * 2.0 / ROPE))
    angles = position.astype(FULL_TYPE)[:, None] * frequency[None, :]
    cosine = jnp.concatenate([jnp.cos(angles), jnp.cos(angles)], axis=1)
    sine_table = jnp.concatenate([jnp.sin(angles), jnp.sin(angles)], axis=1)
    return (cosine, sine_table)


def rotate_half(values):
    half_width = values.shape[-1] // 2
    return jnp.concatenate([-values[..., half_width:], values[..., :half_width]], axis=-1)


def rotate_back(values):
    half_width = values.shape[-1] // 2
    return jnp.concatenate([values[..., half_width:], -values[..., :half_width]], axis=-1)


def apply_rotary(values, cosine, sine_table):
    return values * cosine + rotate_half(values) * sine_table


def rotary_grad(grad_values, cosine, sine_table):
    return grad_values * cosine + rotate_back(grad_values * sine_table)


def rms_scale(values):
    return lax.rsqrt(jnp.mean(values * values, axis=-1, keepdims=True) + EPSILON)


def rms_backward(grad_normed, values, norm_scale, gain_values):
    weighted = grad_normed * gain_values
    mean_term = jnp.mean(weighted * values, axis=-1, keepdims=True)
    grad_values = norm_scale * weighted - values * norm_scale**3 * mean_term
    grad_gain = jnp.sum(grad_normed * values * norm_scale, axis=0)
    return (grad_values, grad_gain)


def product(left_side, right_side):
    return jnp.dot(left_side, right_side, preferred_element_type=FULL_TYPE)


def contract_rows(left_side, right_side):
    return lax.dot_general(
        left_side, right_side, (((0,), (0,)), ((), ())), preferred_element_type=FULL_TYPE
    )


def times_transposed(left_side, right_side):
    return lax.dot_general(
        left_side, right_side, (((1,), (1,)), ((), ())), preferred_element_type=FULL_TYPE
    )


def split_gains(gains_all):
    gains_wide = gains_all.astype(FULL_TYPE)
    return (
        gains_wide[:D],
        gains_wide[D : 2 * D],
        gains_wide[2 * D : 2 * D + Q_RANK],
        gains_wide[2 * D + Q_RANK :],
    )


def block_scores(block_queries, joint_rows, key_rope, segment, start_row):
    score_scale = (NOPE + ROPE) ** (-0.5)
    key_count = joint_rows.shape[0]
    raw_scores = (
        jnp.einsum(
            "qd,kd->qk",
            block_queries[:, :NOPE],
            joint_rows[:, :NOPE],
            preferred_element_type=FULL_TYPE,
        )
        + jnp.einsum(
            "qd,kd->qk", block_queries[:, NOPE:], key_rope, preferred_element_type=FULL_TYPE
        )
    ) * score_scale
    query_ids = start_row + jnp.arange(block_queries.shape[0], dtype=jnp.int32)
    key_ids = jnp.arange(key_count, dtype=jnp.int32)
    query_segment = segment[start_row : start_row + block_queries.shape[0]]
    valid_pairs = (
        (query_segment[:, None] == segment[None, :key_count])
        & (query_segment[:, None] >= 0)
        & (key_ids[None, :] <= query_ids[:, None])
    )
    return jnp.where(valid_pairs, raw_scores, MASKED)


def attend_head(queries, joint_rows, key_rope, segment):
    half_rows = CAP // 2
    outputs = []
    totals = []
    for block_index in range(2):
        start_row = block_index * half_rows
        key_count = start_row + half_rows
        scores = block_scores(
            queries[start_row:key_count],
            joint_rows[:key_count],
            key_rope[:key_count],
            segment,
            start_row,
        )
        row_max = jnp.max(scores, axis=1, keepdims=True)
        powers = jnp.exp(scores - row_max)
        denominator = jnp.sum(powers, axis=1, keepdims=True)
        weights = (powers / denominator).astype(HALF_TYPE)
        outputs.append(
            jnp.einsum(
                "qk,kd->qd",
                weights,
                joint_rows[:key_count, NOPE:],
                preferred_element_type=FULL_TYPE,
            )
        )
        totals.append((row_max + jnp.log(denominator))[:, 0])
    return (jnp.concatenate(outputs, axis=0).astype(HALF_TYPE), jnp.concatenate(totals, axis=0))


def attend_back(queries, joint_rows, grad_out, log_total, key_rope, segment):
    half_rows = CAP // 2
    score_scale = (NOPE + ROPE) ** (-0.5)
    grad_queries = []
    grad_joint = jnp.zeros((CAP, NOPE + VDIM), FULL_TYPE)
    grad_rope = jnp.zeros((CAP, ROPE), FULL_TYPE)
    for block_index in range(2):
        start_row = block_index * half_rows
        key_count = start_row + half_rows
        block_queries = queries[start_row:key_count]
        scores = block_scores(
            block_queries, joint_rows[:key_count], key_rope[:key_count], segment, start_row
        )
        prob_rows = jnp.exp(scores - log_total[start_row:key_count, None])
        block_grad = grad_out[start_row:key_count]
        grad_values = jnp.einsum(
            "qk,qd->kd", prob_rows.astype(HALF_TYPE), block_grad, preferred_element_type=FULL_TYPE
        )
        grad_probs = jnp.einsum(
            "qd,kd->qk", block_grad, joint_rows[:key_count, NOPE:], preferred_element_type=FULL_TYPE
        )
        delta_terms = jnp.sum(prob_rows * grad_probs, axis=1, keepdims=True)
        grad_scores = (prob_rows * (grad_probs - delta_terms)).astype(HALF_TYPE)
        grad_query_nope = (
            jnp.einsum(
                "qk,kd->qd",
                grad_scores,
                joint_rows[:key_count, :NOPE],
                preferred_element_type=FULL_TYPE,
            )
            * score_scale
        )
        grad_query_rope = (
            jnp.einsum(
                "qk,kd->qd", grad_scores, key_rope[:key_count], preferred_element_type=FULL_TYPE
            )
            * score_scale
        )
        grad_key_nope = (
            jnp.einsum(
                "qk,qd->kd", grad_scores, block_queries[:, :NOPE], preferred_element_type=FULL_TYPE
            )
            * score_scale
        )
        grad_key_rope = (
            jnp.einsum(
                "qk,qd->kd", grad_scores, block_queries[:, NOPE:], preferred_element_type=FULL_TYPE
            )
            * score_scale
        )
        grad_queries.append(jnp.concatenate([grad_query_nope, grad_query_rope], axis=1))
        grad_joint = grad_joint.at[:key_count].add(
            jnp.concatenate([grad_key_nope, grad_values], axis=1)
        )
        grad_rope = grad_rope.at[:key_count].add(grad_key_rope)
    return (jnp.concatenate(grad_queries, axis=0), grad_joint, grad_rope)


def learning_rates():
    return (
        3.0 * D ** (-0.5),
        3.0 * D ** (-0.5),
        3.0 * (Q_RANK // 2) ** (-0.5),
        3.0 * KV_RANK ** (-0.5),
        3.0 * max(HEADS * VDIM // 512, 1) ** (-0.5),
        3.0 * D ** (-0.5),
        3.0 * D ** (-0.5),
        3.0 * max(FF // 80, 1) ** (-0.5),
        0.6,
    )


def adam_update(weight_old, grad_value, first_old, second_old, step_rate):
    first_new = BETA_ONE * first_old + (1.0 - BETA_ONE) * grad_value
    second_new = BETA_TWO * second_old + (1.0 - BETA_TWO) * grad_value * grad_value
    first_hat = first_new / (1.0 - BETA_ONE**STEP)
    second_hat = second_new / (1.0 - BETA_TWO**STEP)
    weight_new = weight_old - step_rate * (
        first_hat / (jnp.sqrt(second_hat) + ADAM_EPSILON) + DECAY_RATE * weight_old
    )
    return (second_new, weight_new)


def body(
    tokens,
    dest_row,
    seq_lens,
    cotangent,
    query_down,
    joint_down,
    query_up,
    joint_up,
    out_weight,
    gate_weight,
    up_weight,
    down_weight,
    norm_gains,
    first_query_down,
    first_joint_down,
    first_query_up,
    first_joint_up,
    first_out_weight,
    first_gate_weight,
    first_up_weight,
    first_down_weight,
    first_norm_gains,
    second_query_down,
    second_joint_down,
    second_query_up,
    second_joint_up,
    second_out_weight,
    second_gate_weight,
    second_up_weight,
    second_down_weight,
    second_norm_gains,
):
    params = (
        query_down,
        joint_down,
        query_up,
        joint_up,
        out_weight,
        gate_weight,
        up_weight,
        down_weight,
        norm_gains,
    )
    firsts = (
        first_query_down,
        first_joint_down,
        first_query_up,
        first_joint_up,
        first_out_weight,
        first_gate_weight,
        first_up_weight,
        first_down_weight,
        first_norm_gains,
    )
    seconds = (
        second_query_down,
        second_joint_down,
        second_query_up,
        second_joint_up,
        second_out_weight,
        second_gate_weight,
        second_up_weight,
        second_down_weight,
        second_norm_gains,
    )
    col_count = lax.axis_size("col")
    col_index = lax.axis_index("col")
    local_heads = HEADS // col_count
    width_share = D // col_count
    token_count = tokens.shape[0]
    col_start = col_index * width_share
    target = dest_row // CAP
    local_rows = dest_row - target * CAP
    sort_order = jnp.argsort(target, stable=True)
    arrived, arrived_rows = (
        lax.all_to_all(tokens[sort_order], "row", split_axis=0, concat_axis=0, tiled=True),
        lax.all_to_all(local_rows[sort_order], "row", split_axis=0, concat_axis=0, tiled=True),
    )
    segment, position = layout(seq_lens[0])
    cosine_pad, sine_pad = rotary_tables(position)
    cosine = cosine_pad[arrived_rows]
    sine_table = sine_pad[arrived_rows]

    def to_padded(values):
        return jnp.zeros((CAP,) + values.shape[1:], values.dtype).at[arrived_rows].set(values)

    gathered = (
        lax.all_gather(query_down.astype(HALF_TYPE), "row", axis=0, tiled=True),
        lax.all_gather(joint_down.astype(HALF_TYPE), "row", axis=0, tiled=True),
        lax.all_gather(query_up.astype(HALF_TYPE), "row", axis=0, tiled=True),
        lax.all_gather(joint_up.astype(HALF_TYPE), "row", axis=0, tiled=True),
        lax.all_gather(out_weight.astype(HALF_TYPE), "row", axis=0, tiled=True),
        lax.all_gather(gate_weight.astype(HALF_TYPE), "row", axis=0, tiled=True),
        lax.all_gather(up_weight.astype(HALF_TYPE), "row", axis=0, tiled=True),
        lax.all_gather(down_weight.astype(HALF_TYPE), "row", axis=0, tiled=True),
        lax.all_gather(norm_gains.astype(HALF_TYPE), "row", axis=0, tiled=True),
    )
    (
        query_down_all,
        joint_down_all,
        query_up_all,
        joint_up_all,
        out_all,
        gate_all,
        up_all,
        down_all,
        gains_all,
    ) = gathered
    gain_one, gain_two, gain_query, gain_joint = split_gains(gains_all)
    features = lax.all_gather(arrived, "col", axis=1, tiled=True)
    inputs_full = features.astype(FULL_TYPE)
    scale_one = rms_scale(inputs_full)
    normed_one = (inputs_full * scale_one * gain_one).astype(HALF_TYPE)
    query_latent = product(normed_one, query_down_all)
    joint_latent = product(normed_one, joint_down_all)
    scale_query = rms_scale(query_latent)
    query_normed = (query_latent * scale_query * gain_query).astype(HALF_TYPE)
    compressed_raw = joint_latent[:, :KV_RANK]
    scale_joint = rms_scale(compressed_raw)
    compressed = (compressed_raw * scale_joint * gain_joint).astype(HALF_TYPE)
    key_rope = apply_rotary(joint_latent[:, KV_RANK:], cosine, sine_table).astype(HALF_TYPE)
    query_full = product(query_normed, query_up_all).reshape(token_count, local_heads, NOPE + ROPE)
    query_rot = jnp.concatenate(
        [
            query_full[..., :NOPE],
            apply_rotary(query_full[..., NOPE:], cosine[:, None, :], sine_table[:, None, :]),
        ],
        axis=-1,
    ).astype(HALF_TYPE)
    joint_full = (
        product(compressed, joint_up_all)
        .astype(HALF_TYPE)
        .reshape(token_count, local_heads, NOPE + VDIM)
    )
    query_pad = jnp.swapaxes(to_padded(query_rot), 0, 1)
    joint_pad = jnp.swapaxes(to_padded(joint_full), 0, 1)
    rope_pad = to_padded(key_rope)
    attended_pad, log_totals = lax.map(
        lambda head_pair: attend_head(head_pair[0], head_pair[1], rope_pad, segment),
        (query_pad, joint_pad),
    )
    attended = jnp.swapaxes(attended_pad[:, arrived_rows], 0, 1).reshape(
        token_count, local_heads * VDIM
    )
    branch = lax.psum_scatter(
        times_transposed(attended, out_all), "col", scatter_dimension=1, tiled=True
    )
    residual = arrived.astype(FULL_TYPE) + RESIDUAL_SCALE * branch
    residual_full = lax.all_gather(residual, "col", axis=1, tiled=True)
    scale_two = rms_scale(residual_full)
    normed_two = (residual_full * scale_two * gain_two).astype(HALF_TYPE)
    gate_rows = product(normed_two, gate_all)
    up_rows = product(normed_two, up_all)
    activated = (jax.nn.silu(gate_rows) * up_rows).astype(HALF_TYPE)
    feed_forward = lax.psum_scatter(
        times_transposed(activated, down_all).astype(jnp.bfloat16),
        "col",
        scatter_dimension=1,
        tiled=True,
    ).astype(jnp.float32)
    output_rows = residual + RESIDUAL_SCALE * feed_forward
    output_pad = (
        jnp.zeros((CAP, width_share), HALF_TYPE).at[arrived_rows].set(output_rows.astype(HALF_TYPE))
    )
    back_weights = (
        lax.all_gather(query_down.astype(HALF_TYPE), "row", axis=0, tiled=True),
        lax.all_gather(joint_down.astype(HALF_TYPE), "row", axis=0, tiled=True),
        lax.all_gather(query_up.astype(HALF_TYPE), "row", axis=0, tiled=True),
        lax.all_gather(joint_up.astype(HALF_TYPE), "row", axis=0, tiled=True),
        lax.all_gather(out_weight.astype(HALF_TYPE), "row", axis=0, tiled=True),
        lax.all_gather(gate_weight.astype(HALF_TYPE), "row", axis=0, tiled=True),
        lax.all_gather(up_weight.astype(HALF_TYPE), "row", axis=0, tiled=True),
        lax.all_gather(down_weight.astype(HALF_TYPE), "row", axis=0, tiled=True),
        lax.all_gather(norm_gains.astype(HALF_TYPE), "row", axis=0, tiled=True),
    )
    (
        query_down_back,
        joint_down_back,
        query_up_back,
        joint_up_back,
        out_back,
        gate_back,
        up_back,
        down_back,
        gains_back,
    ) = back_weights
    gain_one_back, gain_two_back, gain_query_back, gain_joint_back = split_gains(gains_back)
    upstream = cotangent[arrived_rows].astype(FULL_TYPE)
    ffn_grad = (RESIDUAL_SCALE * upstream).astype(HALF_TYPE)
    ffn_grad_full = lax.all_gather(ffn_grad, "col", axis=1, tiled=True)
    grad_down_w = contract_rows(ffn_grad_full, activated)
    grad_act = product(ffn_grad_full, down_back)
    sigmoid_gate = jax.nn.sigmoid(gate_rows)
    grad_gate = (
        grad_act * up_rows * sigmoid_gate * (1.0 + gate_rows * (1.0 - sigmoid_gate))
    ).astype(HALF_TYPE)
    grad_up = (grad_act * gate_rows * sigmoid_gate).astype(HALF_TYPE)
    grad_gate_w = contract_rows(normed_two, grad_gate)
    grad_up_w = contract_rows(normed_two, grad_up)
    ffn_reduced = (grad_gate_w, grad_up_w, grad_down_w)
    grad_normed_two = lax.psum_scatter(
        times_transposed(grad_gate, gate_back) + times_transposed(grad_up, up_back),
        "col",
        scatter_dimension=1,
        tiled=True,
    )
    gain_two_local = lax.dynamic_slice_in_dim(gain_two_back, col_start, width_share)
    weighted_two = grad_normed_two * gain_two_local
    local_dots = jnp.sum(weighted_two * residual, axis=1)
    gain_two_terms = jnp.sum(grad_normed_two * residual * scale_two, axis=0)
    gain_two_slot = lax.dynamic_update_slice_in_dim(
        jnp.zeros((D,), FULL_TYPE), gain_two_terms, col_start, 0
    )
    row_dots, gain_two_grad = lax.psum((local_dots, gain_two_slot), "col")
    grad_residual = (
        upstream + scale_two * weighted_two - residual * scale_two**3 * (row_dots / D)[:, None]
    )
    branch_grad = (RESIDUAL_SCALE * grad_residual).astype(HALF_TYPE)
    branch_grad_full = lax.all_gather(branch_grad, "col", axis=1, tiled=True)
    grad_out_w = contract_rows(branch_grad_full, attended)
    grad_attended = product(branch_grad_full, out_back).astype(HALF_TYPE)
    grad_att_pad = jnp.swapaxes(
        to_padded(grad_attended.reshape(token_count, local_heads, VDIM)), 0, 1
    )
    grad_query_pad, grad_joint_pad, grad_rope_heads = lax.map(
        lambda head_items: attend_back(
            head_items[0], head_items[1], head_items[2], head_items[3], rope_pad, segment
        ),
        (query_pad, joint_pad, grad_att_pad, log_totals),
    )
    grad_rope_tokens = jnp.sum(grad_rope_heads, axis=0)[arrived_rows]
    grad_query_tokens = jnp.swapaxes(grad_query_pad[:, arrived_rows], 0, 1)
    grad_query_full = (
        jnp.concatenate(
            [
                grad_query_tokens[..., :NOPE],
                rotary_grad(
                    grad_query_tokens[..., NOPE:], cosine[:, None, :], sine_table[:, None, :]
                ),
            ],
            axis=-1,
        )
        .reshape(token_count, local_heads * (NOPE + ROPE))
        .astype(HALF_TYPE)
    )
    grad_joint_full = (
        jnp.swapaxes(grad_joint_pad[:, arrived_rows], 0, 1)
        .reshape(token_count, local_heads * (NOPE + VDIM))
        .astype(HALF_TYPE)
    )
    grad_query_up_w = contract_rows(query_normed, grad_query_full)
    grad_joint_up_w = contract_rows(compressed, grad_joint_full)
    grad_query_normed, grad_compressed, grad_rope_sum = (
        lax.psum(
            times_transposed(grad_query_full, query_up_back).astype(jnp.bfloat16), "col"
        ).astype(jnp.float32),
        lax.psum(
            times_transposed(grad_joint_full, joint_up_back).astype(jnp.bfloat16), "col"
        ).astype(jnp.float32),
        lax.psum(grad_rope_tokens.astype(jnp.bfloat16), "col").astype(jnp.float32),
    )
    grad_query_latent, gain_query_grad = rms_backward(
        grad_query_normed, query_latent, scale_query, gain_query_back
    )
    grad_compressed_raw, gain_joint_grad = rms_backward(
        grad_compressed, compressed_raw, scale_joint, gain_joint_back
    )
    grad_key_raw = rotary_grad(grad_rope_sum, cosine, sine_table)
    grad_query_latent = grad_query_latent.astype(HALF_TYPE)
    grad_joint_latent = jnp.concatenate([grad_compressed_raw, grad_key_raw], axis=1).astype(
        HALF_TYPE
    )
    grad_query_down_w = contract_rows(normed_one, grad_query_latent)
    grad_joint_down_w = contract_rows(normed_one, grad_joint_latent)
    grad_normed_one = times_transposed(grad_query_latent, query_down_back) + times_transposed(
        grad_joint_latent, joint_down_back
    )
    grad_inputs_full, gain_one_grad = rms_backward(
        grad_normed_one, inputs_full, scale_one, gain_one_back
    )
    grad_inputs = grad_residual + lax.dynamic_slice_in_dim(
        grad_inputs_full, col_start, width_share, 1
    )
    returned = lax.all_to_all(
        grad_inputs.astype(HALF_TYPE), "row", split_axis=0, concat_axis=0, tiled=True
    )
    grad_tokens = jnp.zeros_like(returned).at[sort_order].set(returned)
    gains_grad = jnp.concatenate(
        [gain_one_grad, gain_two_grad, gain_query_grad, gain_joint_grad], axis=0
    )
    reduced = (
        lax.psum_scatter(
            grad_query_down_w.astype(jnp.bfloat16), "row", scatter_dimension=0, tiled=True
        ).astype(jnp.float32),
        lax.psum_scatter(
            grad_joint_down_w.astype(jnp.bfloat16), "row", scatter_dimension=0, tiled=True
        ).astype(jnp.float32),
        lax.psum_scatter(
            grad_query_up_w.astype(jnp.bfloat16), "row", scatter_dimension=0, tiled=True
        ).astype(jnp.float32),
        lax.psum_scatter(
            grad_joint_up_w.astype(jnp.bfloat16), "row", scatter_dimension=0, tiled=True
        ).astype(jnp.float32),
        lax.psum_scatter(
            grad_out_w.astype(jnp.bfloat16), "row", scatter_dimension=0, tiled=True
        ).astype(jnp.float32),
        lax.psum_scatter(
            ffn_reduced[0].astype(jnp.bfloat16), "row", scatter_dimension=0, tiled=True
        ).astype(jnp.float32),
        lax.psum_scatter(
            ffn_reduced[1].astype(jnp.bfloat16), "row", scatter_dimension=0, tiled=True
        ).astype(jnp.float32),
        lax.psum_scatter(
            ffn_reduced[2].astype(jnp.bfloat16), "row", scatter_dimension=0, tiled=True
        ).astype(jnp.float32),
        lax.psum_scatter(
            gains_grad.astype(jnp.bfloat16), "row", scatter_dimension=0, tiled=True
        ).astype(jnp.float32),
    )
    step_rates = learning_rates()
    seconds_next = []
    weights_next = []
    for slot_index in range(9):
        second_new, weight_new = adam_update(
            params[slot_index],
            reduced[slot_index],
            firsts[slot_index],
            seconds[slot_index],
            step_rates[slot_index],
        )
        seconds_next.append(second_new)
        weights_next.append(weight_new)
    return (
        output_pad,
        grad_tokens,
        reduced[0],
        reduced[1],
        reduced[2],
        reduced[3],
        reduced[4],
        reduced[5],
        reduced[6],
        reduced[7],
        reduced[8],
        seconds_next[0],
        seconds_next[1],
        seconds_next[2],
        seconds_next[3],
        seconds_next[4],
        seconds_next[5],
        seconds_next[6],
        seconds_next[7],
        seconds_next[8],
        weights_next[0],
        weights_next[1],
        weights_next[2],
        weights_next[3],
        weights_next[4],
        weights_next[5],
        weights_next[6],
        weights_next[7],
        weights_next[8],
    )


def solution(mesh):
    in_specs = (
        P("row", "col"),
        P("row"),
        P("row", None),
        P("row", "col"),
        P("row", None),
        P("row", None),
        P("row", "col"),
        P("row", "col"),
        P("row", "col"),
        P("row", "col"),
        P("row", "col"),
        P("row", "col"),
        P("row"),
        P("row", None),
        P("row", None),
        P("row", "col"),
        P("row", "col"),
        P("row", "col"),
        P("row", "col"),
        P("row", "col"),
        P("row", "col"),
        P("row"),
        P("row", None),
        P("row", None),
        P("row", "col"),
        P("row", "col"),
        P("row", "col"),
        P("row", "col"),
        P("row", "col"),
        P("row", "col"),
        P("row"),
    )
    out_specs = (
        P("row", "col"),
        P("row", "col"),
        P("row", None),
        P("row", None),
        P("row", "col"),
        P("row", "col"),
        P("row", "col"),
        P("row", "col"),
        P("row", "col"),
        P("row", "col"),
        P("row"),
        P("row", None),
        P("row", None),
        P("row", "col"),
        P("row", "col"),
        P("row", "col"),
        P("row", "col"),
        P("row", "col"),
        P("row", "col"),
        P("row"),
        P("row", None),
        P("row", None),
        P("row", "col"),
        P("row", "col"),
        P("row", "col"),
        P("row", "col"),
        P("row", "col"),
        P("row", "col"),
        P("row"),
    )
    return jax.shard_map(body, mesh=mesh, in_specs=in_specs, out_specs=out_specs, check_vma=False)
```

profile of v0, /device:TPU:0, one launch (start us, length us, event | category | flops | bytes accessed | tf_op | source)
XLA Modules:
  0.0 2912.2 jit_solution(9415126970989158882)
XLA Ops:
  17.0 31.0 %all_to_all.36 = bf16[16,24,1280]{2,1,0:T(8,128)(2,1)} all-to-all(bf16[16,24,1280]{2,1,0:T(8,128)(2,1)S(1)} %bitcast.200), channel_id=1, replica_groups=mesh['row'=16,'col'=2] {'row'}, dimensions={0} | all-to-all | bytes 1966080 | tf_op jit(solution)/shard_map/all_to_all | solution.py:321
  64.8 21.8 all-gather
  94.0 29.6 %all-gather.20.cloned.1.call-done = bf16[2560,288]{1,0:T(8,128)(2,1)} async-done(((bf16[160,288]{1,0:T(8,128)(2,1)}), bf16[2560,288]{1,0:T(8,128)(2,1)}) %all-gather.20.cloned.1.call-update) | async-done | bytes 1474576 | tf_op jit(solution)/shard_map/all_gather | solution.py:334
  127.7 36.5 %all-gather.22.cloned.1.call-done = bf16[256,2560]{1,0:T(8,128)(2,1)} async-done(((bf16[16,2560]{1,0:T(8,128)(2,1)}), bf16[256,2560]{1,0:T(8,128)(2,1)}) %all-gather.22.cloned.1.call-update) | async-done | bytes 1310736 | tf_op jit(solution)/shard_map/all_gather | solution.py:336
  180.5 49.9 %scatter_fusion.1 = bf16[896,20,128]{2,1,0:T(8,128)(2,1)} fusion(bf16[896,20,128]{2,1,0:T(8,128)(2,1)} %broadcast_in_dim.127, s32[384]{0:T(512)S(1)} %fusion.104, bf16[384,20,128]{2,1,0:T(8,128)(2,1)} %copy.201), kind=kCustom, calls=%fused_computation.10 | custom fusion | bytes 5899776 | tf_op jit(solution)/shard_map/scatter | solution.py:330
  242.1 18.9 all-gather.18.cloned.1.call-done
  274.5 50.2 %scatter_fusion = bf16[896,20,96]{2,1,0:T(8,128)(2,1)} fusion(bf16[896,20,96]{2,1,0:T(8,128)(2,1)} %broadcast_in_dim.126, s32[384]{0:T(512)S(1)} %fusion.104, bf16[384,20,96]{2,1,0:T(8,128)(2,1)} %copy.199), kind=kCustom, calls=%fused_computation.9 | custom fusion | bytes 4425216 | tf_op jit(solution)/shard_map/scatter | solution.py:330
  330.3 204.0 %while.35 = (s32[]{:T(128)}, bf16[20,896,64]{1,2,0:T(8,128)(2,1)}, f32[20,896]{1,0:T(8,128)}, s32[896]{0:T(1024)S(1)}, bf16[20,896,96]{2,1,0:T(8,128)(2,1)}, /*i...) while((s32[]{:T(128)}, bf16[20,896,64]{1,2,0:T(8,128)(2,1)}, ...), condition=%wide.region_16.17_spmd, body=%wide.region_11.16_spmd.sunk | while | flops 200791360 | bytes 29522740 | solution.py:383
  558.6 50.6 %reduce-scatter.12.cloned.1.call-done = f32[384,1280]{1,0:T(8,128)} async-done(((f32[384,2560]{1,0:T(8,128)}), f32[384,1280]{1,0:T(8,128)}) %reduce-scatter.12.cloned.1.call-update) | async-done | bytes 1966096 | tf_op jit(solution)/shard_map/reduce_scatter | solution.py:390
  623.3 43.0 %all-gather.26.cloned.1.call-done = f32[384,2560]{1,0:T(8,128)} async-done(((f32[384,1280]{1,0:T(8,128)}), f32[384,2560]{1,0:T(8,128)}) %all-gather.26.cloned.1.call-update) | async-done | bytes 3932176 | tf_op jit(solution)/shard_map/all_gather | solution.py:394
  670.0 123.8 %all-gather.28.cloned.1.call-done = bf16[2560,3200]{1,0:T(8,128)(2,1)} async-done(((bf16[160,3200]{1,0:T(8,128)(2,1)}), bf16[2560,3200]{1,0:T(8,128)(2,1)}) %all-gather.28.cloned.1.call-update) | async-done | bytes 16384016 | tf_op jit(solution)/shard_map/all_gather | solution.py:338
  793.8 12.7 fusion.133
  806.4 112.8 %all-gather.30.cloned.1.call-done = bf16[2560,3200]{1,0:T(8,128)(2,1)} async-done(((bf16[160,3200]{1,0:T(8,128)(2,1)}), bf16[2560,3200]{1,0:T(8,128)(2,1)}) %all-gather.30.cloned.1.call-update) | async-done | bytes 16384016 | tf_op jit(solution)/shard_map/all_gather | solution.py:339
  919.3 12.7 fusion.134
  932.0 19.4 all-gather.34.cloned.1.call-done
  951.3 127.4 %all-gather.32.cloned.1.call-done = bf16[2560,3200]{1,0:T(8,128)(2,1)} async-done(((bf16[160,3200]{1,0:T(8,128)(2,1)}), bf16[2560,3200]{1,0:T(8,128)(2,1)}) %all-gather.32.cloned.1.call-update) | async-done | bytes 16384016 | tf_op jit(solution)/shard_map/all_gather | solution.py:340
  1078.7 17.0 multiply_convert_fusion.2
  1120.1 50.2 %reduce-scatter.16.cloned.1.call-done = f32[384,1280]{1,0:T(8,128)} async-done(((f32[384,2560]{1,0:T(8,128)}), f32[384,1280]{1,0:T(8,128)}) %reduce-scatter.16.cloned.1.call-update) | async-done | bytes 1966096 | tf_op jit(solution)/shard_map/reduce_scatter | solution.py:446
  1184.0 32.9 %all-gather.36.cloned.1.call-done = bf16[384,2560]{1,0:T(8,128)(2,1)} async-done(((bf16[384,1280]{1,0:T(8,128)(2,1)}), bf16[384,2560]{1,0:T(8,128)(2,1)}) %all-gather.36.cloned.1.call-update) | async-done | bytes 1966096 | tf_op jit(solution)/shard_map/all_gather | solution.py:464
  1229.5 49.8 %scatter_fusion.2 = bf16[896,20,64]{2,1,0:T(8,128)(2,1)} fusion(bf16[896,20,64]{2,1,0:T(8,128)(2,1)} %broadcast_in_dim.133, s32[384]{0:T(512)S(1)} %copy-done.50, bf16[384,20,64]{2,1,0:T(8,128)(2,1)} %copy.210), kind=kCustom, calls=%fused_computation.13 | custom fusion | bytes 2950656 | tf_op jit(solution)/shard_map/scatter | solution.py:330
  1285.1 585.3 %while.36 = (s32[]{:T(128)}, f32[20,896,96]{1,2,0:T(8,128)}, bf16[20,896,128]{2,0,1:T(8,128)(2,1)}, f32[20,896,32]{1,2,0:T(8,128)}, s32[896]{0:T(1024)S(1)}, /*i...) while((s32[]{:T(128)}, f32[20,896,96]{1,2,0:T(8,128)}, ...), condition=%wide.region_28.29_spmd, body=%wide.region_25.28_spmd.sunk | while | flops 510691776 | bytes 33048556 | solution.py:470
  1561.6 12.6 dynamic_update_slice.48
  1988.8 14.4 convolution_convert_fusion.3
  2003.3 14.4 convolution_convert_fusion.4
  2018.0 14.5 convolution_convert_fusion.2
  2052.6 67.3 %all-reduce.2 = bf16[6144]{0:T(1024)(128)(2,1)S(1)} all-reduce(bf16[6144]{0:T(1024)(128)(2,1)S(1)} %pad_maximum_fusion.8), channel_id=13, replica_groups=mesh['row'=16,'col'=2] {'row'}, use_global_device_ids=true, to_apply=%region_50.51.clone | all-reduce | flops 6144 | bytes 24576
  2129.6 66.8 %reduce-scatter.22.cloned.1.call-done = bf16[48,1920]{1,0:T(8,128)(2,1)} async-done(((bf16[768,1920]{1,0:T(8,128)(2,1)}), bf16[48,1920]{1,0:T(8,128)(2,1)}) %reduce-scatter.22.cloned.1.call-update) | async-done | bytes 184336 | tf_op jit(solution)/shard_map/reduce_scatter | solution.py:543
  2198.6 71.3 %reduce-scatter.18.cloned.1.call-done = bf16[160,768]{1,0:T(8,128)(2,1)} async-done(((bf16[2560,768]{1,0:T(8,128)(2,1)}), bf16[160,768]{1,0:T(8,128)(2,1)}) %reduce-scatter.18.cloned.1.call-update) | async-done | bytes 245776 | tf_op jit(solution)/shard_map/reduce_scatter | solution.py:537
  2272.1 87.6 %reduce-scatter.26.cloned.1.call-done = bf16[160,1280]{1,0:T(8,128)(2,1)} async-done(((bf16[2560,1280]{1,0:T(8,128)(2,1)}), bf16[160,1280]{1,0:T(8,128)(2,1)}) %reduce-scatter.26.cloned.1.call-update) | async-done | bytes 409616 | tf_op jit(solution)/shard_map/reduce_scatter | solution.py:549
  2362.8 176.9 %reduce-scatter.30.cloned.1.call-done = bf16[160,3200]{1,0:T(8,128)(2,1)} async-done(((bf16[2560,3200]{1,0:T(8,128)(2,1)}), bf16[160,3200]{1,0:T(8,128)(2,1)}) %reduce-scatter.30.cloned.1.call-update) | async-done | bytes 1024016 | tf_op jit(solution)/shard_map/reduce_scatter | solution.py:555
  2545.2 173.8 %reduce-scatter.28.cloned.1.call-done = bf16[160,3200]{1,0:T(8,128)(2,1)} async-done(((bf16[2560,3200]{1,0:T(8,128)(2,1)}), bf16[160,3200]{1,0:T(8,128)(2,1)}) %reduce-scatter.28.cloned.1.call-update) | async-done | bytes 1024016 | tf_op jit(solution)/shard_map/reduce_scatter | solution.py:552
  2725.1 173.8 %reduce-scatter.32.cloned.1.call-done = bf16[160,3200]{1,0:T(8,128)(2,1)} async-done(((bf16[2560,3200]{1,0:T(8,128)(2,1)}), bf16[160,3200]{1,0:T(8,128)(2,1)}) %reduce-scatter.32.cloned.1.call-update) | async-done | bytes 1024016 | tf_op jit(solution)/shard_map/reduce_scatter | solution.py:558
  (1443 shorter events, 1128.0 us)
Async XLA Ops:
  7.2 610.6 %copy-start = (bf16[896,1280]{1,0:T(8,128)(2,1)S(1)}, bf16[896,1280]{1,0:T(8,128)(2,1)}, u32[]{:S(2)}) copy-start(bf16[896,1280]{1,0:T(8,128)(2,1)} %param.50) | copy-start | bytes 6881284
  7.2 84.1 %all-gather.14.cloned.1.call-start = ((), (), s32[]{:S(2)}) async-start(), calls=%async_computation.14 | async-start | bytes 2949120 | tf_op jit(solution)/shard_map/all_gather | solution.py:355
  48.0 75.6 %all-gather.20.cloned.1.call-start = ((), (), s32[]{:S(2)}) async-start(), calls=%async_computation.17 | async-start | bytes 2088960 | tf_op jit(solution)/shard_map/all_gather | solution.py:334
  49.8 114.5 %all-gather.22.cloned.1.call-start = ((), (), s32[]{:S(2)}) async-start(), calls=%async_computation.18 | async-start | bytes 1392640 | tf_op jit(solution)/shard_map/all_gather | solution.py:336
  51.5 184.6 %all-gather.16.cloned.1.call-start = ((), (), s32[]{:S(2)}) async-start(), calls=%async_computation.15 | async-start | bytes 4177920 | tf_op jit(solution)/shard_map/all_gather | solution.py:333
  53.3 207.8 %all-gather.18.cloned.1.call-start = ((), (), s32[]{:S(2)}) async-start(), calls=%async_computation.16 | async-start | bytes 3133440 | tf_op jit(solution)/shard_map/all_gather | solution.py:335
  57.6 30.0 %all-to-all-start = ((s32[16,24,1]{1,2,0:T(1,128)}), s32[16,24,1]{1,2,0:T(1,128)S(1)}, u32[]{:S(2)}, u32[]{:S(2)}) async-start(s32[16,24,1]{1,2,0:T(1,128)} %bitcast.17), calls=%async_computation | async-start | bytes 16384 | tf_op jit(solution)/shard_map/all_to_all | solution.py:322
  62.3 487.8 %all-gather.24.cloned.1.call-start = ((), (), s32[]{:S(2)}) async-start(), calls=%async_computation.19 | async-start | bytes 6963200 | tf_op jit(solution)/shard_map/all_gather | solution.py:337
  63.2 546.0 %reduce-scatter.12.cloned.1.call-start = ((), (), s32[]{:S(2)}) async-start(), calls=%async_computation.20 | async-start | bytes 5898240 | tf_op jit(solution)/shard_map/reduce_scatter | solution.py:390
  87.1 174.0 %copy-start.43 = (f32[768]{0:T(1024)}, f32[768]{0:T(1024)S(1)}, u32[]{:S(2)}) copy-start(f32[768]{0:T(1024)S(1)} %slice.387) | copy-start | bytes 9220
  88.8 185.7 %copy-start.49 = (s32[384]{0:T(512)}, s32[384]{0:T(512)S(1)}, u32[]{:S(2)}) copy-start(s32[384]{0:T(512)S(1)} %fusion.104) | copy-start | bytes 4612
  88.9 528.9 %copy-start.45 = (s32[1024]{0:T(1024)}, s32[1024]{0:T(1024)S(1)}, u32[]{:S(2)}) copy-start(s32[1024]{0:T(1024)S(1)} %pad_clamp_fusion) | copy-start | bytes 12292
  558.6 107.7 %all-gather.26.cloned.1.call-start = ((), (), s32[]{:S(2)}) async-start(), calls=%async_computation.21 | async-start | bytes 5898240 | tf_op jit(solution)/shard_map/all_gather | solution.py:394
  612.3 181.4 %all-gather.28.cloned.1.call-start = ((), (), s32[]{:S(2)}) async-start(), calls=%async_computation.22 | async-start | bytes 17408000 | tf_op jit(solution)/shard_map/all_gather | solution.py:338
  615.0 304.3 %all-gather.30.cloned.1.call-start = ((), (), s32[]{:S(2)}) async-start(), calls=%async_computation.23 | async-start | bytes 17408000 | tf_op jit(solution)/shard_map/all_gather | solution.py:339
  617.7 333.6 %all-gather.34.cloned.1.call-start = ((), (), s32[]{:S(2)}) async-start(), calls=%async_computation.26 | async-start | bytes 2949120 | tf_op jit(solution)/shard_map/all_gather | solution.py:435
  621.1 457.5 %all-gather.32.cloned.1.call-start = ((), (), s32[]{:S(2)}) async-start(), calls=%async_computation.24 | async-start | bytes 17408000 | tf_op jit(solution)/shard_map/all_gather | solution.py:340
  623.2 547.1 %reduce-scatter.16.cloned.1.call-start = ((), (), s32[]{:S(2)}) async-start(), calls=%async_computation.27 | async-start | bytes 5898240 | tf_op jit(solution)/shard_map/reduce_scatter | solution.py:446
  670.0 249.3 %copy-start.23 = (bf16[384,2560]{1,0:T(8,128)(2,1)}, bf16[384,2560]{1,0:T(8,128)(2,1)S(1)}, u32[]{:S(2)}) copy-start(bf16[384,2560]{1,0:T(8,128)(2,1)S(1)} %multiply_convert_fusion.5) | copy-start | bytes 5898244
  1120.0 96.9 %all-gather.36.cloned.1.call-start = ((), (), s32[]{:S(2)}) async-start(), calls=%async_computation.28 | async-start | bytes 2949120 | tf_op jit(solution)/shard_map/all_gather | solution.py:464
  1183.9 778.5 %all-reduce.7.cloned.1.call-start = ((), (), s32[]{:S(2)}) async-start(), calls=%async_computation.37 | async-start | bytes 1572864 | tf_op jit(solution)/shard_map/psum | solution.py:499
  1927.8 119.4 %reduce-scatter.14.cloned.1.call-start = ((), (), s32[]{:S(2)}) async-start(), calls=%async_computation.25 | async-start | bytes 2949120 | tf_op jit(solution)/shard_map/reduce_scatter | solution.py:400
  1939.8 180.7 %reduce-scatter.24.cloned.1.call-start = ((), (), s32[]{:S(2)}) async-start(), calls=%async_computation.32 | async-start | bytes 1392640 | tf_op jit(solution)/shard_map/reduce_scatter | solution.py:546
  1942.8 184.9 %reduce-scatter.20.cloned.1.call-start = ((), (), s32[]{:S(2)}) async-start(), calls=%async_computation.30 | async-start | bytes 2088960 | tf_op jit(solution)/shard_map/reduce_scatter | solution.py:540
  1968.0 228.4 %reduce-scatter.22.cloned.1.call-start = ((), (), s32[]{:S(2)}) async-start(), calls=%async_computation.31 | async-start | bytes 3133440 | tf_op jit(solution)/shard_map/reduce_scatter | solution.py:543
  1973.2 296.8 %reduce-scatter.18.cloned.1.call-start = ((), (), s32[]{:S(2)}) async-start(), calls=%async_computation.29 | async-start | bytes 4177920 | tf_op jit(solution)/shard_map/reduce_scatter | solution.py:537
  1980.1 379.6 %reduce-scatter.26.cloned.1.call-start = ((), (), s32[]{:S(2)}) async-start(), calls=%async_computation.33 | async-start | bytes 6963200 | tf_op jit(solution)/shard_map/reduce_scatter | solution.py:549
  1988.4 551.3 %reduce-scatter.30.cloned.1.call-start = ((), (), s32[]{:S(2)}) async-start(), calls=%async_computation.35 | async-start | bytes 17408000 | tf_op jit(solution)/shard_map/reduce_scatter | solution.py:555
  2003.3 715.7 %reduce-scatter.28.cloned.1.call-start = ((), (), s32[]{:S(2)}) async-start(), calls=%async_computation.34 | async-start | bytes 17408000 | tf_op jit(solution)/shard_map/reduce_scatter | solution.py:552
  2017.7 881.1 %reduce-scatter.32.cloned.1.call-start = ((), (), s32[]{:S(2)}) async-start(), calls=%async_computation.36 | async-start | bytes 17408000 | tf_op jit(solution)/shard_map/reduce_scatter | solution.py:558
  2040.0 82.4 %all-to-all-start.2 = ((bf16[16,24,1280]{2,1,0:T(8,128)(2,1)}), bf16[16,24,1280]{2,1,0:T(8,128)(2,1)S(1)}, u32[]{:S(2)}, u32[]{:S(2)}) async-start(bf16[16,24,1280]{2,1,0:T(8,128)(2,1)} %bitcast.35), calls=%async_computation.5 | async-start | bytes 1966080 | tf_op jit(solution)/shard_map/all_to_all | solution.py:529
  2272.1 267.6 %copy-start.14 = (f32[160,3200]{1,0:T(8,128)S(1)}, f32[160,3200]{1,0:T(8,128)}, u32[]{:S(2)}) copy-start(f32[160,3200]{1,0:T(8,128)} %param.57) | copy-start | bytes 6144004
  (141 other events, 2315.9 us)
Sparse Core Ops, SparseCore 0:
  48.1 31.7 all-gather.13
  82.7 40.8 all-gather.19
  126.5 37.7 all-gather.21
  166.9 47.5 all-gather.15
  217.2 43.8 all-gather.17
  263.8 61.7 all-gather.23
  558.7 50.4 reduce-scatter.11
  612.4 53.7 all-gather.25
  669.4 124.3 all-gather.27
  796.7 122.5 all-gather.29
  921.5 29.8 all-gather.33
  954.3 124.3 all-gather.31
  1120.1 50.1 reduce-scatter.15
  1184.0 32.8 all-gather.35
  1927.9 34.5 all-reduce.6
  1965.2 30.5 reduce-scatter.13
  1999.8 62.9 reduce-scatter.23
  2067.4 60.2 reduce-scatter.19
  2132.1 64.2 reduce-scatter.21
  2200.7 69.2 reduce-scatter.17
  2273.9 85.7 reduce-scatter.25
  2364.6 175.0 reduce-scatter.29
  2544.0 175.0 reduce-scatter.27
  2723.7 175.0 reduce-scatter.31
where the time goes:
time: 2940 us; the launch traced here: 2910 us
  waiting for transfers between devices  1410 us (48%)
  local copies, waits for them, and re-layouts  715 us (24%)
  matrix products  475 us (16%)
  other arithmetic  148 us (5%)
  blocking collectives  135 us (5%)
    dynamic_update_slice x40, local copies, waits for them, and re-layouts, body(): lax.map(lambda head_items: attend_back(head_items[0], head_items[1], head...  268 us
    reduce_scatter x1, waiting for transfers between devices, body(): lax.psum_scatter(ffn_reduced[1].astype(jnp.bfloat16), 'row', scatter_dime...  177 us
    reduce_scatter x1, waiting for transfers between devices, body(): lax.psum_scatter(ffn_reduced[0].astype(jnp.bfloat16), 'row', scatter_dime...  174 us
    reduce_scatter x1, waiting for transfers between devices, body(): lax.psum_scatter(ffn_reduced[2].astype(jnp.bfloat16), 'row', scatter_dime...  174 us
    scatter x4, local copies, waits for them, and re-layouts, to_padded(): jnp.zeros((CAP,) + values.shape[1:], values.dtype).at[arrived_rows]  151 us
    all_gather x1, waiting for transfers between devices, body(): lax.all_gather(down_weight.astype(HALF_TYPE), 'row', axis=0, tiled=True)  127 us
    all_gather x1, waiting for transfers between devices, body(): lax.all_gather(gate_weight.astype(HALF_TYPE), 'row', axis=0, tiled=True)  124 us
    all_gather x1, waiting for transfers between devices, body(): lax.all_gather(up_weight.astype(HALF_TYPE), 'row', axis=0, tiled=True)  113 us
  transfers between devices with their start and end apart: 26, of which 19 were waited for; matrix products, arithmetic and copies ran while one was open for 19% of the time, Pallas kernels for 0%

commit v1 on v0

v1 whole, which is shorter than its diff:
```python
import functools

import jax
import jax.numpy as jnp
from jax import lax
from jax.experimental import pallas as pl
from jax.experimental.pallas import tpu as pltpu
from jax.sharding import PartitionSpec as P

D = 2560
FF = 6400
HEADS = 40
NOPE = 64
ROPE = 32
VDIM = 64
Q_RANK = 768
KV_RANK = 256
SEQS = 4
BLK = 128
STEP = 10
CAP = 896

Z_SIZE = 4
CORES = 2

EPSILON = 1e-05
RESIDUAL_SCALE = 1.4 / 62**0.5
BETA_ONE = 0.9
BETA_TWO = 0.95
ADAM_EPSILON = 1e-08
DECAY_RATE = 0.1
MASKED = -1e30
SCORE_SCALE = (NOPE + ROPE) ** (-0.5)
FULL_TYPE = jnp.float32
HALF_TYPE = jnp.bfloat16


def rms_scale(values):
    return lax.rsqrt(jnp.mean(values * values, axis=-1, keepdims=True) + EPSILON)


def rms_backward(grad_normed, values, norm_scale, gain_values):
    weighted = grad_normed * gain_values
    mean_term = jnp.mean(weighted * values, axis=-1, keepdims=True)
    grad_values = norm_scale * weighted - values * norm_scale**3 * mean_term
    grad_gain = jnp.sum(grad_normed * values * norm_scale, axis=0)
    return (grad_values, grad_gain)


def product(left_side, right_side):
    return jnp.dot(left_side, right_side, preferred_element_type=FULL_TYPE)


def contract_rows(left_side, right_side):
    return lax.dot_general(
        left_side, right_side, (((0,), (0,)), ((), ())), preferred_element_type=FULL_TYPE
    )


def times_transposed(left_side, right_side):
    return lax.dot_general(
        left_side, right_side, (((1,), (1,)), ((), ())), preferred_element_type=FULL_TYPE
    )


def rotate_half(values):
    half_width = values.shape[-1] // 2
    return jnp.concatenate([-values[..., half_width:], values[..., :half_width]], axis=-1)


def rotate_back(values):
    half_width = values.shape[-1] // 2
    return jnp.concatenate([values[..., half_width:], -values[..., :half_width]], axis=-1)


def learning_rates():
    return (
        3.0 * D ** (-0.5),
        3.0 * D ** (-0.5),
        3.0 * (Q_RANK // 2) ** (-0.5),
        3.0 * KV_RANK ** (-0.5),
        3.0 * max(HEADS * VDIM // 512, 1) ** (-0.5),
        3.0 * D ** (-0.5),
        3.0 * D ** (-0.5),
        3.0 * max(FF // 80, 1) ** (-0.5),
        0.6,
    )


def adam_update(weight_old, grad_value, first_old, second_old, step_rate):
    first_new = BETA_ONE * first_old + (1.0 - BETA_ONE) * grad_value
    second_new = BETA_TWO * second_old + (1.0 - BETA_TWO) * grad_value * grad_value
    first_hat = first_new / (1.0 - BETA_ONE**STEP)
    second_hat = second_new / (1.0 - BETA_TWO**STEP)
    weight_new = weight_old - step_rate * (
        first_hat / (jnp.sqrt(second_hat) + ADAM_EPSILON) + DECAY_RATE * weight_old
    )
    return (second_new, weight_new)


def turn_matrix(width):
    rows = lax.broadcasted_iota(jnp.int32, (width, width), 0)
    columns = lax.broadcasted_iota(jnp.int32, (width, width), 1)
    half = ROPE // 2
    in_first = (columns % ROPE) < half
    minus = in_first & (rows == columns + half)
    plus = jnp.logical_not(in_first) & (rows == columns - half)
    return jnp.where(plus, 1.0, jnp.where(minus, -1.0, 0.0)).astype(HALF_TYPE)


def split_dot(values, matrix, dims):
    high = values.astype(HALF_TYPE)
    low = (values - high.astype(FULL_TYPE)).astype(HALF_TYPE)
    dot = functools.partial(
        lax.dot_general, dimension_numbers=(dims, ((), ())), preferred_element_type=FULL_TYPE
    )
    return dot(high, matrix) + dot(low, matrix)


NT = ((1,), (1,))
NN = ((1,), (0,))


def kernel_dot(left_side, right_side, dims):
    return lax.dot_general(
        left_side, right_side, (dims, ((), ())), preferred_element_type=FULL_TYPE
    )


def fill_bias(bias_ref, row_here, row_across, first_across):
    key_rows = row_here[...]
    allowed = (key_rows >= first_across[...]) & (key_rows <= row_across[...])
    bias_ref[...] = jnp.where(allowed, 0.0, MASKED)


def attend_kernel(
    group,
    row_here,
    row_across,
    first_across,
    cosine,
    sine,
    key_rope,
    query_nope,
    query_rope,
    joint,
    attended,
    rotated,
    totals,
    bias,
):
    @pl.when(pl.program_id(0) == 0)
    def _():
        fill_bias(bias, row_here, row_across, first_across)

    turn = turn_matrix(group * ROPE)
    rope_in = query_rope[...]
    rotated[...] = (
        rope_in * cosine[...] + split_dot(rope_in, turn, NN) * sine[...]
    ).astype(HALF_TYPE)
    rope_keys = key_rope[...]
    for head in range(group):
        keys = joint[:, head * 128 : head * 128 + NOPE]
        values = joint[:, head * 128 + NOPE : (head + 1) * 128]
        scores = (
            kernel_dot(keys, query_nope[:, head * NOPE : (head + 1) * NOPE], NT)
            + kernel_dot(rope_keys, rotated[:, head * ROPE : (head + 1) * ROPE], NT)
        ) * SCORE_SCALE + bias[...]
        top = jnp.max(scores, axis=0, keepdims=True)
        powers = jnp.exp(scores - top)
        total = jnp.sum(powers, axis=0, keepdims=True)
        weights = (powers * (1.0 / total)).astype(HALF_TYPE)
        found = kernel_dot(values.T, weights, NN)
        attended[:, head * VDIM : (head + 1) * VDIM] = found.T.astype(HALF_TYPE)
        totals[0, head : head + 1, :] = top + jnp.log(total)


def attend_back_kernel(
    group,
    row_here,
    row_across,
    first_across,
    cosine,
    sine,
    key_rope,
    query_nope,
    rotated,
    joint,
    grad_out,
    totals,
    grad_nope,
    grad_rope,
    grad_joint,
    grad_key,
    bias,
):
    @pl.when(pl.program_id(0) == 0)
    def _():
        fill_bias(bias, row_here, row_across, first_across)
        grad_key[...] = jnp.zeros_like(grad_key)

    turn = turn_matrix(group * ROPE)
    rope_keys = key_rope[...]
    rope_keys_across = rope_keys.T
    rope_grads = []
    key_grad = jnp.zeros(grad_key.shape, FULL_TYPE)
    for head in range(group):
        keys = joint[:, head * 128 : head * 128 + NOPE]
        values = joint[:, head * 128 + NOPE : (head + 1) * 128]
        queries = query_nope[:, head * NOPE : (head + 1) * NOPE]
        turned = rotated[:, head * ROPE : (head + 1) * ROPE]
        out_grad = grad_out[:, head * VDIM : (head + 1) * VDIM]
        scores = (
            kernel_dot(keys, queries, NT) + kernel_dot(rope_keys, turned, NT)
        ) * SCORE_SCALE + bias[...]
        probs = jnp.exp(scores - totals[0, head : head + 1, :])
        value_grad = kernel_dot(probs.astype(HALF_TYPE), out_grad, NN)
        prob_grad = kernel_dot(values, out_grad, NT)
        delta = jnp.sum(probs * prob_grad, axis=0, keepdims=True)
        score_grad = (probs * (prob_grad - delta)).astype(HALF_TYPE)
        nope_key_grad = kernel_dot(score_grad, queries, NN) * SCORE_SCALE
        key_grad = key_grad + kernel_dot(score_grad, turned, NN)
        query_grad = kernel_dot(keys.T, score_grad, NN) * SCORE_SCALE
        rope_grads.append(kernel_dot(rope_keys_across, score_grad, NN))
        grad_nope[:, head * NOPE : (head + 1) * NOPE] = query_grad.T.astype(HALF_TYPE)
        grad_joint[:, head * 128 : head * 128 + NOPE] = nope_key_grad.astype(HALF_TYPE)
        grad_joint[:, head * 128 + NOPE : (head + 1) * 128] = value_grad.astype(HALF_TYPE)
    rope_grad = jnp.concatenate(rope_grads, axis=0).T * SCORE_SCALE
    grad_rope[...] = (
        rope_grad * cosine[...] + split_dot(rope_grad * sine[...], turn, NT)
    ).astype(HALF_TYPE)
    grad_key[...] += key_grad * SCORE_SCALE


def head_group(heads):
    return 4 if heads % 4 == 0 else heads


def attention_specs(tokens, group):
    whole = lambda *shape: pl.BlockSpec(shape, lambda step: (0,) * len(shape))
    wide = lambda width: pl.BlockSpec((tokens, width), lambda step: (0, step))
    shared = [
        whole(tokens, 1),
        whole(1, tokens),
        whole(1, tokens),
        whole(tokens, group * ROPE),
        whole(tokens, group * ROPE),
        whole(tokens, ROPE),
    ]
    totals = pl.BlockSpec((1, group, tokens), lambda step: (step, 0, 0))
    return (whole, wide, shared, totals)


def attention_forward(places, key_rope, query_nope, query_rope, joint, heads):
    tokens = joint.shape[0]
    group = head_group(heads)
    _, wide, shared, totals = attention_specs(tokens, group)
    return pl.pallas_call(
        functools.partial(attend_kernel, group),
        grid=(heads // group,),
        in_specs=shared + [wide(group * NOPE), wide(group * ROPE), wide(group * 128)],
        out_specs=[wide(group * VDIM), wide(group * ROPE), totals],
        out_shape=[
            jax.ShapeDtypeStruct((tokens, heads * VDIM), HALF_TYPE),
            jax.ShapeDtypeStruct((tokens, heads * ROPE), HALF_TYPE),
            jax.ShapeDtypeStruct((heads // group, group, tokens), FULL_TYPE),
        ],
        scratch_shapes=[pltpu.VMEM((tokens, tokens), FULL_TYPE)],
        compiler_params=pltpu.CompilerParams(vmem_limit_bytes=40 << 20),
        cost_estimate=pl.CostEstimate(
            flops=heads * tokens * tokens * 320,
            bytes_accessed=tokens * heads * 800,
            transcendentals=heads * tokens * tokens,
        ),
    )(*places, key_rope, query_nope, query_rope, joint)


def attention_backward(places, key_rope, query_nope, rotated, joint, grad_out, log_totals, heads):
    tokens = joint.shape[0]
    group = head_group(heads)
    whole, wide, shared, totals = attention_specs(tokens, group)
    return pl.pallas_call(
        functools.partial(attend_back_kernel, group),
        grid=(heads // group,),
        in_specs=shared
        + [wide(group * NOPE), wide(group * ROPE), wide(group * 128), wide(group * VDIM), totals],
        out_specs=[
            wide(group * NOPE),
            wide(group * ROPE),
            wide(group * 128),
            whole(tokens, ROPE),
        ],
        out_shape=[
            jax.ShapeDtypeStruct((tokens, heads * NOPE), HALF_TYPE),
            jax.ShapeDtypeStruct((tokens, heads * ROPE), HALF_TYPE),
            jax.ShapeDtypeStruct((tokens, heads * 128), HALF_TYPE),
            jax.ShapeDtypeStruct((tokens, ROPE), FULL_TYPE),
        ],
        scratch_shapes=[pltpu.VMEM((tokens, tokens), FULL_TYPE)],
        compiler_params=pltpu.CompilerParams(vmem_limit_bytes=40 << 20),
        cost_estimate=pl.CostEstimate(
            flops=heads * tokens * tokens * 900,
            bytes_accessed=tokens * heads * 1200,
            transcendentals=heads * tokens * tokens,
        ),
    )(*places, key_rope, query_nope, rotated, joint, grad_out, log_totals)


class Row:
    def __init__(self, size):
        self.size = size
        self.x_size = size // (Z_SIZE * CORES)
        index = lax.axis_index("row")
        self.z = index // (self.x_size * CORES)
        self.x = (index // CORES) % self.x_size
        self.core = index % CORES

    def move(self, values, dz=0, dx=0, dc=0):
        def at(z, x, c):
            return ((z % Z_SIZE) * self.x_size + x % self.x_size) * CORES + c % CORES

        pairs = [
            (at(z, x, c), at(z + dz, x + dx, c + dc))
            for z in range(Z_SIZE)
            for x in range(self.x_size)
            for c in range(CORES)
        ]
        return lax.ppermute(values, "row", pairs)

    def quarter(self, array, dx, dc):
        blocks = array.reshape(
            (Z_SIZE, self.x_size, CORES, array.shape[0] // self.size, array.shape[1])
        )
        x_at = lax.rem(self.x + dx, self.x_size)
        core_at = lax.rem(self.core + dc, CORES)
        part = lax.dynamic_slice(
            blocks,
            (0, x_at, core_at, 0, 0),
            (Z_SIZE, 1, 1) + blocks.shape[3:],
        )
        return part.reshape((-1, array.shape[1]))

    def reduce_scatter(self, piece):
        def over_cores(dx):
            other = self.move(piece(dx, 1).astype(HALF_TYPE), dc=1)
            return piece(dx, 0) + other.astype(FULL_TYPE)

        total = over_cores(self.x_size - 1).astype(HALF_TYPE)
        for step in range(1, self.x_size):
            came = self.move(total, dx=1)
            mine = over_cores(self.x_size - 1 - step)
            total = (came.astype(FULL_TYPE) + mine).astype(HALF_TYPE)
        blocks = total.reshape((Z_SIZE, -1, total.shape[1]))

        def block(dz):
            return lax.dynamic_index_in_dim(
                blocks, lax.rem(self.z + dz, Z_SIZE), 0, keepdims=False
            )

        total = block(Z_SIZE - 1)
        for step in range(1, Z_SIZE):
            came = self.move(total, dz=1)
            total = came.astype(FULL_TYPE) + block(Z_SIZE - 1 - step).astype(FULL_TYPE)
            if step < Z_SIZE - 1:
                total = total.astype(HALF_TYPE)
        return total


def col_gather(values, col_count):
    if col_count != 2:
        return lax.all_gather(values, "col", axis=1, tiled=True)
    other = lax.ppermute(values, "col", [(0, 1), (1, 0)])
    first = lax.axis_index("col") == 0
    return jnp.concatenate(
        [jnp.where(first, values, other), jnp.where(first, other, values)], axis=1
    )


def col_sum(values, col_count):
    half = values.astype(HALF_TYPE)
    if col_count != 2:
        return lax.psum(half.astype(FULL_TYPE), "col")
    other = lax.ppermute(half, "col", [(0, 1), (1, 0)])
    return half.astype(FULL_TYPE) + other.astype(FULL_TYPE)


def heads_apart(weight, heads):
    split = weight.reshape(weight.shape[0], heads, NOPE + ROPE)
    return jnp.concatenate(
        [
            split[:, :, :NOPE].reshape(weight.shape[0], heads * NOPE),
            split[:, :, NOPE:].reshape(weight.shape[0], heads * ROPE),
        ],
        axis=1,
    )


def heads_together(weight, heads):
    rows = weight.shape[0]
    return jnp.concatenate(
        [
            weight[:, : heads * NOPE].reshape(rows, heads, NOPE),
            weight[:, heads * NOPE :].reshape(rows, heads, ROPE),
        ],
        axis=2,
    ).reshape(rows, heads * (NOPE + ROPE))


def fold_count(height, width, rows):
    count = rows // height
    while width % count:
        count -= 1
    return count


def fold_up(weight, devices, rows):
    height = weight.shape[0] // devices
    count = fold_count(height, weight.shape[1], rows)
    width = weight.shape[1] // count
    folded = jnp.swapaxes(weight.reshape(devices, height, count, width), 1, 2)
    folded = folded.reshape(devices, count * height, width)
    folded = jnp.pad(folded, ((0, 0), (0, rows - count * height), (0, 0)))
    return folded.reshape(devices * rows, width)


def unfold(folded, devices, height, width):
    rows = folded.shape[0] // devices
    count = fold_count(height, width, rows)
    blocks = folded.reshape(devices, rows, folded.shape[1])[:, : count * height]
    blocks = blocks.reshape(devices, count, height, folded.shape[1])
    return jnp.swapaxes(blocks, 1, 2).reshape(devices * height, width)


GAIN_LANES = 32


def fold_gains(gains, devices, rows):
    flat = gains.reshape(devices, -1)
    short = -flat.shape[1] % GAIN_LANES
    flat = jnp.pad(flat, ((0, 0), (0, short)))
    blocks = flat.reshape(devices, -1, GAIN_LANES)
    blocks = jnp.pad(blocks, ((0, 0), (0, rows - blocks.shape[1]), (0, 0)))
    return blocks.reshape(devices * rows, GAIN_LANES)


def unfold_gains(folded, devices, count):
    flat = folded.reshape(devices, -1)
    return flat[:, :count].reshape(-1)


def body(
    tokens,
    dest_row,
    seq_lens,
    cotangent,
    query_down,
    joint_down,
    query_up,
    joint_up,
    out_weight,
    gate_weight,
    up_weight,
    down_weight,
    norm_gains,
    first_query_down,
    first_joint_down,
    first_query_up,
    first_joint_up,
    first_out_weight,
    first_gate_weight,
    first_up_weight,
    first_down_weight,
    first_norm_gains,
    second_query_down,
    second_joint_down,
    second_query_up,
    second_joint_up,
    second_out_weight,
    second_gate_weight,
    second_up_weight,
    second_down_weight,
    second_norm_gains,
):
    params = (
        query_down,
        joint_down,
        query_up,
        joint_up,
        out_weight,
        gate_weight,
        up_weight,
        down_weight,
        norm_gains,
    )
    firsts = (
        first_query_down,
        first_joint_down,
        first_query_up,
        first_joint_up,
        first_out_weight,
        first_gate_weight,
        first_up_weight,
        first_down_weight,
        first_norm_gains,
    )
    seconds = (
        second_query_down,
        second_joint_down,
        second_query_up,
        second_joint_up,
        second_out_weight,
        second_gate_weight,
        second_up_weight,
        second_down_weight,
        second_norm_gains,
    )
    col_count = lax.axis_size("col")
    col_index = lax.axis_index("col")
    row_count = lax.axis_size("row")
    row = Row(row_count)
    heads = HEADS // col_count
    width_share = D // col_count
    token_count = tokens.shape[0]
    col_start = col_index * width_share
    shard_rows = query_down.shape[0]
    gain_count = norm_gains.shape[0]
    ffn_width = gate_weight.shape[1]

    half = lambda weight: weight.astype(HALF_TYPE)
    parts = [
        half(query_down),
        half(out_weight),
        fold_up(half(joint_up), 1, shard_rows),
        fold_up(heads_apart(half(query_up), heads), 1, shard_rows),
        half(joint_down),
        fold_gains(half(norm_gains), 1, shard_rows),
    ]
    offsets = [0]
    for part in parts:
        offsets.append(offsets[-1] + part.shape[1])
    spare = -offsets[-1] % 128
    packed_one = jnp.concatenate(
        parts + [jnp.zeros((shard_rows, spare), HALF_TYPE), half(gate_weight)], axis=1
    )
    packed_two = jnp.concatenate([half(up_weight), half(down_weight)], axis=1)
    gathered_one = lax.all_gather(packed_one, "row", axis=0, tiled=True)
    gathered_two = lax.all_gather(packed_two, "row", axis=0, tiled=True)
    taken = [gathered_one[:, offsets[i] : offsets[i + 1]] for i in range(6)]
    query_down_all = taken[0]
    out_all = taken[1]
    joint_up_all = unfold(taken[2], row_count, joint_up.shape[0], joint_up.shape[1])
    query_up_all = unfold(taken[3], row_count, query_up.shape[0], query_up.shape[1])
    joint_down_all = taken[4]
    gains_all = unfold_gains(taken[5], row_count, gain_count).astype(FULL_TYPE)
    gate_all = gathered_one[:, offsets[-1] + spare :]
    up_all = gathered_two[:, :ffn_width]
    down_all = gathered_two[:, ffn_width:]
    gain_one = gains_all[:D]
    gain_two = gains_all[D : 2 * D]
    gain_query = gains_all[2 * D : 2 * D + Q_RANK]
    gain_joint = gains_all[2 * D + Q_RANK :]
    query_nope_all = query_up_all[:, : heads * NOPE]
    query_rope_all = query_up_all[:, heads * NOPE :]

    share = token_count // row_count
    target = dest_row // CAP
    local_rows = dest_row - target * CAP
    ids = jnp.arange(token_count, dtype=jnp.int32)
    same_before = (target[:, None] == target[None, :]) & (ids[None, :] < ids[:, None])
    slots = target * share + jnp.sum(same_before.astype(jnp.int32), axis=1)
    sends = slots[None, :] == ids[:, None]
    send_matrix = sends.astype(HALF_TYPE)
    sorted_rows = jnp.sum(jnp.where(sends, local_rows[None, :], 0), axis=1)
    sorted_tokens = product(send_matrix, tokens).astype(HALF_TYPE)
    arrived_rows = lax.all_to_all(
        sorted_rows, "row", split_axis=0, concat_axis=0, tiled=True
    )
    arrived = lax.all_to_all(sorted_tokens, "row", split_axis=0, concat_axis=0, tiled=True)

    lengths = seq_lens[0]
    padded = (lengths + BLK - 1) // BLK * BLK
    endings = CAP - jnp.sum(padded) + jnp.cumsum(padded)
    starts = endings - lengths
    inside = (arrived_rows[:, None] >= starts[None, :]) & (
        arrived_rows[:, None] < endings[None, :]
    )
    first_rows = jnp.sum(jnp.where(inside, starts[None, :], 0), axis=1)
    position = (arrived_rows - first_rows).astype(FULL_TYPE)
    frequency = 10000.0 ** (-(jnp.arange(ROPE // 2, dtype=FULL_TYPE) * 2.0 / ROPE))
    angles = position[:, None] * frequency[None, :]
    cosine = jnp.tile(jnp.cos(angles), (1, 2))
    sine = jnp.tile(jnp.sin(angles), (1, 2))
    group = head_group(heads)
    places = (
        arrived_rows[:, None],
        arrived_rows[None, :],
        first_rows[None, :],
        jnp.tile(cosine, (1, group)),
        jnp.tile(sine, (1, group)),
    )
    row_matrix = (
        jnp.arange(CAP, dtype=jnp.int32)[:, None] == arrived_rows[None, :]
    ).astype(HALF_TYPE)
    upstream_part = contract_rows(row_matrix, cotangent).astype(HALF_TYPE)

    features = col_gather(arrived, col_count)
    upstream = col_gather(upstream_part, col_count).astype(FULL_TYPE)
    ffn_grad = (RESIDUAL_SCALE * upstream).astype(HALF_TYPE)

    inputs = features.astype(FULL_TYPE)
    scale_one = rms_scale(inputs)
    normed_one = (inputs * scale_one * gain_one).astype(HALF_TYPE)
    query_latent = product(normed_one, query_down_all)
    joint_latent = product(normed_one, joint_down_all)
    scale_query = rms_scale(query_latent)
    query_normed = (query_latent * scale_query * gain_query).astype(HALF_TYPE)
    compressed_raw = joint_latent[:, :KV_RANK]
    scale_joint = rms_scale(compressed_raw)
    compressed = (compressed_raw * scale_joint * gain_joint).astype(HALF_TYPE)
    rope_raw = joint_latent[:, KV_RANK:]
    key_rope = (rope_raw * cosine + rotate_half(rope_raw) * sine).astype(HALF_TYPE)
    query_nope = product(query_normed, query_nope_all).astype(HALF_TYPE)
    query_rope = product(query_normed, query_rope_all)
    joint_full = product(compressed, joint_up_all).astype(HALF_TYPE)
    attended, rotated, log_totals = attention_forward(
        places, key_rope, query_nope, query_rope, joint_full, heads
    )
    branch = col_sum(times_transposed(attended, out_all), col_count)
    residual = inputs + RESIDUAL_SCALE * branch

    scale_two = rms_scale(residual)
    normed_two = (residual * scale_two * gain_two).astype(HALF_TYPE)
    gate_rows = product(normed_two, gate_all)
    up_rows = product(normed_two, up_all)
    sigmoid_gate = jax.nn.sigmoid(gate_rows)
    activated = (gate_rows * sigmoid_gate * up_rows).astype(HALF_TYPE)
    ffn_grad_across = ffn_grad.T
    normed_two_across = normed_two.T
    normed_one_across = normed_one.T

    def from_rows(across, right_side):
        return lambda dx, dc: product(row.quarter(across, dx, dc), right_side)

    down_grad = row.reduce_scatter(from_rows(ffn_grad_across, activated))
    grad_act = product(ffn_grad, down_all)
    grad_gate = (
        grad_act * up_rows * sigmoid_gate * (1.0 + gate_rows * (1.0 - sigmoid_gate))
    ).astype(HALF_TYPE)
    grad_up = (grad_act * gate_rows * sigmoid_gate).astype(HALF_TYPE)
    gate_grad = row.reduce_scatter(from_rows(normed_two_across, grad_gate))
    up_grad = row.reduce_scatter(from_rows(normed_two_across, grad_up))

    feed_forward = times_transposed(activated, down_all)
    feed_forward = lax.psum_scatter(
        feed_forward.astype(HALF_TYPE), "col", scatter_dimension=1, tiled=True
    ).astype(FULL_TYPE)
    residual_part = lax.dynamic_slice_in_dim(residual, col_start, width_share, 1)
    output_rows = residual_part + RESIDUAL_SCALE * feed_forward
    output_pad = product(row_matrix, output_rows.astype(HALF_TYPE)).astype(HALF_TYPE)

    grad_normed_two = col_sum(
        times_transposed(grad_gate, gate_all) + times_transposed(grad_up, up_all), col_count
    )
    through_two, gain_two_grad = rms_backward(grad_normed_two, residual, scale_two, gain_two)
    grad_residual = upstream + through_two
    branch_grad = (RESIDUAL_SCALE * grad_residual).astype(HALF_TYPE)
    out_grad = row.reduce_scatter(from_rows(branch_grad.T, attended))
    grad_attended = product(branch_grad, out_all).astype(HALF_TYPE)

    grad_nope, grad_rope, grad_joint_full, grad_key = attention_backward(
        places, key_rope, query_nope, rotated, joint_full, grad_attended, log_totals, heads
    )
    query_up_grad = jnp.concatenate(
        [contract_rows(query_normed, grad_nope), contract_rows(query_normed, grad_rope)], axis=1
    )
    joint_up_grad = contract_rows(compressed, grad_joint_full)
    folded_grads = jnp.concatenate(
        [
            fold_up(query_up_grad.astype(HALF_TYPE), row_count, shard_rows),
            fold_up(joint_up_grad.astype(HALF_TYPE), row_count, shard_rows),
        ],
        axis=1,
    )
    heads_grad = row.reduce_scatter(
        lambda dx, dc: row.quarter(folded_grads, dx, dc).astype(FULL_TYPE)
    )
    latents = col_sum(
        jnp.concatenate(
            [
                times_transposed(grad_nope, query_nope_all)
                + times_transposed(grad_rope, query_rope_all),
                times_transposed(grad_joint_full, joint_up_all),
                grad_key,
            ],
            axis=1,
        ),
        col_count,
    )
    grad_query_normed = latents[:, :Q_RANK]
    grad_compressed = latents[:, Q_RANK : Q_RANK + KV_RANK]
    grad_rope_sum = latents[:, Q_RANK + KV_RANK :]
    grad_query_latent, gain_query_grad = rms_backward(
        grad_query_normed, query_latent, scale_query, gain_query
    )
    grad_compressed_raw, gain_joint_grad = rms_backward(
        grad_compressed, compressed_raw, scale_joint, gain_joint
    )
    grad_key_raw = grad_rope_sum * cosine + rotate_back(grad_rope_sum * sine)
    grad_latents = jnp.concatenate(
        [grad_query_latent, grad_compressed_raw, grad_key_raw], axis=1
    ).astype(HALF_TYPE)
    grad_normed_one = times_transposed(
        grad_latents[:, :Q_RANK], query_down_all
    ) + times_transposed(grad_latents[:, Q_RANK:], joint_down_all)
    through_one, gain_one_grad = rms_backward(grad_normed_one, inputs, scale_one, gain_one)
    grad_inputs = lax.dynamic_slice_in_dim(
        grad_residual + through_one, col_start, width_share, 1
    ).astype(HALF_TYPE)
    returned = lax.all_to_all(grad_inputs, "row", split_axis=0, concat_axis=0, tiled=True)
    grad_tokens = contract_rows(send_matrix, returned).astype(HALF_TYPE)
    gains_grad = fold_gains(
        jnp.concatenate([gain_one_grad, gain_two_grad, gain_query_grad, gain_joint_grad]),
        row_count,
        shard_rows,
    )
    downs_grad = row.reduce_scatter(
        lambda dx, dc: jnp.concatenate(
            [
                product(row.quarter(normed_one_across, dx, dc), grad_latents),
                row.quarter(gains_grad, dx, dc),
            ],
            axis=1,
        )
    )
    query_fold = taken[3].shape[1]
    reduced = (
        downs_grad[:, :Q_RANK],
        downs_grad[:, Q_RANK : Q_RANK + KV_RANK + ROPE],
        heads_together(
            unfold(heads_grad[:, :query_fold], 1, query_up.shape[0], query_up.shape[1]), heads
        ),
        unfold(heads_grad[:, query_fold:], 1, joint_up.shape[0], joint_up.shape[1]),
        out_grad,
        gate_grad,
        up_grad,
        down_grad,
        unfold_gains(downs_grad[:, Q_RANK + KV_RANK + ROPE :], 1, gain_count),
    )
    step_rates = learning_rates()
    seconds_next = []
    weights_next = []
    for slot_index in range(9):
        second_new, weight_new = adam_update(
            params[slot_index],
            reduced[slot_index],
            firsts[slot_index],
            seconds[slot_index],
            step_rates[slot_index],
        )
        seconds_next.append(second_new)
        weights_next.append(weight_new)
    return (output_pad, grad_tokens) + reduced + tuple(seconds_next) + tuple(weights_next)


def solution(mesh):
    in_specs = (
        P("row", "col"),
        P("row"),
        P("row", None),
        P("row", "col"),
        P("row", None),
        P("row", None),
        P("row", "col"),
        P("row", "col"),
        P("row", "col"),
        P("row", "col"),
        P("row", "col"),
        P("row", "col"),
        P("row"),
        P("row", None),
        P("row", None),
        P("row", "col"),
        P("row", "col"),
        P("row", "col"),
        P("row", "col"),
        P("row", "col"),
        P("row", "col"),
        P("row"),
        P("row", None),
        P("row", None),
        P("row", "col"),
        P("row", "col"),
        P("row", "col"),
        P("row", "col"),
        P("row", "col"),
        P("row", "col"),
        P("row"),
    )
    out_specs = (
        P("row", "col"),
        P("row", "col"),
        P("row", None),
        P("row", None),
        P("row", "col"),
        P("row", "col"),
        P("row", "col"),
        P("row", "col"),
        P("row", "col"),
        P("row", "col"),
        P("row"),
        P("row", None),
        P("row", None),
        P("row", "col"),
        P("row", "col"),
        P("row", "col"),
        P("row", "col"),
        P("row", "col"),
        P("row", "col"),
        P("row"),
        P("row", None),
        P("row", None),
        P("row", "col"),
        P("row", "col"),
        P("row", "col"),
        P("row", "col"),
        P("row", "col"),
        P("row", "col"),
        P("row"),
    )
    return jax.shard_map(body, mesh=mesh, in_specs=in_specs, out_specs=out_specs, check_vma=False)
```

time: 2940 us -> 1270 us (0.43)
  waiting for transfers between devices: 1410 us -> 746 us
  local copies, waits for them, and re-layouts: 715 us -> 77.9 us
  matrix products: 475 us -> 217 us
  blocking collectives: 135 us -> 0 us
  starting transfers between devices: 12.3 us -> 48.3 us
  Pallas kernels: 0 us -> 34.4 us
    reduce_scatter x11 -> x1, waiting for transfers between devices: 853 us -> 0.01 us  [body(): lax.psum_scatter(feed_forward.astype(HALF_TYPE), 'col', scatter_dimension...]
    ppermute x0 -> x41, waiting for transfers between devices: none -> 494 us  [the longest x36 430 us: move(): return lax.ppermute(values, 'row', pairs)]
    all_gather x12 -> x2, waiting for transfers between devices: 544 us -> 217 us  [the longest x1 118 us: body(): gathered_two = lax.all_gather(packed_two, 'row', axis=0, tiled=True)]
    dynamic_update_slice x61 -> x0, local copies, waits for them, and re-layouts: 296 us -> none  [the longest x40 268 us: body(): lax.map(lambda head_items: attend_back(head_items[0], head_items[1], head...]
    dot_general x440 -> x0, matrix products: 290 us -> none  [the longest x80 61.4 us: block_scores(): jnp.einsum('qd,kd->qk', block_queries[:, NOPE:], key_rope, preferred_elem...]
    scatter x5 -> x0, local copies, waits for them, and re-layouts: 155 us -> none  [the longest x4 151 us: to_padded(): jnp.zeros((CAP,) + values.shape[1:], values.dtype).at[arrived_rows]]
    slice x106 -> x19, local copies, waits for them, and re-layouts: 105 us -> 8.5 us  [the longest x5 6.86 us: body(): taken = [gathered_one[:, offsets[i]:offsets[i + 1]] for i in range(6)]]
    dot_general x8 -> x31, matrix products: 64.6 us -> 148 us  [product(): return jnp.dot(left_side, right_side, preferred_element_type=FULL_TYPE)]
  transfers between devices with their start and end apart: 26 -> 47, of which waited for: 19 -> 26; matrix products, arithmetic and copies ran while one was open for 19% -> 26% of each run, Pallas kernels for 0% -> 3%
where the time goes in v1:
time: 1270 us; the launch traced here: 1260 us
  waiting for transfers between devices  746 us (59%)
  matrix products  217 us (17%)
  other arithmetic  123 us (10%)
  local copies, waits for them, and re-layouts  77.9 us (6%)
  starting transfers between devices  48.3 us (4%)
  Pallas kernels  34.4 us (3%)
  between operations  16.7 us (1%)
    ppermute x36, waiting for transfers between devices, move(): return lax.ppermute(values, 'row', pairs)  430 us
    dot_general x31, matrix products, product(): return jnp.dot(left_side, right_side, preferred_element_type=FULL_TYPE)  148 us
    all_gather x1, waiting for transfers between devices, body(): gathered_two = lax.all_gather(packed_two, 'row', axis=0, tiled=True)  118 us
    all_gather x1, waiting for transfers between devices, body(): gathered_one = lax.all_gather(packed_one, 'row', axis=0, tiled=True)  98.9 us
    dot_general x9, matrix products, times_transposed(): lax.dot_general(left_side, right_side, (((1,), (1,)), ((), ())), preferre...  58.5 us
    ppermute x3, waiting for transfers between devices, col_sum(): other = lax.ppermute(half, 'col', [(0, 1), (1, 0)])  45.8 us
    all_to_all x1, waiting for transfers between devices, body(): lax.all_to_all(sorted_tokens, 'row', split_axis=0, concat_axis=0, tiled=T...  30.4 us
    convert_element_type x6, other arithmetic, reduce_scatter(): total = (came.astype(FULL_TYPE) + mine).astype(HALF_TYPE)  30 us
  transfers between devices with their start and end apart: 47, of which 26 were waited for; matrix products, arithmetic and copies ran while one was open for 26% of the time, Pallas kernels for 3%

profile of v1, /device:TPU:0, one launch (start us, length us, event | category | flops | bytes accessed | tf_op | source)
XLA Modules:
  0.0 1264.1 jit_solution(8382638729513519682)
XLA Ops:
  26.8 7.4 all-to-all-start
  52.3 30.4 %all-to-all-done.1 = bf16[16,24,1280]{2,1,0:T(8,128)(2,1)} async-done(((bf16[16,24,1280]{2,1,0:T(8,128)(2,1)}), bf16[16,24,1280]{2,1,0:T(8,128)(2,1)}, u32[]{:S(2)}, u32[]{:S(2)}) %all-to-all-start.1) | async-done | bytes 983072 | tf_op jit(solution)/shard_map/all_to_all | solution.py:578
  88.2 18.1 %collective-permute-done = bf16[384,1280]{1,0:T(8,128)(2,1)} collective-permute-done((bf16[384,1280]{1,0:T(8,128)(2,1)}, bf16[384,1280]{1,0:T(8,128)(2,1)}, u32[]{:S(2)}, u32[]{:S(2)}) %collective-permute-start) | collective-permute-done | bytes 983072 | tf_op jit(solution)/shard_map/ppermute | solution.py:372
  109.2 98.9 %all-gather.3.cloned.1.call-done = bf16[2560,6528]{1,0:T(8,128)(2,1)} async-done(((bf16[160,6528]{1,0:T(8,128)(2,1)}), bf16[2560,6528]{1,0:T(8,128)(2,1)}) %all-gather.3.cloned.1.call-update) | async-done | bytes 33423376 | tf_op jit(solution)/shard_map/all_gather | solution.py:546
  234.5 13.7 %shard_map.518 = (bf16[384,1280]{1,0:T(8,128)(2,1)S(1)}, bf16[384,640]{1,0:T(8,128)(2,1)S(1)}, f32[5,4,384]{2,1,0:T(4,128)S(1)}) custom-call(s32[384,1]{1,0:T(8,128)S(1)} %broadcast_in_dim.37.row_here, s32[1,384]{1,0:T(1,128)S(1)} %broadcast_in_dim.33.row_across, s32[1,384]{1,0:T(1,128)S(1)} %broadcast_in_dim.35.first_across, f32[384,128]{1,0:T(8,128)S(1)} %copy.241.cosine, ...), custom_call_target="tpu_custom_call" | custom-call | flops 943718400 | bytes 6144000 | tf_op jit(solution)/shard_map/pallas_call | solution.py:258
  248.2 8.7 fusion.22
  260.9 118.1 %all-gather.5.cloned.1.call-done = bf16[2560,6400]{1,0:T(8,128)(2,1)} async-done(((bf16[160,6400]{1,0:T(8,128)(2,1)}), bf16[2560,6400]{1,0:T(8,128)(2,1)}) %all-gather.5.cloned.1.call-update) | async-done | bytes 32768016 | tf_op jit(solution)/shard_map/all_gather | solution.py:547
  379.0 13.0 %fusion = f32[384,3200]{1,0:T(8,128)} fusion(bf16[2560,6400]{1,0:T(8,128)(2,1)} %all-gather.5.cloned.1.call-done, bf16[384,1280]{1,0:T(8,128)(2,1)} %get-tuple-element.108, bf16[384,1280]{1,0:T(8,128)(2,1)} %get-tuple-element.107), kind=kOutput, calls=%fused_computation | convolution fusion | flops 6297354240 | bytes 23265280 | tf_op jit(solution)/shard_map/dot_general | solution.py:51
  397.1 13.6 %fusion.6 = f32[384,3200]{1,0:T(8,128)} fusion(bf16[2560,6400]{1,0:T(8,128)(2,1)} %all-gather.5.cloned.1.call-done, f32[384,2560]{1,0:T(8,128)} %get-tuple-element.79, f32[2560]{0:T(1024)S(1)} %get-tuple-element.119, f32[384]{0:T(512)S(1)} %get-tuple-element.130), kind=kOutput, calls=%fused_computation.6 | convolution fusion | flops 6294405120 | bytes 25243136 | tf_op jit(solution)/shard_map/dot_general | solution.py:51
  410.7 17.4 %multiply_convert_fusion.1 = (bf16[384,3200]{1,0:T(8,128)(2,1)}, bf16[384,3200]{1,0:T(8,128)(2,1)}, bf16[384,3200]{1,0:T(8,128)(2,1)}) fusion(f32[384,3200]{1,0:T(8,128)} %fusion, f32[384,3200]{1,0:T(8,128)} %fusion.6, bf16[2560,6528]{1,0:T(8,128)(2,1)} %all-gather.3.cloned.1.call-done, f32[384,2560]{1,0:T(8,128)} %get-tuple-element.79, ...), kind=kOutput, calls=%fused_computation.37 | convolution fusion | flops 6314065920 | bytes 37531136 | tf_op jit(solution)/shard_map/dot_general | solution.py:51
  428.1 11.2 fusion.4
  439.3 11.5 fusion.25
  452.3 11.3 fusion.19
  471.4 45.8 %collective-permute-done.3 = bf16[384,2560]{1,0:T(8,128)(2,1)} collective-permute-done((bf16[384,2560]{1,0:T(8,128)(2,1)}, bf16[384,2560]{1,0:T(8,128)(2,1)}, u32[]{:S(2)}, u32[]{:S(2)}) %collective-permute-start.3) | collective-permute-done | bytes 1966112 | tf_op jit(solution)/shard_map/ppermute | solution.py:383
  535.4 20.7 %shard_map.519 = (bf16[384,1280]{1,0:T(8,128)(2,1)S(1)}, bf16[384,640]{1,0:T(8,128)(2,1)S(1)}, bf16[384,2560]{1,0:T(8,128)(2,1)S(1)}, f32[384,32]{1,0:T(8,128)S(1)}) custom-call(s32[384,1]{1,0:T(8,128)S(1)} %broadcast_in_dim.37.row_here, s32[1,384]{1,0:T(1,128)S(1)} %broadcast_in_dim.33.row_across, s32[1,384]{1,0:T(1,128)S(1)} %broadcast_in_dim.35.first_across, ...), custom_call_target="tpu_custom_call" | custom-call | flops 2654208000 | bytes 9216000 | tf_op jit(solution)/shard_map/pallas_call | solution.py:282
  695.9 17.8 %collective-permute-done.12 = bf16[640,896]{1,0:T(8,128)(2,1)S(1)} collective-permute-done((bf16[640,896]{1,0:T(8,128)(2,1)S(1)}, bf16[640,896]{1,0:T(8,128)(2,1)S(1)}, u32[]{:S(2)}, u32[]{:S(2)}) %collective-permute-start.12) | collective-permute-done | bytes 1146912 | tf_op jit(solution)/shard_map/ppermute | solution.py:328
  775.5 29.8 %collective-permute-done.18 = bf16[640,1280]{1,0:T(8,128)(2,1)S(1)} collective-permute-done((bf16[640,1280]{1,0:T(8,128)(2,1)}, bf16[640,1280]{1,0:T(8,128)(2,1)S(1)}, u32[]{:S(2)}, u32[]{:S(2)}) %collective-permute-start.18) | collective-permute-done | bytes 1638432 | tf_op jit(solution)/shard_map/ppermute | solution.py:328
  832.5 10.2 collective-permute-done.10
  846.0 8.6 collective-permute-done.21
  859.0 7.5 collective-permute-done.22
  869.8 44.2 %collective-permute-done.24 = bf16[640,3200]{1,0:T(8,128)(2,1)} collective-permute-done((bf16[640,3200]{1,0:T(8,128)(2,1)}, bf16[640,3200]{1,0:T(8,128)(2,1)}, u32[]{:S(2)}, u32[]{:S(2)}) %collective-permute-start.24) | collective-permute-done | bytes 4096032 | tf_op jit(solution)/shard_map/ppermute | solution.py:328
  914.0 9.0 add_convert_fusion.4
  925.9 75.9 %collective-permute-done.30 = bf16[640,3200]{1,0:T(8,128)(2,1)} collective-permute-done((bf16[640,3200]{1,0:T(8,128)(2,1)}, bf16[640,3200]{1,0:T(8,128)(2,1)}, u32[]{:S(2)}, u32[]{:S(2)}) %collective-permute-start.30) | collective-permute-done | bytes 4096032 | tf_op jit(solution)/shard_map/ppermute | solution.py:328
  1011.6 76.9 %collective-permute-done.36 = bf16[640,3200]{1,0:T(8,128)(2,1)} collective-permute-done((bf16[640,3200]{1,0:T(8,128)(2,1)}, bf16[640,3200]{1,0:T(8,128)(2,1)}, u32[]{:S(2)}, u32[]{:S(2)}) %collective-permute-start.36) | collective-permute-done | bytes 4096032 | tf_op jit(solution)/shard_map/ppermute | solution.py:328
  1088.5 7.1 add_convert_fusion
  1104.8 18.3 %collective-permute-done.38 = bf16[160,3200]{1,0:T(8,128)(2,1)S(1)} collective-permute-done((bf16[160,3200]{1,0:T(8,128)(2,1)S(1)}, bf16[160,3200]{1,0:T(8,128)(2,1)S(1)}, u32[]{:S(2)}, u32[]{:S(2)}) %collective-permute-start.38) | collective-permute-done | bytes 1024032 | tf_op jit(solution)/shard_map/ppermute | solution.py:328
  1123.4 21.6 %collective-permute-done.27 = bf16[160,3200]{1,0:T(8,128)(2,1)S(1)} collective-permute-done((bf16[160,3200]{1,0:T(8,128)(2,1)S(1)}, bf16[160,3200]{1,0:T(8,128)(2,1)S(1)}, u32[]{:S(2)}, u32[]{:S(2)}) %collective-permute-start.27) | collective-permute-done | bytes 1024032 | tf_op jit(solution)/shard_map/ppermute | solution.py:328
  1145.4 21.6 %collective-permute-done.33 = bf16[160,3200]{1,0:T(8,128)(2,1)S(1)} collective-permute-done((bf16[160,3200]{1,0:T(8,128)(2,1)S(1)}, bf16[160,3200]{1,0:T(8,128)(2,1)S(1)}, u32[]{:S(2)}, u32[]{:S(2)}) %collective-permute-start.33) | collective-permute-done | bytes 1024032 | tf_op jit(solution)/shard_map/ppermute | solution.py:328
  1168.2 20.7 %collective-permute-done.39 = bf16[160,3200]{1,0:T(8,128)(2,1)S(1)} collective-permute-done((bf16[160,3200]{1,0:T(8,128)(2,1)S(1)}, bf16[160,3200]{1,0:T(8,128)(2,1)S(1)}, u32[]{:S(2)}, u32[]{:S(2)}) %collective-permute-start.39) | collective-permute-done | bytes 1024032 | tf_op jit(solution)/shard_map/ppermute | solution.py:328
  1190.2 20.7 %collective-permute-done.28 = bf16[160,3200]{1,0:T(8,128)(2,1)S(1)} collective-permute-done((bf16[160,3200]{1,0:T(8,128)(2,1)S(1)}, bf16[160,3200]{1,0:T(8,128)(2,1)S(1)}, u32[]{:S(2)}, u32[]{:S(2)}) %collective-permute-start.28) | collective-permute-done | bytes 1024032 | tf_op jit(solution)/shard_map/ppermute | solution.py:328
  1214.1 18.8 %collective-permute-done.34 = bf16[160,3200]{1,0:T(8,128)(2,1)S(1)} collective-permute-done((bf16[160,3200]{1,0:T(8,128)(2,1)}, bf16[160,3200]{1,0:T(8,128)(2,1)S(1)}, u32[]{:S(2)}, u32[]{:S(2)}) %collective-permute-start.34) | collective-permute-done | bytes 1024032 | tf_op jit(solution)/shard_map/ppermute | solution.py:328
  1236.0 16.8 %collective-permute-done.40 = bf16[160,3200]{1,0:T(8,128)(2,1)S(1)} collective-permute-done((bf16[160,3200]{1,0:T(8,128)(2,1)}, bf16[160,3200]{1,0:T(8,128)(2,1)S(1)}, u32[]{:S(2)}, u32[]{:S(2)}) %collective-permute-start.40) | collective-permute-done | bytes 1024032 | tf_op jit(solution)/shard_map/ppermute | solution.py:328
  (566 shorter events, 382.2 us)
Async XLA Ops:
  7.2 200.8 %all-gather.3.cloned.1.call-start = ((), (), s32[]{:S(2)}) async-start(), calls=%async_computation.4 | async-start | bytes 35512320 | tf_op jit(solution)/shard_map/all_gather | solution.py:546
  21.8 357.2 %all-gather.5.cloned.1.call-start = ((), (), s32[]{:S(2)}) async-start(), calls=%async_computation.5 | async-start | bytes 34816000 | tf_op jit(solution)/shard_map/all_gather | solution.py:547
  40.6 42.1 %all-to-all-start.1 = ((bf16[16,24,1280]{2,1,0:T(8,128)(2,1)}), bf16[16,24,1280]{2,1,0:T(8,128)(2,1)}, u32[]{:S(2)}, u32[]{:S(2)}) async-start(bf16[16,24,1280]{2,1,0:T(8,128)(2,1)} %bitcast), calls=%async_computation.1 | async-start | bytes 1966080 | tf_op jit(solution)/shard_map/all_to_all | solution.py:578
  45.0 681.8 %reduce-scatter.2.cloned.1.call-start = ((), (), s32[]{:S(2)}) async-start(), calls=%async_computation.6 | async-start | bytes 2949120 | tf_op jit(solution)/shard_map/reduce_scatter | solution.py:654
  50.5 35.1 %collective-permute-start.2 = (bf16[384,1280]{1,0:T(8,128)(2,1)}, bf16[384,1280]{1,0:T(8,128)(2,1)S(1)}, u32[]{:S(2)}, u32[]{:S(2)}) collective-permute-start(bf16[384,1280]{1,0:T(8,128)(2,1)} %convolution_convert_fusion.14), channel_id=1, source_target_pairs={{0,1},{1,0},{2,3},{3,2},{4,5},{5,4},{6,7},{7,6},{8,9},{9,8},{10,11... | collective-permute-start | bytes 2949128 | tf_op jit(solution)/shard_map/ppermute | solution.py:372
  257.0 135.0 %collective-permute-start.1 = (bf16[384,2560]{1,0:T(8,128)(2,1)}, bf16[384,2560]{1,0:T(8,128)(2,1)}, u32[]{:S(2)}, u32[]{:S(2)}) collective-permute-start(bf16[384,2560]{1,0:T(8,128)(2,1)} %fusion.22), channel_id=1, source_target_pairs={{0,1},{1,0},{2,3},{3,2},{4,5},{5,4},{6,7},{7,6},{8,9},{9,8},{10,11... | collective-permute-start | bytes 5898248 | tf_op jit(solution)/shard_map/ppermute | solution.py:383
  450.8 66.4 %collective-permute-start.3 = (bf16[384,2560]{1,0:T(8,128)(2,1)}, bf16[384,2560]{1,0:T(8,128)(2,1)}, u32[]{:S(2)}, u32[]{:S(2)}) collective-permute-start(bf16[384,2560]{1,0:T(8,128)(2,1)} %fusion.25), channel_id=1, source_target_pairs={{0,1},{1,0},{2,3},{3,2},{4,5},{5,4},{6,7},{7,6},{8,9},{9,8},{10,11... | collective-permute-start | bytes 5898248 | tf_op jit(solution)/shard_map/ppermute | solution.py:383
  606.9 35.9 %collective-permute-start.4 = (bf16[384,1056]{0,1:T(8,128)(2,1)}, bf16[384,1056]{0,1:T(8,128)(2,1)}, u32[]{:S(2)}, u32[]{:S(2)}) collective-permute-start(bf16[384,1056]{0,1:T(8,128)(2,1)} %pad_maximum_fusion.6), channel_id=1, source_target_pairs={{0,1},{1,0},{2,3},{3,2},{4,5},{5,4},{6,7},{7,6},{8,9},{9,8},{10,11... | collective-permute-start | bytes 2433032 | tf_op jit(solution)/shard_map/ppermute | solution.py:383
  627.6 68.3 %collective-permute-start.13 = (bf16[640,896]{1,0:T(8,128)(2,1)}, bf16[640,896]{1,0:T(8,128)(2,1)}, u32[]{:S(2)}, u32[]{:S(2)}) collective-permute-start(bf16[640,896]{1,0:T(8,128)(2,1)} %bitcast.45), channel_id=1, source_target_pairs={{0,2},{2,0},{4,6},{6,4},{8,10},{10,8},{12,14},{14,12},{16,18},{18,... | collective-permute-start | bytes 3440648 | tf_op jit(solution)/shard_map/ppermute | solution.py:328
  627.6 56.6 %collective-permute-start.11 = (bf16[640,896]{1,0:T(8,128)(2,1)}, bf16[640,896]{1,0:T(8,128)(2,1)}, u32[]{:S(2)}, u32[]{:S(2)}) collective-permute-start(bf16[640,896]{1,0:T(8,128)(2,1)} %bitcast.43), channel_id=1, source_target_pairs={{0,2},{2,0},{4,6},{6,4},{8,10},{10,8},{12,14},{14,12},{16,18},{18,... | collective-permute-start | bytes 3440648 | tf_op jit(solution)/shard_map/ppermute | solution.py:328
  628.1 179.3 %collective-permute-start.23 = (bf16[640,3200]{1,0:T(8,128)(2,1)}, bf16[640,3200]{1,0:T(8,128)(2,1)}, u32[]{:S(2)}, u32[]{:S(2)}) collective-permute-start(bf16[640,3200]{1,0:T(8,128)(2,1)} %convolution_convert_fusion.5), channel_id=1, source_target_pairs={{0,2},{2,0},{4,6},{6,4},{8,10},{10,8},{12,14},{14,12},{16,18},{18,... | collective-permute-start | bytes 12288008 | tf_op jit(solution)/shard_map/ppermute | solution.py:328
  662.2 77.5 %all-to-all-start.2 = ((bf16[16,24,1280]{2,1,0:T(8,128)(2,1)}), bf16[16,24,1280]{2,1,0:T(8,128)(2,1)}, u32[]{:S(2)}, u32[]{:S(2)}) async-start(bf16[16,24,1280]{2,1,0:T(8,128)(2,1)} %bitcast.23), calls=%async_computation.3 | async-start | bytes 1966080 | tf_op jit(solution)/shard_map/all_to_all | solution.py:719
  677.9 71.0 %collective-permute-start.7 = (bf16[640,1088]{0,1:T(8,128)(2,1)}, bf16[640,1088]{0,1:T(8,128)(2,1)}, u32[]{:S(2)}, u32[]{:S(2)}) collective-permute-start(bf16[640,1088]{0,1:T(8,128)(2,1)} %pad_maximum_fusion.5), channel_id=1, source_target_pairs={{0,2},{2,0},{4,6},{6,4},{8,10},{10,8},{12,14},{14,12},{16,18},{18,... | collective-permute-start | bytes 4177928 | tf_op jit(solution)/shard_map/ppermute | solution.py:328
  681.4 36.8 %collective-permute-start.5 = (bf16[640,1088]{0,1:T(8,128)(2,1)S(1)}, bf16[640,1088]{0,1:T(8,128)(2,1)S(1)}, u32[]{:S(2)}, u32[]{:S(2)}) collective-permute-start(bf16[640,1088]{0,1:T(8,128)(2,1)S(1)} %pad_maximum_fusion.4), channel_id=1, source_target_pairs={{0,2},{2,0},{4,6},{6,4},{8,10},{10,8},{12,14},{14,12},{16,18},{18,... | collective-permute-start | bytes 4177928 | tf_op jit(solution)/shard_map/ppermute | solution.py:328
  695.9 39.7 %collective-permute-start.17 = (bf16[640,1280]{1,0:T(8,128)(2,1)}, bf16[640,1280]{1,0:T(8,128)(2,1)}, u32[]{:S(2)}, u32[]{:S(2)}) collective-permute-start(bf16[640,1280]{1,0:T(8,128)(2,1)} %convolution_convert_fusion.13), channel_id=1, source_target_pairs={{0,2},{2,0},{4,6},{6,4},{8,10},{10,8},{12,14},{14,12},{16,18},{18,... | collective-permute-start | bytes 4915208 | tf_op jit(solution)/shard_map/ppermute | solution.py:328
  735.5 78.8 %collective-permute-start.29 = (bf16[640,3200]{1,0:T(8,128)(2,1)}, bf16[640,3200]{1,0:T(8,128)(2,1)}, u32[]{:S(2)}, u32[]{:S(2)}) collective-permute-start(bf16[640,3200]{1,0:T(8,128)(2,1)} %convolution_convert_fusion.3), channel_id=1, source_target_pairs={{0,2},{2,0},{4,6},{6,4},{8,10},{10,8},{12,14},{14,12},{16,18},{18,... | collective-permute-start | bytes 12288008 | tf_op jit(solution)/shard_map/ppermute | solution.py:328
  747.1 75.2 %collective-permute-start.35 = (bf16[640,3200]{1,0:T(8,128)(2,1)}, bf16[640,3200]{1,0:T(8,128)(2,1)}, u32[]{:S(2)}, u32[]{:S(2)}) collective-permute-start(bf16[640,3200]{1,0:T(8,128)(2,1)} %convolution_convert_fusion.1), channel_id=1, source_target_pairs={{0,2},{2,0},{4,6},{6,4},{8,10},{10,8},{12,14},{14,12},{16,18},{18,... | collective-permute-start | bytes 12288008 | tf_op jit(solution)/shard_map/ppermute | solution.py:328
  769.6 35.7 %collective-permute-start.18 = (bf16[640,1280]{1,0:T(8,128)(2,1)}, bf16[640,1280]{1,0:T(8,128)(2,1)S(1)}, u32[]{:S(2)}, u32[]{:S(2)}) collective-permute-start(bf16[640,1280]{1,0:T(8,128)(2,1)} %add_convert_fusion.7), channel_id=1, source_target_pairs={{0,4},{2,6},{4,0},{6,2},{8,12},{10,14},{12,8},{14,10},{16,20},{18,... | collective-permute-start | bytes 4915208 | tf_op jit(solution)/shard_map/ppermute | solution.py:328
  775.4 83.6 %collective-permute-start.25 = (bf16[640,3200]{1,0:T(8,128)(2,1)}, bf16[640,3200]{1,0:T(8,128)(2,1)}, u32[]{:S(2)}, u32[]{:S(2)}) collective-permute-start(bf16[640,3200]{1,0:T(8,128)(2,1)} %convolution_convert_fusion.4), channel_id=1, source_target_pairs={{0,2},{2,0},{4,6},{6,4},{8,10},{10,8},{12,14},{14,12},{16,18},{18,... | collective-permute-start | bytes 12288008 | tf_op jit(solution)/shard_map/ppermute | solution.py:328
  805.3 120.6 %collective-permute-start.31 = (bf16[640,3200]{1,0:T(8,128)(2,1)}, bf16[640,3200]{1,0:T(8,128)(2,1)}, u32[]{:S(2)}, u32[]{:S(2)}) collective-permute-start(bf16[640,3200]{1,0:T(8,128)(2,1)} %convolution_convert_fusion.2), channel_id=1, source_target_pairs={{0,2},{2,0},{4,6},{6,4},{8,10},{10,8},{12,14},{14,12},{16,18},{18,... | collective-permute-start | bytes 12288008 | tf_op jit(solution)/shard_map/ppermute | solution.py:328
  822.3 91.7 %collective-permute-start.24 = (bf16[640,3200]{1,0:T(8,128)(2,1)}, bf16[640,3200]{1,0:T(8,128)(2,1)}, u32[]{:S(2)}, u32[]{:S(2)}) collective-permute-start(bf16[640,3200]{1,0:T(8,128)(2,1)} %add_convert_fusion.5), channel_id=1, source_target_pairs={{0,4},{2,6},{4,0},{6,2},{8,12},{10,14},{12,8},{14,10},{16,20},{18,... | collective-permute-start | bytes 12288008 | tf_op jit(solution)/shard_map/ppermute | solution.py:328
  829.9 171.8 %collective-permute-start.30 = (bf16[640,3200]{1,0:T(8,128)(2,1)}, bf16[640,3200]{1,0:T(8,128)(2,1)}, u32[]{:S(2)}, u32[]{:S(2)}) collective-permute-start(bf16[640,3200]{1,0:T(8,128)(2,1)} %add_convert_fusion.3), channel_id=1, source_target_pairs={{0,4},{2,6},{4,0},{6,2},{8,12},{10,14},{12,8},{14,10},{16,20},{18,... | collective-permute-start | bytes 12288008 | tf_op jit(solution)/shard_map/ppermute | solution.py:328
  859.0 152.6 %collective-permute-start.37 = (bf16[640,3200]{1,0:T(8,128)(2,1)}, bf16[640,3200]{1,0:T(8,128)(2,1)}, u32[]{:S(2)}, u32[]{:S(2)}) collective-permute-start(bf16[640,3200]{1,0:T(8,128)(2,1)} %convolution_convert_fusion), channel_id=1, source_target_pairs={{0,2},{2,0},{4,6},{6,4},{8,10},{10,8},{12,14},{14,12},{16,18},{18,... | collective-permute-start | bytes 12288008 | tf_op jit(solution)/shard_map/ppermute | solution.py:328
  866.5 222.0 %collective-permute-start.36 = (bf16[640,3200]{1,0:T(8,128)(2,1)}, bf16[640,3200]{1,0:T(8,128)(2,1)}, u32[]{:S(2)}, u32[]{:S(2)}) collective-permute-start(bf16[640,3200]{1,0:T(8,128)(2,1)} %add_convert_fusion.1), channel_id=1, source_target_pairs={{0,4},{2,6},{4,0},{6,2},{8,12},{10,14},{12,8},{14,10},{16,20},{18,... | collective-permute-start | bytes 12288008 | tf_op jit(solution)/shard_map/ppermute | solution.py:328
  925.2 171.3 %collective-permute-start.26 = (bf16[160,3200]{1,0:T(8,128)(2,1)}, bf16[160,3200]{1,0:T(8,128)(2,1)}, u32[]{:S(2)}, u32[]{:S(2)}) collective-permute-start(bf16[160,3200]{1,0:T(8,128)(2,1)} %dynamic-slice_bitcast_fusion.2), channel_id=1, source_target_pairs={{0,8},{2,10},{4,12},{6,14},{8,16},{10,18},{12,20},{14,22},{16,24},... | collective-permute-start | bytes 3072008 | tf_op jit(solution)/shard_map/ppermute | solution.py:328
  1011.0 89.9 %collective-permute-start.32 = (bf16[160,3200]{1,0:T(8,128)(2,1)}, bf16[160,3200]{1,0:T(8,128)(2,1)}, u32[]{:S(2)}, u32[]{:S(2)}) collective-permute-start(bf16[160,3200]{1,0:T(8,128)(2,1)} %dynamic-slice_bitcast_fusion.1), channel_id=1, source_target_pairs={{0,8},{2,10},{4,12},{6,14},{8,16},{10,18},{12,20},{14,22},{16,24},... | collective-permute-start | bytes 3072008 | tf_op jit(solution)/shard_map/ppermute | solution.py:328
  1099.6 45.5 %collective-permute-start.27 = (bf16[160,3200]{1,0:T(8,128)(2,1)S(1)}, bf16[160,3200]{1,0:T(8,128)(2,1)S(1)}, u32[]{:S(2)}, u32[]{:S(2)}) collective-permute-start(bf16[160,3200]{1,0:T(8,128)(2,1)S(1)} %fusion.57), channel_id=1, source_target_pairs={{0,8},{2,10},{4,12},{6,14},{8,16},{10,18},{12,20},{14,22},{16,24},... | collective-permute-start | bytes 3072008 | tf_op jit(solution)/shard_map/ppermute | solution.py:328
  1102.3 64.7 %collective-permute-start.33 = (bf16[160,3200]{1,0:T(8,128)(2,1)S(1)}, bf16[160,3200]{1,0:T(8,128)(2,1)S(1)}, u32[]{:S(2)}, u32[]{:S(2)}) collective-permute-start(bf16[160,3200]{1,0:T(8,128)(2,1)S(1)} %fusion.55), channel_id=1, source_target_pairs={{0,8},{2,10},{4,12},{6,14},{8,16},{10,18},{12,20},{14,22},{16,24},... | collective-permute-start | bytes 3072008 | tf_op jit(solution)/shard_map/ppermute | solution.py:328
  1123.4 65.6 %collective-permute-start.39 = (bf16[160,3200]{1,0:T(8,128)(2,1)S(1)}, bf16[160,3200]{1,0:T(8,128)(2,1)S(1)}, u32[]{:S(2)}, u32[]{:S(2)}) collective-permute-start(bf16[160,3200]{1,0:T(8,128)(2,1)S(1)} %fusion.53), channel_id=1, source_target_pairs={{0,8},{2,10},{4,12},{6,14},{8,16},{10,18},{12,20},{14,22},{16,24},... | collective-permute-start | bytes 3072008 | tf_op jit(solution)/shard_map/ppermute | solution.py:328
  1145.3 65.6 %collective-permute-start.28 = (bf16[160,3200]{1,0:T(8,128)(2,1)S(1)}, bf16[160,3200]{1,0:T(8,128)(2,1)S(1)}, u32[]{:S(2)}, u32[]{:S(2)}) collective-permute-start(bf16[160,3200]{1,0:T(8,128)(2,1)S(1)} %fusion.56), channel_id=1, source_target_pairs={{0,8},{2,10},{4,12},{6,14},{8,16},{10,18},{12,20},{14,22},{16,24},... | collective-permute-start | bytes 3072008 | tf_op jit(solution)/shard_map/ppermute | solution.py:328
  1168.2 64.6 %collective-permute-start.34 = (bf16[160,3200]{1,0:T(8,128)(2,1)}, bf16[160,3200]{1,0:T(8,128)(2,1)S(1)}, u32[]{:S(2)}, u32[]{:S(2)}) collective-permute-start(bf16[160,3200]{1,0:T(8,128)(2,1)} %fusion.54), channel_id=1, source_target_pairs={{0,8},{2,10},{4,12},{6,14},{8,16},{10,18},{12,20},{14,22},{16,24},... | collective-permute-start | bytes 3072008 | tf_op jit(solution)/shard_map/ppermute | solution.py:328
  1190.1 62.7 %collective-permute-start.40 = (bf16[160,3200]{1,0:T(8,128)(2,1)}, bf16[160,3200]{1,0:T(8,128)(2,1)S(1)}, u32[]{:S(2)}, u32[]{:S(2)}) collective-permute-start(bf16[160,3200]{1,0:T(8,128)(2,1)} %fusion.52), channel_id=1, source_target_pairs={{0,8},{2,10},{4,12},{6,14},{8,16},{10,18},{12,20},{14,22},{16,24},... | collective-permute-start | bytes 3072008 | tf_op jit(solution)/shard_map/ppermute | solution.py:328
  (150 other events, 2562.3 us)
Sparse Core Ops, SparseCore 0:
  21.9 186.0 all-gather.2
  210.2 168.7 all-gather.4
  463.7 50.6 reduce-scatter.1

commit v2 on v1

--- a/solution.py
+++ b/solution.py
@@ -267,11 +267,7 @@
         ],
         scratch_shapes=[pltpu.VMEM((tokens, tokens), FULL_TYPE)],
         compiler_params=pltpu.CompilerParams(vmem_limit_bytes=40 << 20),
-        cost_estimate=pl.CostEstimate(
-            flops=heads * tokens * tokens * 320,
-            bytes_accessed=tokens * heads * 800,
-            transcendentals=heads * tokens * tokens,
-        ),
+        cost_estimate=hint(),
     )(*places, key_rope, query_nope, query_rope, joint)
 
 
@@ -298,12 +294,131 @@
         ],
         scratch_shapes=[pltpu.VMEM((tokens, tokens), FULL_TYPE)],
         compiler_params=pltpu.CompilerParams(vmem_limit_bytes=40 << 20),
-        cost_estimate=pl.CostEstimate(
-            flops=heads * tokens * tokens * 900,
-            bytes_accessed=tokens * heads * 1200,
-            transcendentals=heads * tokens * tokens,
+        cost_estimate=hint(),
+    )(*places, key_rope, query_nope, rotated, joint, grad_out, log_totals)
+
+
+LANES = 128
+KERNEL_MEMORY = 58 << 20
+
+
+def tile_of(width, most):
+    return max(
+        (tile for tile in range(LANES, most + 1, LANES) if width % tile == 0), default=None
+    )
+
+
+def hint():
+    return pl.CostEstimate(flops=1, bytes_accessed=1, transcendentals=0)
+
+
+def feed_terms(gate_rows, up_rows, grad_act):
+    sigmoid_gate = 1.0 / (1.0 + jnp.exp(-gate_rows))
+    silu = gate_rows * sigmoid_gate
+    activated = silu * up_rows
+    grad_gate = grad_act * up_rows * sigmoid_gate * (1.0 + gate_rows * (1.0 - sigmoid_gate))
+    return [value.astype(HALF_TYPE) for value in (activated, grad_gate, grad_act * silu)]
+
+
+def feed_kernel(normed, ffn_grad, gate, up, down, activated, grad_gate, grad_up):
+    gate_rows = kernel_dot(normed[...], gate[...], NN)
+    up_rows = kernel_dot(normed[...], up[...], NN)
+    grad_act = kernel_dot(ffn_grad[...], down[...], NN)
+    activated[...], grad_gate[...], grad_up[...] = feed_terms(gate_rows, up_rows, grad_act)
+
+
+def feed_part(normed, ffn_grad, gathered, width):
+    tokens, depth = normed.shape
+    tile = tile_of(width, 512)
+    if tile is None:
+        gate, up, down = [gathered[:, index * width : (index + 1) * width] for index in range(3)]
+        return feed_terms(product(normed, gate), product(normed, up), product(ffn_grad, down))
+    count = width // tile
+    whole = pl.BlockSpec((tokens, depth), lambda step: (0, 0))
+    part = lambda index: pl.BlockSpec((depth, tile), lambda step: (0, index * count + step))
+    return pl.pallas_call(
+        feed_kernel,
+        grid=(count,),
+        in_specs=[whole, whole, part(0), part(1), part(2)],
+        out_specs=[pl.BlockSpec((tokens, tile), lambda step: (0, step))] * 3,
+        out_shape=[jax.ShapeDtypeStruct((tokens, width), HALF_TYPE)] * 3,
+        compiler_params=pltpu.CompilerParams(vmem_limit_bytes=KERNEL_MEMORY),
+        cost_estimate=hint(),
+    )(normed, ffn_grad, gathered, gathered, gathered)
+
+
+def across_kernel(count, *refs):
+    total = kernel_dot(refs[0][...], refs[count][...], NT)
+    for index in range(1, count):
+        total = total + kernel_dot(refs[index][...], refs[count + index][...], NT)
+    for more in refs[2 * count : -1]:
+        total = total + more[...]
+    refs[-1][...] = total.astype(refs[-1].dtype)
+
+
+def across_part(sides, places, gathered, earlier, kind):
+    tokens, width = sides[0].shape
+    depth = gathered.shape[0]
+    if width % LANES:
+        total = sum(
+            times_transposed(side, gathered[:, place * width : (place + 1) * width])
+            for side, place in zip(sides, places, strict=True)
+        )
+        return sum(earlier, total).astype(kind)
+    tile = tile_of(depth, 512)
+    block = pl.BlockSpec((tokens, tile), lambda step: (0, step))
+    rows = lambda place: pl.BlockSpec((tile, width), lambda step: (step, place))
+    return pl.pallas_call(
+        functools.partial(across_kernel, len(sides)),
+        grid=(depth // tile,),
+        in_specs=[pl.BlockSpec((tokens, width), lambda step: (0, 0))] * len(sides)
+        + [rows(place) for place in places]
+        + [block] * len(earlier),
+        out_specs=block,
+        out_shape=jax.ShapeDtypeStruct((tokens, depth), kind),
+        compiler_params=pltpu.CompilerParams(vmem_limit_bytes=KERNEL_MEMORY),
+        cost_estimate=hint(),
+    )(*sides, *[gathered] * len(sides), *earlier)
+
+
+def piece_kernel(places, left_side, right_side, *refs):
+    rows = left_side[...].reshape(-1, left_side.shape[-1])
+    total = kernel_dot(rows, right_side[...], NN)
+    for more in refs[:-1]:
+        total = total + more[...].astype(FULL_TYPE)
+    refs[-1][...] = total.astype(HALF_TYPE)
+
+
+def piece_product(blocks, x_at, core_at, right_side, earlier):
+    z_size, _, _, rows, tokens = blocks.shape
+    width = right_side.shape[1]
+    tile = tile_of(width, 1280)
+    if tile is None or rows % 16:
+        left_side = lax.dynamic_slice(
+            blocks, (0, x_at, core_at, 0, 0), (z_size, 1, 1, rows, tokens)
+        )
+        total = product(left_side.reshape(-1, tokens), right_side)
+        return sum([more.astype(FULL_TYPE) for more in earlier], total).astype(HALF_TYPE)
+    block = pl.BlockSpec((z_size * rows, tile), lambda step, places: (0, step))
+    return pl.pallas_call(
+        piece_kernel,
+        grid_spec=pltpu.PrefetchScalarGridSpec(
+            num_scalar_prefetch=1,
+            grid=(width // tile,),
+            in_specs=[
+                pl.BlockSpec(
+                    (z_size, 1, 1, rows, tokens),
+                    lambda step, places: (0, places[0], places[1], 0, 0),
+                ),
+                pl.BlockSpec((tokens, tile), lambda step, places: (0, step)),
+            ]
+            + [block] * len(earlier),
+            out_specs=block,
         ),
-    )(*places, key_rope, query_nope, rotated, joint, grad_out, log_totals)
+        out_shape=jax.ShapeDtypeStruct((z_size * rows, width), HALF_TYPE),
+        compiler_params=pltpu.CompilerParams(vmem_limit_bytes=KERNEL_MEMORY),
+        cost_estimate=hint(),
+    )(jnp.stack([x_at, core_at]).astype(jnp.int32), blocks, right_side, *earlier)
 
 
 class Row:
@@ -314,6 +429,7 @@
         self.z = index // (self.x_size * CORES)
         self.x = (index // CORES) % self.x_size
         self.core = index % CORES
+        self.x_link = Link(functools.partial(self.move, dx=1))
 
     def move(self, values, dz=0, dx=0, dc=0):
         def at(z, x, c):
@@ -340,30 +456,125 @@
         )
         return part.reshape((-1, array.shape[1]))
 
-    def reduce_scatter(self, piece):
-        def over_cores(dx):
-            other = self.move(piece(dx, 1).astype(HALF_TYPE), dc=1)
-            return piece(dx, 0) + other.astype(FULL_TYPE)
-
-        total = over_cores(self.x_size - 1).astype(HALF_TYPE)
-        for step in range(1, self.x_size):
-            came = self.move(total, dx=1)
-            mine = over_cores(self.x_size - 1 - step)
-            total = (came.astype(FULL_TYPE) + mine).astype(HALF_TYPE)
-        blocks = total.reshape((Z_SIZE, -1, total.shape[1]))
-
-        def block(dz):
+    def halves(self, array, dc):
+        blocks = array.reshape(
+            (Z_SIZE * self.x_size, CORES, array.shape[0] // self.size, array.shape[1])
+        )
+        part = lax.dynamic_slice_in_dim(blocks, lax.rem(self.core + dc, CORES), 1, 1)
+        return part.reshape((-1, array.shape[1]))
+
+    def over_cores(self, terms):
+        other = self.move(terms(1).astype(HALF_TYPE), dc=1)
+        return terms(0) + other.astype(FULL_TYPE)
+
+    def over_z(self, values):
+        lines = [
+            [(z * self.x_size + x) * CORES + c for z in range(Z_SIZE)]
+            for x in range(self.x_size)
+            for c in range(CORES)
+        ]
+        found = lax.psum_scatter(
+            values, "row", scatter_dimension=0, axis_index_groups=lines, tiled=True
+        )
+        return found.astype(FULL_TYPE)
+
+    def over_z_direct(self, values, *earlier):
+        blocks = values.reshape((Z_SIZE, -1, values.shape[1]))
+
+        def block(ahead):
             return lax.dynamic_index_in_dim(
-                blocks, lax.rem(self.z + dz, Z_SIZE), 0, keepdims=False
+                blocks, lax.rem(self.z + ahead, Z_SIZE), 0, keepdims=False
             )
 
-        total = block(Z_SIZE - 1)
-        for step in range(1, Z_SIZE):
-            came = self.move(total, dz=1)
-            total = came.astype(FULL_TYPE) + block(Z_SIZE - 1 - step).astype(FULL_TYPE)
-            if step < Z_SIZE - 1:
-                total = total.astype(HALF_TYPE)
+        total = block(0).astype(FULL_TYPE)
+        for ahead in range(1, Z_SIZE):
+            came = after(self.move(block(ahead), dz=ahead), *earlier)
+            total = total + came.astype(FULL_TYPE)
         return total
+
+
+def after(values, *earlier):
+    return lax.optimization_barrier((values, earlier))[0]
+
+
+class Link:
+    def __init__(self, move):
+        self.move = move
+        self.came = None
+
+    def send(self, values, *earlier, last=True):
+        if self.came is not None:
+            values = after(values, self.came, *earlier)
+        came = self.move(values)
+        if last:
+            self.came = came
+        return (values, came)
+
+
+class Sum:
+    def __init__(self, row, terms):
+        self.row = row
+        self.terms = terms
+
+    def over_cores(self, dx):
+        other = self.row.move(self.terms(dx, 1, ()), dc=1)
+        return self.terms(dx, 0, (other,))
+
+    def prepare(self):
+        self.total = self.over_cores(self.row.x_size - 1)
+        return self.total
+
+    def send(self, *earlier, last=True):
+        sent, self.came = self.row.x_link.send(self.total, *earlier, last=last)
+        return sent
+
+    def hold(self):
+        terms = self.terms(0, 1, ())
+        self.other = self.row.move(terms, dc=1)
+        return terms
+
+    def finish(self, *earlier):
+        came = after(self.came, *earlier)
+        for dx in range(self.row.x_size - 2, -1, -1):
+            other = self.row.move(self.terms(dx, 1, ()), dc=1) if dx else self.other
+            total = self.terms(dx, 0, (other, came))
+            if dx:
+                came = self.row.move(total, dx=1)
+        return total
+
+
+class Terms:
+    def __init__(self, row, across, right_side):
+        self.row = row
+        self.blocks = across.reshape((Z_SIZE, row.x_size, CORES, -1, across.shape[1]))
+        self.right_side = right_side
+
+    def __call__(self, dx, dc, earlier):
+        x_at = lax.rem(self.row.x + dx, self.row.x_size)
+        core_at = lax.rem(self.row.core + dc, CORES)
+        return piece_product(self.blocks, x_at, core_at, self.right_side, earlier)
+
+    def wait(self, *earlier):
+        self.right_side = after(self.right_side, *earlier)
+
+
+def taken_terms(row, rows_of):
+    def terms(dx, dc, earlier):
+        total = rows_of(lambda array: row.quarter(array, dx, dc)).astype(FULL_TYPE)
+        return sum([more.astype(FULL_TYPE) for more in earlier], total).astype(HALF_TYPE)
+
+    return terms
+
+
+def col_scatter(values, col_count):
+    half = values.astype(HALF_TYPE)
+    if col_count != 2:
+        return lax.psum_scatter(half, "col", scatter_dimension=1, tiled=True).astype(FULL_TYPE)
+    width = half.shape[1] // 2
+    first = lax.axis_index("col") == 0
+    left, right = half[:, :width], half[:, width:]
+    other = lax.ppermute(jnp.where(first, right, left), "col", [(0, 1), (1, 0)])
+    return jnp.where(first, left, right).astype(FULL_TYPE) + other.astype(FULL_TYPE)
 
 
 def col_gather(values, col_count):
@@ -376,11 +587,18 @@
     )
 
 
-def col_sum(values, col_count):
+def col_send(values, col_count):
     half = values.astype(HALF_TYPE)
     if col_count != 2:
+        return (half, None)
+    return (half, lax.ppermute(half, "col", [(0, 1), (1, 0)]))
+
+
+def col_sum(pair, *earlier):
+    half, other = pair
+    if other is None:
         return lax.psum(half.astype(FULL_TYPE), "col")
-    other = lax.ppermute(half, "col", [(0, 1), (1, 0)])
+    other = after(other, *earlier)
     return half.astype(FULL_TYPE) + other.astype(FULL_TYPE)
 
 
@@ -417,18 +635,26 @@
     height = weight.shape[0] // devices
     count = fold_count(height, weight.shape[1], rows)
     width = weight.shape[1] // count
-    folded = jnp.swapaxes(weight.reshape(devices, height, count, width), 1, 2)
-    folded = folded.reshape(devices, count * height, width)
-    folded = jnp.pad(folded, ((0, 0), (0, rows - count * height), (0, 0)))
-    return folded.reshape(devices * rows, width)
+    blocks = [
+        weight[:, index * width : (index + 1) * width].reshape(devices, height, width)
+        for index in range(count)
+    ]
+    if count * height < rows:
+        blocks.append(jnp.zeros((devices, rows - count * height, width), weight.dtype))
+    return jnp.concatenate(blocks, axis=1).reshape(devices * rows, width)
 
 
 def unfold(folded, devices, height, width):
     rows = folded.shape[0] // devices
     count = fold_count(height, width, rows)
-    blocks = folded.reshape(devices, rows, folded.shape[1])[:, : count * height]
-    blocks = blocks.reshape(devices, count, height, folded.shape[1])
-    return jnp.swapaxes(blocks, 1, 2).reshape(devices * height, width)
+    blocks = folded.reshape(devices, rows, folded.shape[1])
+    return jnp.concatenate(
+        [
+            blocks[:, index * height : (index + 1) * height].reshape(devices * height, -1)
+            for index in range(count)
+        ],
+        axis=1,
+    )
 
 
 GAIN_LANES = 32
@@ -535,14 +761,19 @@
         half(joint_down),
         fold_gains(half(norm_gains), 1, shard_rows),
     ]
-    offsets = [0]
+    first_width = ffn_width - max(2 * ffn_width // 3 // 256, 1) * 256
+    offsets = [3 * first_width]
     for part in parts:
         offsets.append(offsets[-1] + part.shape[1])
     spare = -offsets[-1] % 128
+    ffn_weights = [half(gate_weight), half(up_weight), half(down_weight)]
     packed_one = jnp.concatenate(
-        parts + [jnp.zeros((shard_rows, spare), HALF_TYPE), half(gate_weight)], axis=1
-    )
-    packed_two = jnp.concatenate([half(up_weight), half(down_weight)], axis=1)
+        [weight[:, :first_width] for weight in ffn_weights]
+        + parts
+        + [jnp.zeros((shard_rows, spare), HALF_TYPE)],
+        axis=1,
+    )
+    packed_two = jnp.concatenate([weight[:, first_width:] for weight in ffn_weights], axis=1)
     gathered_one = lax.all_gather(packed_one, "row", axis=0, tiled=True)
     gathered_two = lax.all_gather(packed_two, "row", axis=0, tiled=True)
     taken = [gathered_one[:, offsets[i] : offsets[i + 1]] for i in range(6)]
@@ -552,9 +783,6 @@
     query_up_all = unfold(taken[3], row_count, query_up.shape[0], query_up.shape[1])
     joint_down_all = taken[4]
     gains_all = unfold_gains(taken[5], row_count, gain_count).astype(FULL_TYPE)
-    gate_all = gathered_one[:, offsets[-1] + spare :]
-    up_all = gathered_two[:, :ffn_width]
-    down_all = gathered_two[:, ffn_width:]
     gain_one = gains_all[:D]
     gain_two = gains_all[D : 2 * D]
     gain_query = gains_all[2 * D : 2 * D + Q_RANK]
@@ -625,51 +853,75 @@
     attended, rotated, log_totals = attention_forward(
         places, key_rope, query_nope, query_rope, joint_full, heads
     )
-    branch = col_sum(times_transposed(attended, out_all), col_count)
+    branch = col_sum(col_send(times_transposed(attended, out_all), col_count))
     residual = inputs + RESIDUAL_SCALE * branch
 
     scale_two = rms_scale(residual)
     normed_two = (residual * scale_two * gain_two).astype(HALF_TYPE)
-    gate_rows = product(normed_two, gate_all)
-    up_rows = product(normed_two, up_all)
-    sigmoid_gate = jax.nn.sigmoid(gate_rows)
-    activated = (gate_rows * sigmoid_gate * up_rows).astype(HALF_TYPE)
     ffn_grad_across = ffn_grad.T
     normed_two_across = normed_two.T
     normed_one_across = normed_one.T
-
-    def from_rows(across, right_side):
-        return lambda dx, dc: product(row.quarter(across, dx, dc), right_side)
-
-    down_grad = row.reduce_scatter(from_rows(ffn_grad_across, activated))
-    grad_act = product(ffn_grad, down_all)
-    grad_gate = (
-        grad_act * up_rows * sigmoid_gate * (1.0 + gate_rows * (1.0 - sigmoid_gate))
-    ).astype(HALF_TYPE)
-    grad_up = (grad_act * gate_rows * sigmoid_gate).astype(HALF_TYPE)
-    gate_grad = row.reduce_scatter(from_rows(normed_two_across, grad_gate))
-    up_grad = row.reduce_scatter(from_rows(normed_two_across, grad_up))
-
-    feed_forward = times_transposed(activated, down_all)
-    feed_forward = lax.psum_scatter(
-        feed_forward.astype(HALF_TYPE), "col", scatter_dimension=1, tiled=True
-    ).astype(FULL_TYPE)
-    residual_part = lax.dynamic_slice_in_dim(residual, col_start, width_share, 1)
-    output_rows = residual_part + RESIDUAL_SCALE * feed_forward
-    output_pad = product(row_matrix, output_rows.astype(HALF_TYPE)).astype(HALF_TYPE)
-
-    grad_normed_two = col_sum(
-        times_transposed(grad_gate, gate_all) + times_transposed(grad_up, up_all), col_count
-    )
+    activated, grad_gate, grad_up = feed_part(normed_two, ffn_grad, gathered_one, first_width)
+    down_sum = Sum(row, Terms(row, ffn_grad_across, activated))
+    both_sum = Sum(
+        row, Terms(row, normed_two_across, jnp.concatenate([grad_gate, grad_up], axis=1))
+    )
+    down_sum.prepare()
+    down_sum.send()
+    both_sum.prepare()
+    held = (down_sum.hold(), both_sum.hold())
+    forward_one = across_part([activated], [2], gathered_one, [], FULL_TYPE)
+    backward_one = across_part([grad_gate, grad_up], [0, 1], gathered_one, [], FULL_TYPE)
+    both_sent = both_sum.send(held)
+    down_one = down_sum.finish(both_sent, forward_one, backward_one)
+    gathered_two = after(gathered_two, forward_one, backward_one, down_one)
+
+    activated, grad_gate, grad_up = feed_part(
+        normed_two, ffn_grad, gathered_two, ffn_width - first_width
+    )
+    down_terms = Terms(row, ffn_grad_across, activated)
+    gate_terms = Terms(row, normed_two_across, grad_gate)
+    up_terms = Terms(row, normed_two_across, grad_up)
+    down_sum = Sum(row, down_terms)
+    gate_sum = Sum(row, gate_terms)
+    up_sum = Sum(row, up_terms)
+    down_sum.prepare()
+    gate_total = gate_sum.prepare()
+    down_sent = down_sum.send(gate_total)
+
+    one_grads = row.over_z(jnp.concatenate([both_sum.finish(down_sent), down_one], axis=1))
+    grad_gate, grad_up = after((grad_gate, grad_up), down_sent)
+    backward_two = across_part(
+        [grad_gate, grad_up], [0, 1], gathered_two, [backward_one], HALF_TYPE
+    )
+    up_terms.wait(backward_two)
+    up_total = up_sum.prepare()
+    grad_normed_two = col_send(backward_two, col_count)
+    activated = after(activated, up_total)
+    forward_two = across_part([activated], [2], gathered_two, [forward_one], HALF_TYPE)
+    down_terms.wait(forward_two)
+    gate_terms.wait(forward_two)
+    held = (down_sum.hold(), gate_sum.hold())
+    gate_sent = gate_sum.send(up_total, held)
+
+    down_two = row.over_z(down_sum.finish(gate_sent))
+    grad_normed_two = col_sum(grad_normed_two, gate_sent)
     through_two, gain_two_grad = rms_backward(grad_normed_two, residual, scale_two, gain_two)
     grad_residual = upstream + through_two
     branch_grad = (RESIDUAL_SCALE * grad_residual).astype(HALF_TYPE)
-    out_grad = row.reduce_scatter(from_rows(branch_grad.T, attended))
+    out_sum = Sum(row, Terms(row, branch_grad.T, attended))
+    out_total = out_sum.prepare()
+    branch_grad = after(branch_grad, out_total)
     grad_attended = product(branch_grad, out_all).astype(HALF_TYPE)
 
     grad_nope, grad_rope, grad_joint_full, grad_key = attention_backward(
         places, key_rope, query_nope, rotated, joint_full, grad_attended, log_totals, heads
     )
+    up_sent = up_sum.send(grad_joint_full)
+    grad_nope, grad_rope, grad_joint_full = after(
+        (grad_nope, grad_rope, grad_joint_full), up_sent
+    )
+    gate_two = row.over_z(gate_sum.finish(up_sent))
     query_up_grad = jnp.concatenate(
         [contract_rows(query_normed, grad_nope), contract_rows(query_normed, grad_rope)], axis=1
     )
@@ -681,10 +933,11 @@
         ],
         axis=1,
     )
-    heads_grad = row.reduce_scatter(
-        lambda dx, dc: row.quarter(folded_grads, dx, dc).astype(FULL_TYPE)
-    )
-    latents = col_sum(
+    up_terms.wait(grad_joint_full)
+    held = up_sum.hold()
+    heads_sum = Sum(row, taken_terms(row, lambda take: take(folded_grads)))
+    heads_total = heads_sum.prepare()
+    latents = col_send(
         jnp.concatenate(
             [
                 times_transposed(grad_nope, query_nope_all)
@@ -696,6 +949,7 @@
         ),
         col_count,
     )
+    latents = col_sum(latents)
     grad_query_normed = latents[:, :Q_RANK]
     grad_compressed = latents[:, Q_RANK : Q_RANK + KV_RANK]
     grad_rope_sum = latents[:, Q_RANK + KV_RANK :]
@@ -716,22 +970,49 @@
     grad_inputs = lax.dynamic_slice_in_dim(
         grad_residual + through_one, col_start, width_share, 1
     ).astype(HALF_TYPE)
-    returned = lax.all_to_all(grad_inputs, "row", split_axis=0, concat_axis=0, tiled=True)
-    grad_tokens = contract_rows(send_matrix, returned).astype(HALF_TYPE)
     gains_grad = fold_gains(
         jnp.concatenate([gain_one_grad, gain_two_grad, gain_query_grad, gain_joint_grad]),
         row_count,
         shard_rows,
     )
-    downs_grad = row.reduce_scatter(
-        lambda dx, dc: jnp.concatenate(
-            [
-                product(row.quarter(normed_one_across, dx, dc), grad_latents),
-                row.quarter(gains_grad, dx, dc),
-            ],
-            axis=1,
+    downs_sum = Sum(
+        row,
+        taken_terms(
+            row,
+            lambda take: jnp.concatenate(
+                [product(take(normed_one_across), grad_latents), take(gains_grad)], axis=1
+            ),
+        ),
+    )
+    downs_total = downs_sum.prepare()
+    out_sent = out_sum.send(heads_total, held, downs_total, last=False)
+    heads_sent = heads_sum.send(last=False)
+    downs_sent = downs_sum.send(last=False)
+
+    up_two = row.over_z(up_sum.finish(out_sent))
+    returned = lax.all_to_all(
+        after(grad_inputs, out_sent), "row", split_axis=0, concat_axis=0, tiled=True
+    )
+    grad_tokens = contract_rows(send_matrix, returned).astype(HALF_TYPE)
+    feed_forward = col_scatter(after(forward_two, out_sent), col_count)
+    residual_part = lax.dynamic_slice_in_dim(residual, col_start, width_share, 1)
+    output_rows = residual_part + RESIDUAL_SCALE * feed_forward
+    output_pad = product(row_matrix, output_rows.astype(HALF_TYPE)).astype(HALF_TYPE)
+    out_sum.hold()
+    heads_sum.hold()
+    downs_sum.hold()
+    out_total = out_sum.finish(heads_sent, downs_sent)
+    heads_total = heads_sum.finish(downs_sent)
+    downs_total = downs_sum.finish()
+    out_grad = row.over_z_direct(out_total, downs_total)
+    heads_grad = row.over_z_direct(heads_total, downs_total)
+    downs_grad = row.over_z_direct(downs_total)
+    gate_grad, up_grad, down_grad = [
+        jnp.concatenate(
+            [one_grads[:, index * first_width : (index + 1) * first_width], two], axis=1
         )
-    )
+        for index, two in enumerate((gate_two, up_two, down_two))
+    ]
     query_fold = taken[3].shape[1]
     reduced = (
         downs_grad[:, :Q_RANK],

time: 1270 us -> 922 us (0.73)
  waiting for transfers between devices: 746 us -> 353 us
  Pallas kernels: 34.4 us -> 237 us
  matrix products: 217 us -> 60.5 us
  other arithmetic: 123 us -> 95.2 us
  starting transfers between devices: 48.3 us -> 62.2 us
    ppermute x36 -> x33, waiting for transfers between devices: 430 us -> 142 us  [move(): return lax.ppermute(values, 'row', pairs)]
    pallas_call x0 -> x30, Pallas kernels: none -> 202 us  [the longest x24 121 us: piece_product(): pl.pallas_call(piece_kernel, grid_spec=pltpu.PrefetchScalarGridSpec(num_s...]
    dot_general x31 -> x12, matrix products: 148 us -> 27.9 us  [product(): return jnp.dot(left_side, right_side, preferred_element_type=FULL_TYPE)]
    all_gather x1, waiting for transfers between devices: 118 us -> 0.01 us  [body(): gathered_two = lax.all_gather(packed_two, 'row', axis=0, tiled=True)]
    dot_general x9 -> x6, matrix products: 58.5 us -> 24.8 us  [times_transposed(): lax.dot_general(left_side, right_side, (((1,), (1,)), ((), ())), preferre...]
    convert_element_type x20 -> x9, other arithmetic: 43.8 us -> 21.7 us  [the longest x4 11 us: terms(): sum([more.astype(FULL_TYPE) for more in earlier], total).astype(HALF_TYPE)]
    unnamed x269 -> x330, local copies, waits for them, and re-layouts: 4.85 us -> 26.7 us
    ppermute x36 -> x33, starting transfers between devices: 24 us -> 36.8 us  [move(): return lax.ppermute(values, 'row', pairs)]
  transfers between devices with their start and end apart: 47 -> 48, of which waited for: 26 -> 17; matrix products, arithmetic and copies ran while one was open for 26% -> 20% of each run, Pallas kernels for 3% -> 25%
where the time goes in v2:
time: 922 us; the launch traced here: 908 us
  waiting for transfers between devices  353 us (38%)
  Pallas kernels  237 us (26%)
  other arithmetic  95.2 us (10%)
  local copies, waits for them, and re-layouts  82.2 us (9%)
  starting transfers between devices  62.2 us (7%)
  matrix products  60.5 us (7%)
  between operations  17.5 us (2%)
    ppermute x33, waiting for transfers between devices, move(): return lax.ppermute(values, 'row', pairs)  142 us
    pallas_call x24, Pallas kernels, piece_product(): pl.pallas_call(piece_kernel, grid_spec=pltpu.PrefetchScalarGridSpec(num_s...  121 us
    all_gather x1, waiting for transfers between devices, body(): gathered_one = lax.all_gather(packed_one, 'row', axis=0, tiled=True)  110 us
    pallas_call x4, Pallas kernels, across_part(): pl.pallas_call(functools.partial(across_kernel, len(sides)), grid=(depth...  45.8 us
    ppermute x3, waiting for transfers between devices, col_send(): return (half, lax.ppermute(half, 'col', [(0, 1), (1, 0)]))  40.2 us
    ppermute x33, starting transfers between devices, move(): return lax.ppermute(values, 'row', pairs)  36.8 us
    all_to_all x1, waiting for transfers between devices, body(): lax.all_to_all(sorted_tokens, 'row', split_axis=0, concat_axis=0, tiled=T...  35.5 us
    pallas_call x2, Pallas kernels, feed_part(): pl.pallas_call(feed_kernel, grid=(count,), in_specs=[whole, whole, part(0...  34.9 us
  transfers between devices with their start and end apart: 48, of which 17 were waited for; matrix products, arithmetic and copies ran while one was open for 20% of the time, Pallas kernels for 25%

profile of v2, /device:TPU:0, one launch (start us, length us, event | category | flops | bytes accessed | tf_op | source)
XLA Modules:
  0.0 908.0 jit_solution(1461602616313225697)
XLA Ops:
  31.1 7.4 all-to-all-start.1
  40.9 35.5 %all-to-all-done.1 = bf16[16,24,1280]{2,1,0:T(8,128)(2,1)} async-done(((bf16[16,24,1280]{2,1,0:T(8,128)(2,1)}), bf16[16,24,1280]{2,1,0:T(8,128)(2,1)}, u32[]{:S(2)}, u32[]{:S(2)}) %all-to-all-start.1) | async-done | bytes 983072 | tf_op jit(solution)/shard_map/all_to_all | solution.py:806
  91.4 13.1 %collective-permute-done = bf16[384,1280]{1,0:T(8,128)(2,1)} collective-permute-done((bf16[384,1280]{1,0:T(8,128)(2,1)}, bf16[384,1280]{1,0:T(8,128)(2,1)}, u32[]{:S(2)}, u32[]{:S(2)}) %collective-permute-start) | collective-permute-done | bytes 983072 | tf_op jit(solution)/shard_map/ppermute | solution.py:583
  107.3 110.4 %all-gather.3.cloned.1.call-done.gate.up.down.refs_1_.refs_2_.refs_3_ = bf16[2560,6784]{1,0:T(8,128)(2,1)} async-done(((bf16[160,6784]{1,0:T(8,128)(2,1)}), bf16[2560,6784]{1,0:T(8,128)(2,1)}) %all-gather.3.cloned.1.call-update) | async-done | bytes 34734096 | tf_op jit(solution)/shard_map/all_gather | solution.py:777
  241.4 14.2 %shard_map.518 = (bf16[384,1280]{1,0:T(8,128)(2,1)S(1)}, bf16[384,640]{1,0:T(8,128)(2,1)S(1)}, f32[5,4,384]{2,1,0:T(4,128)S(1)}) custom-call(s32[384,1]{1,0:T(8,128)S(1)} %broadcast_in_dim.43.row_here, s32[1,384]{1,0:T(1,128)S(1)} %broadcast_in_dim.37.row_across, s32[1,384]{1,0:T(1,128)S(1)} %broadcast_in_dim.39.first_across, f32[384,128]{1,0:T(8,128)S(1)} %copy.216.cosine, ...), custom_call_target="tpu_custom_call" | custom-call | flops 1 | bytes 1 | tf_op jit(solution)/shard_map/pallas_call | solution.py:258
  255.6 8.9 fusion.4
  273.6 36.0 %collective-permute-done.1 = bf16[384,2560]{1,0:T(8,128)(2,1)} collective-permute-done((bf16[384,2560]{1,0:T(8,128)(2,1)}, bf16[384,2560]{1,0:T(8,128)(2,1)}, u32[]{:S(2)}, u32[]{:S(2)}) %collective-permute-start.1) | collective-permute-done | bytes 1966112 | tf_op jit(solution)/shard_map/ppermute | solution.py:594
  315.4 14.8 %shard_map.519 = (bf16[384,1152]{1,0:T(8,128)(2,1)}, bf16[384,1152]{1,0:T(8,128)(2,1)}, bf16[384,1152]{1,0:T(8,128)(2,1)}) custom-call(bf16[384,2560]{1,0:T(8,128)(2,1)} %multiply_convert_fusion.1.normed, bf16[384,2560]{1,0:T(8,128)(2,1)} %get-tuple-element.208.ffn_grad, bf16[2560,6784]{1,0:T(8,128)(2,1)} %all-gather.3.cloned.1.call-done.gate.up.down.refs_1_.refs_2_.refs_3_, ...), custom_call_target="tpu_custom_call" | custom-call | flops 1 | bytes 1 | tf_op jit(solution)/shard_map/pallas_call | solution.py:339
  367.1 5.6 shard_map.526
  372.7 39.3 %collective-permute-done.5.refs_1_ = bf16[640,1152]{1,0:T(8,128)(2,1)} collective-permute-done((bf16[640,1152]{1,0:T(8,128)(2,1)}, bf16[640,1152]{1,0:T(8,128)(2,1)}, u32[]{:S(2)}, u32[]{:S(2)}) %collective-permute-start.5) | collective-permute-done | bytes 1474592 | tf_op jit(solution)/shard_map/ppermute | solution.py:444
  412.9 10.6 %shard_map.521.refs_4_ = f32[384,2560]{1,0:T(8,128)} custom-call(bf16[384,1152]{1,0:T(8,128)(2,1)} %get-tuple-element.79.refs_0_, bf16[384,1152]{1,0:T(8,128)(2,1)} %get-tuple-element.80.refs_1_, bf16[2560,6784]{1,0:T(8,128)(2,1)} %all-gather.3.cloned.1.call-done.gate.up.down.refs_1_.refs_2_.refs_3_, ...), custom_call_target="tpu_custom_call" | custom-call | flops 1 | bytes 1 | tf_op jit(solution)/shard_map/pallas_call | solution.py:371
  423.5 7.7 shard_map.520.refs_2_
  437.4 20.0 %shard_map.529 = (bf16[384,2048]{1,0:T(8,128)(2,1)}, bf16[384,2048]{1,0:T(8,128)(2,1)}, bf16[384,2048]{1,0:T(8,128)(2,1)}) custom-call(bf16[384,2560]{1,0:T(8,128)(2,1)} %multiply_convert_fusion.1.normed, bf16[384,2560]{1,0:T(8,128)(2,1)} %get-tuple-element.208.ffn_grad, bf16[2560,6144]{1,0:T(8,128)(2,1)} %all-gather.5.cloned.1.call-done.gate.up.down.refs_2_.refs_3_.refs_1_, ...), custom_call_target="tpu_custom_call" | custom-call | flops 1 | bytes 1 | tf_op jit(solution)/shard_map/pallas_call | solution.py:339
  481.1 6.5 shard_map.546
  491.9 16.8 %shard_map.534 = bf16[384,2560]{1,0:T(8,128)(2,1)} custom-call(bf16[384,2048]{1,0:T(8,128)(2,1)} %get-tuple-element.93.right_side.refs_0_, bf16[384,2048]{1,0:T(8,128)(2,1)} %get-tuple-element.106.refs_1_.right_side, bf16[2560,6144]{1,0:T(8,128)(2,1)} %all-gather.5.cloned.1.call-done.gate.up.down.refs_2_.refs_3_.refs_1_, ...), custom_call_target="tpu_custom_call" | custom-call | flops 1 | bytes 1 | tf_op jit(solution)/shard_map/pallas_call | solution.py:371
  525.4 10.6 %shard_map.537 = bf16[384,2560]{1,0:T(8,128)(2,1)} custom-call(bf16[384,2048]{1,0:T(8,128)(2,1)} %get-tuple-element.92.right_side.refs_0_, bf16[2560,6144]{1,0:T(8,128)(2,1)} %all-gather.5.cloned.1.call-done.gate.up.down.refs_2_.refs_3_.refs_1_, f32[384,2560]{1,0:T(8,128)} %shard_map.520.refs_2_), custom_call_target="tpu_custom_call" | custom-call | flops 1 | bytes 1 | tf_op jit(solution)/shard_map/pallas_call | solution.py:371
  540.9 5.4 shard_map.538
  546.7 26.6 %collective-permute-done.12.refs_1_ = bf16[640,2048]{1,0:T(8,128)(2,1)} collective-permute-done((bf16[640,2048]{1,0:T(8,128)(2,1)}, bf16[640,2048]{1,0:T(8,128)(2,1)}, u32[]{:S(2)}, u32[]{:S(2)}) %collective-permute-start.12) | collective-permute-done | bytes 2621472 | tf_op jit(solution)/shard_map/ppermute | solution.py:444
  601.1 5.8 shard_map.549
  607.6 6.4 fusion.19.grad_out
  614.1 20.7 %shard_map.542 = (bf16[384,1280]{1,0:T(8,128)(2,1)S(1)}, bf16[384,640]{1,0:T(8,128)(2,1)S(1)}, bf16[384,2560]{1,0:T(8,128)(2,1)S(1)}, f32[384,32]{1,0:T(8,128)S(1)}) custom-call(s32[384,1]{1,0:T(8,128)S(1)} %copy-done.10, s32[1,384]{1,0:T(1,128)S(1)} %copy-done.22, s32[1,384]{1,0:T(1,128)S(1)} %copy-done.24, f32[384,128]{1,0:T(8,128)S(1)} %copy-done.12, ...), custom_call_target="tpu_custom_call" | custom-call | flops 1 | bytes 1 | tf_op jit(solution)/shard_map/pallas_call | solution.py:278
  653.9 6.1 shard_map.547
  671.0 6.9 fusion.12
  725.9 5.8 shard_map.548
  731.8 7.1 collective-permute-done.19
  748.7 5.4 collective-permute-done.26
  758.6 28.1 %collective-permute-done.21 = bf16[640,1088]{0,1:T(8,128)(2,1)} collective-permute-done((bf16[640,1088]{0,1:T(8,128)(2,1)}, bf16[640,1088]{0,1:T(8,128)(2,1)}, u32[]{:S(2)}, u32[]{:S(2)}) %collective-permute-start.21) | collective-permute-done | bytes 1392672 | tf_op jit(solution)/shard_map/ppermute | solution.py:444
  797.6 21.4 %collective-permute-done.28 = bf16[160,896]{1,0:T(8,128)(2,1)} collective-permute-done((bf16[160,896]{1,0:T(8,128)(2,1)}, bf16[160,896]{1,0:T(8,128)(2,1)}, u32[]{:S(2)}, u32[]{:S(2)}) %collective-permute-start.28) | collective-permute-done | bytes 286752 | tf_op jit(solution)/shard_map/ppermute | solution.py:444
  837.1 14.9 %collective-permute-start.32 = (bf16[160,1280]{1,0:T(8,128)(2,1)}, bf16[160,1280]{1,0:T(8,128)(2,1)}, u32[]{:S(2)}, u32[]{:S(2)}) collective-permute-start(bf16[160,1280]{1,0:T(8,128)(2,1)} %get-tuple-element.213), channel_id=1, source_target_pairs={{0,8},{2,10},{4,12},{6,14},{8,16},{10,18},{12,20},{14,22},{16,24},... | collective-permute-start | bytes 1228808 | tf_op jit(solution)/shard_map/ppermute | solution.py:444
  865.0 14.1 %collective-permute-done.33 = bf16[160,1280]{1,0:T(8,128)(2,1)} collective-permute-done((bf16[160,1280]{1,0:T(8,128)(2,1)}, bf16[160,1280]{1,0:T(8,128)(2,1)}, u32[]{:S(2)}, u32[]{:S(2)}) %collective-permute-start.33) | collective-permute-done | bytes 409632 | tf_op jit(solution)/shard_map/ppermute | solution.py:444
  885.1 5.4 multiply_subtract_fusion
  894.9 6.0 multiply_subtract_fusion.1
  (639 shorter events, 346.9 us)
Async XLA Ops:
  7.2 210.5 %all-gather.3.cloned.1.call-start = ((), (), s32[]{:S(2)}) async-start(), calls=%async_computation.7 | async-start | bytes 36904960 | tf_op jit(solution)/shard_map/all_gather | solution.py:777
  25.4 412.1 %all-gather.5.cloned.1.call-start = ((), (), s32[]{:S(2)}) async-start(), calls=%async_computation.8 | async-start | bytes 33423360 | tf_op jit(solution)/shard_map/all_gather | solution.py:778
  31.1 45.2 %all-to-all-start.1 = ((bf16[16,24,1280]{2,1,0:T(8,128)(2,1)}), bf16[16,24,1280]{2,1,0:T(8,128)(2,1)}, u32[]{:S(2)}, u32[]{:S(2)}) async-start(bf16[16,24,1280]{2,1,0:T(8,128)(2,1)} %bitcast), calls=%async_computation.1 | async-start | bytes 1966080 | tf_op jit(solution)/shard_map/all_to_all | solution.py:806
  79.8 666.1 %reduce-scatter.5.cloned.1.call-start = ((), (), s32[]{:S(2)}) async-start(), calls=%async_computation.9 | async-start | bytes 5529600 | tf_op jit(solution)/shard_map/reduce_scatter | solution.py:476
  264.6 45.0 %collective-permute-start.1 = (bf16[384,2560]{1,0:T(8,128)(2,1)}, bf16[384,2560]{1,0:T(8,128)(2,1)}, u32[]{:S(2)}, u32[]{:S(2)}) collective-permute-start(bf16[384,2560]{1,0:T(8,128)(2,1)} %fusion.4), channel_id=1, source_target_pairs={{0,1},{1,0},{2,3},{3,2},{4,5},{5,4},{6,7},{7,6},{8,9},{9,8},{10,11... | collective-permute-start | bytes 5898248 | tf_op jit(solution)/shard_map/ppermute | solution.py:594
  354.2 57.9 %collective-permute-start.5 = (bf16[640,1152]{1,0:T(8,128)(2,1)}, bf16[640,1152]{1,0:T(8,128)(2,1)}, u32[]{:S(2)}, u32[]{:S(2)}) collective-permute-start(bf16[640,1152]{1,0:T(8,128)(2,1)} %shard_map.524), channel_id=1, source_target_pairs={{0,4},{2,6},{4,0},{6,2},{8,12},{10,14},{12,8},{14,10},{16,20},{18,... | collective-permute-start | bytes 4423688 | tf_op jit(solution)/shard_map/ppermute | solution.py:444
  360.2 71.0 %collective-permute-start.3 = (bf16[640,1152]{1,0:T(8,128)(2,1)}, bf16[640,1152]{1,0:T(8,128)(2,1)S(1)}, u32[]{:S(2)}, u32[]{:S(2)}) collective-permute-start(bf16[640,1152]{1,0:T(8,128)(2,1)} %shard_map.522), channel_id=1, source_target_pairs={{0,2},{2,0},{4,6},{6,4},{8,10},{10,8},{12,14},{14,12},{16,18},{18,... | collective-permute-start | bytes 4423688 | tf_op jit(solution)/shard_map/ppermute | solution.py:444
  412.1 67.5 %collective-permute-start.8 = (bf16[640,2304]{1,0:T(8,128)(2,1)}, bf16[640,2304]{1,0:T(8,128)(2,1)S(1)}, u32[]{:S(2)}, u32[]{:S(2)}) collective-permute-start(bf16[640,2304]{1,0:T(8,128)(2,1)} %shard_map.526), channel_id=1, source_target_pairs={{0,4},{2,6},{4,0},{6,2},{8,12},{10,14},{12,8},{14,10},{16,20},{18,... | collective-permute-start | bytes 8847368 | tf_op jit(solution)/shard_map/ppermute | solution.py:444
  412.4 67.2 %collective-permute-start.35 = (bf16[640,2304]{1,0:T(8,128)(2,1)}, bf16[640,2304]{1,0:T(8,128)(2,1)}, u32[]{:S(2)}, u32[]{:S(2)}) collective-permute-start(bf16[640,2304]{1,0:T(8,128)(2,1)} %shard_map.527), channel_id=1, source_target_pairs={{0,2},{2,0},{4,6},{6,4},{8,10},{10,8},{12,14},{14,12},{16,18},{18,... | collective-permute-start | bytes 8847368 | tf_op jit(solution)/shard_map/ppermute | solution.py:444
  491.9 390.4 %reduce-scatter.11.cloned.1.call-start = ((), (), s32[]{:S(2)}) async-start(), calls=%async_computation.12 | async-start | bytes 3276800 | tf_op jit(solution)/shard_map/reduce_scatter | solution.py:476
  514.0 59.3 %collective-permute-start.12 = (bf16[640,2048]{1,0:T(8,128)(2,1)}, bf16[640,2048]{1,0:T(8,128)(2,1)}, u32[]{:S(2)}, u32[]{:S(2)}) collective-permute-start(bf16[640,2048]{1,0:T(8,128)(2,1)} %shard_map.531), channel_id=1, source_target_pairs={{0,4},{2,6},{4,0},{6,2},{8,12},{10,14},{12,8},{14,10},{16,20},{18,... | collective-permute-start | bytes 7864328 | tf_op jit(solution)/shard_map/ppermute | solution.py:444
  515.7 59.3 %collective-permute-start.11 = (bf16[384,2560]{1,0:T(8,128)(2,1)S(1)}, bf16[384,2560]{1,0:T(8,128)(2,1)}, u32[]{:S(2)}, u32[]{:S(2)}) collective-permute-start(bf16[384,2560]{1,0:T(8,128)(2,1)S(1)} %copy-done.32), channel_id=1, source_target_pairs={{0,1},{1,0},{2,3},{3,2},{4,5},{5,4},{6,7},{7,6},{8,9},{9,8},{10,11... | collective-permute-start | bytes 5898248 | tf_op jit(solution)/shard_map/ppermute | solution.py:594
  546.3 54.9 %collective-permute-start.38 = (bf16[640,2048]{1,0:T(8,128)(2,1)}, bf16[640,2048]{1,0:T(8,128)(2,1)}, u32[]{:S(2)}, u32[]{:S(2)}) collective-permute-start(bf16[640,2048]{1,0:T(8,128)(2,1)} %shard_map.538), channel_id=1, source_target_pairs={{0,2},{2,0},{4,6},{6,4},{8,10},{10,8},{12,14},{14,12},{16,18},{18,... | collective-permute-start | bytes 7864328 | tf_op jit(solution)/shard_map/ppermute | solution.py:444
  573.2 63.9 %collective-permute-start.14 = (bf16[640,2048]{1,0:T(8,128)(2,1)}, bf16[640,2048]{1,0:T(8,128)(2,1)}, u32[]{:S(2)}, u32[]{:S(2)}) collective-permute-start(bf16[640,2048]{1,0:T(8,128)(2,1)} %shard_map.533), channel_id=1, source_target_pairs={{0,4},{2,6},{4,0},{6,2},{8,12},{10,14},{12,8},{14,10},{16,20},{18,... | collective-permute-start | bytes 7864328 | tf_op jit(solution)/shard_map/ppermute | solution.py:444
  592.3 61.6 %collective-permute-start.36 = (bf16[640,2048]{1,0:T(8,128)(2,1)}, bf16[640,2048]{1,0:T(8,128)(2,1)}, u32[]{:S(2)}, u32[]{:S(2)}) collective-permute-start(bf16[640,2048]{1,0:T(8,128)(2,1)} %shard_map.539), channel_id=1, source_target_pairs={{0,2},{2,0},{4,6},{6,4},{8,10},{10,8},{12,14},{14,12},{16,18},{18,... | collective-permute-start | bytes 7864328 | tf_op jit(solution)/shard_map/ppermute | solution.py:444
  607.1 276.6 %reduce-scatter.7.cloned.1.call-start = ((), (), s32[]{:S(2)}) async-start(), calls=%async_computation.10 | async-start | bytes 3276800 | tf_op jit(solution)/shard_map/reduce_scatter | solution.py:476
  637.2 76.4 %collective-permute-start.15 = (bf16[640,2048]{1,0:T(8,128)(2,1)}, bf16[640,2048]{1,0:T(8,128)(2,1)}, u32[]{:S(2)}, u32[]{:S(2)}) collective-permute-start(bf16[640,2048]{1,0:T(8,128)(2,1)} %shard_map.536), channel_id=1, source_target_pairs={{0,4},{2,6},{4,0},{6,2},{8,12},{10,14},{12,8},{14,10},{16,20},{18,... | collective-permute-start | bytes 7864328 | tf_op jit(solution)/shard_map/ppermute | solution.py:444
  653.9 53.6 %collective-permute-start.16 = (bf16[640,896]{1,0:T(8,128)(2,1)}, bf16[640,896]{1,0:T(8,128)(2,1)}, u32[]{:S(2)}, u32[]{:S(2)}) collective-permute-start(bf16[640,896]{1,0:T(8,128)(2,1)} %bitcast.66), channel_id=1, source_target_pairs={{0,2},{2,0},{4,6},{6,4},{8,10},{10,8},{12,14},{14,12},{16,18},{18,... | collective-permute-start | bytes 3440648 | tf_op jit(solution)/shard_map/ppermute | solution.py:444
  696.1 133.3 %collective-permute-start.30 = (bf16[640,1280]{1,0:T(8,128)(2,1)}, bf16[640,1280]{1,0:T(8,128)(2,1)}, u32[]{:S(2)}, u32[]{:S(2)}) collective-permute-start(bf16[640,1280]{1,0:T(8,128)(2,1)} %shard_map.544), channel_id=1, source_target_pairs={{0,2},{2,0},{4,6},{6,4},{8,10},{10,8},{12,14},{14,12},{16,18},{18,... | collective-permute-start | bytes 4915208 | tf_op jit(solution)/shard_map/ppermute | solution.py:444
  707.4 47.2 %collective-permute-start.25 = (bf16[640,896]{1,0:T(8,128)(2,1)}, bf16[640,896]{1,0:T(8,128)(2,1)}, u32[]{:S(2)}, u32[]{:S(2)}) collective-permute-start(bf16[640,896]{1,0:T(8,128)(2,1)} %bitcast.82), channel_id=1, source_target_pairs={{0,2},{2,0},{4,6},{6,4},{8,10},{10,8},{12,14},{14,12},{16,18},{18,... | collective-permute-start | bytes 3440648 | tf_op jit(solution)/shard_map/ppermute | solution.py:444
  717.9 36.2 %collective-permute-start.26 = (bf16[640,896]{1,0:T(8,128)(2,1)}, bf16[640,896]{1,0:T(8,128)(2,1)}, u32[]{:S(2)}, u32[]{:S(2)}) collective-permute-start(bf16[640,896]{1,0:T(8,128)(2,1)} %fusion.27), channel_id=1, source_target_pairs={{0,4},{2,6},{4,0},{6,2},{8,12},{10,14},{12,8},{14,10},{16,20},{18,... | collective-permute-start | bytes 3440648 | tf_op jit(solution)/shard_map/ppermute | solution.py:444
  720.6 141.6 %all-to-all-start.2 = ((bf16[16,24,1280]{2,1,0:T(8,128)(2,1)}), bf16[16,24,1280]{2,1,0:T(8,128)(2,1)}, u32[]{:S(2)}, u32[]{:S(2)}) async-start(bf16[16,24,1280]{2,1,0:T(8,128)(2,1)} %bitcast.296), calls=%async_computation.2 | async-start | bytes 1966080 | tf_op jit(solution)/shard_map/all_to_all | solution.py:993
  725.4 168.2 %reduce-scatter.9.cloned.1.call-start = ((), (), s32[]{:S(2)}) async-start(), calls=%async_computation.11 | async-start | bytes 3276800 | tf_op jit(solution)/shard_map/reduce_scatter | solution.py:476
  725.5 61.2 %collective-permute-start.20 = (bf16[640,1088]{0,1:T(8,128)(2,1)}, bf16[640,1088]{0,1:T(8,128)(2,1)}, u32[]{:S(2)}, u32[]{:S(2)}) collective-permute-start(bf16[640,1088]{0,1:T(8,128)(2,1)} %pad_maximum_fusion.10), channel_id=1, source_target_pairs={{0,2},{2,0},{4,6},{6,4},{8,10},{10,8},{12,14},{14,12},{16,18},{18,... | collective-permute-start | bytes 4177928 | tf_op jit(solution)/shard_map/ppermute | solution.py:444
  738.9 47.8 %collective-permute-start.21 = (bf16[640,1088]{0,1:T(8,128)(2,1)}, bf16[640,1088]{0,1:T(8,128)(2,1)}, u32[]{:S(2)}, u32[]{:S(2)}) collective-permute-start(bf16[640,1088]{0,1:T(8,128)(2,1)} %fusion.22), channel_id=1, source_target_pairs={{0,4},{2,6},{4,0},{6,2},{8,12},{10,14},{12,8},{14,10},{16,20},{18,... | collective-permute-start | bytes 4177928 | tf_op jit(solution)/shard_map/ppermute | solution.py:444
  754.1 75.3 %collective-permute-start.31 = (bf16[640,1280]{1,0:T(8,128)(2,1)}, bf16[640,1280]{1,0:T(8,128)(2,1)}, u32[]{:S(2)}, u32[]{:S(2)}) collective-permute-start(bf16[640,1280]{1,0:T(8,128)(2,1)} %shard_map.541), channel_id=1, source_target_pairs={{0,4},{2,6},{4,0},{6,2},{8,12},{10,14},{12,8},{14,10},{16,20},{18,... | collective-permute-start | bytes 4915208 | tf_op jit(solution)/shard_map/ppermute | solution.py:444
  758.6 38.4 %collective-permute-start.27 = (bf16[160,896]{1,0:T(8,128)(2,1)}, bf16[160,896]{1,0:T(8,128)(2,1)S(1)}, u32[]{:S(2)}, u32[]{:S(2)}) collective-permute-start(bf16[160,896]{1,0:T(8,128)(2,1)} %get-tuple-element.239), channel_id=1, source_target_pairs={{0,8},{2,10},{4,12},{6,14},{8,16},{10,18},{12,20},{14,22},{16,24},... | collective-permute-start | bytes 860168 | tf_op jit(solution)/shard_map/ppermute | solution.py:444
  786.7 32.2 %collective-permute-start.28 = (bf16[160,896]{1,0:T(8,128)(2,1)}, bf16[160,896]{1,0:T(8,128)(2,1)}, u32[]{:S(2)}, u32[]{:S(2)}) collective-permute-start(bf16[160,896]{1,0:T(8,128)(2,1)} %get-tuple-element.241), channel_id=1, source_target_pairs={{0,16},{2,18},{4,20},{6,22},{8,24},{10,26},{12,28},{14,30},{16,0},... | collective-permute-start | bytes 860168 | tf_op jit(solution)/shard_map/ppermute | solution.py:444
  786.7 32.2 %collective-permute-start.29 = (bf16[160,896]{1,0:T(8,128)(2,1)S(1)}, bf16[160,896]{1,0:T(8,128)(2,1)}, u32[]{:S(2)}, u32[]{:S(2)}) collective-permute-start(bf16[160,896]{1,0:T(8,128)(2,1)S(1)} %get-tuple-element.240), channel_id=1, source_target_pairs={{0,24},{2,26},{4,28},{6,30},{8,0},{10,2},{12,4},{14,6},{16,8},{18,... | collective-permute-start | bytes 860168 | tf_op jit(solution)/shard_map/ppermute | solution.py:444
  797.0 56.4 %collective-permute-start.22 = (bf16[160,1088]{1,0:T(8,128)(2,1)}, bf16[160,1088]{1,0:T(8,128)(2,1)}, u32[]{:S(2)}, u32[]{:S(2)}) collective-permute-start(bf16[160,1088]{1,0:T(8,128)(2,1)} %get-tuple-element.216), channel_id=1, source_target_pairs={{0,8},{2,10},{4,12},{6,14},{8,16},{10,18},{12,20},{14,22},{16,24},... | collective-permute-start | bytes 1044488 | tf_op jit(solution)/shard_map/ppermute | solution.py:444
  819.0 37.4 %collective-permute-start.23 = (bf16[160,1088]{1,0:T(8,128)(2,1)}, bf16[160,1088]{1,0:T(8,128)(2,1)}, u32[]{:S(2)}, u32[]{:S(2)}) collective-permute-start(bf16[160,1088]{1,0:T(8,128)(2,1)} %get-tuple-element.218), channel_id=1, source_target_pairs={{0,16},{2,18},{4,20},{6,22},{8,24},{10,26},{12,28},{14,30},{16,0},... | collective-permute-start | bytes 1044488 | tf_op jit(solution)/shard_map/ppermute | solution.py:444
  819.0 37.4 %collective-permute-start.24 = (bf16[160,1088]{1,0:T(8,128)(2,1)}, bf16[160,1088]{1,0:T(8,128)(2,1)}, u32[]{:S(2)}, u32[]{:S(2)}) collective-permute-start(bf16[160,1088]{1,0:T(8,128)(2,1)} %get-tuple-element.217), channel_id=1, source_target_pairs={{0,24},{2,26},{4,28},{6,30},{8,0},{10,2},{12,4},{14,6},{16,8},{18,... | collective-permute-start | bytes 1044488 | tf_op jit(solution)/shard_map/ppermute | solution.py:444
  (168 other events, 2527.8 us)
Sparse Core Ops, SparseCore 0:
  25.5 192.2 all-gather.2
  219.9 185.4 all-gather.4
  492.0 81.6 reduce-scatter.4
  607.1 52.1 reduce-scatter.10
  661.5 51.7 reduce-scatter.6
  731.9 68.3 reduce-scatter.8

commit v3 on v2

--- a/solution.py
+++ b/solution.py
@@ -267,7 +267,7 @@
         ],
         scratch_shapes=[pltpu.VMEM((tokens, tokens), FULL_TYPE)],
         compiler_params=pltpu.CompilerParams(vmem_limit_bytes=40 << 20),
-        cost_estimate=hint(),
+        cost_estimate=cost(heads * tokens * tokens * 1000, query_rope, joint, query_nope),
     )(*places, key_rope, query_nope, query_rope, joint)
 
 
@@ -294,7 +294,7 @@
         ],
         scratch_shapes=[pltpu.VMEM((tokens, tokens), FULL_TYPE)],
         compiler_params=pltpu.CompilerParams(vmem_limit_bytes=40 << 20),
-        cost_estimate=hint(),
+        cost_estimate=cost(heads * tokens * tokens * 2000, joint, joint, grad_out, grad_out),
     )(*places, key_rope, query_nope, rotated, joint, grad_out, log_totals)
 
 
@@ -308,8 +308,9 @@
     )
 
 
-def hint():
-    return pl.CostEstimate(flops=1, bytes_accessed=1, transcendentals=0)
+def cost(flops, *arrays):
+    moved = sum(array.size * array.dtype.itemsize for array in arrays)
+    return pl.CostEstimate(flops=flops, bytes_accessed=moved, transcendentals=0)
 
 
 def feed_terms(gate_rows, up_rows, grad_act):
@@ -320,65 +321,77 @@
     return [value.astype(HALF_TYPE) for value in (activated, grad_gate, grad_act * silu)]
 
 
-def feed_kernel(normed, ffn_grad, gate, up, down, activated, grad_gate, grad_up):
+def feed_kernel(share, normed, ffn_grad, gate, up, down, activated, grad_gate, grad_up):
     gate_rows = kernel_dot(normed[...], gate[...], NN)
     up_rows = kernel_dot(normed[...], up[...], NN)
     grad_act = kernel_dot(ffn_grad[...], down[...], NN)
     activated[...], grad_gate[...], grad_up[...] = feed_terms(gate_rows, up_rows, grad_act)
 
 
-def feed_part(normed, ffn_grad, gathered, width):
+def feed_part(normed, ffn_grad, gathered, width, shares=1, share=0):
     tokens, depth = normed.shape
     tile = tile_of(width, 512)
     if tile is None:
-        gate, up, down = [gathered[:, index * width : (index + 1) * width] for index in range(3)]
+        gate, up, down = [
+            lax.dynamic_slice_in_dim(gathered, (index * shares + share) * width, width, 1)
+            for index in range(3)
+        ]
         return feed_terms(product(normed, gate), product(normed, up), product(ffn_grad, down))
     count = width // tile
-    whole = pl.BlockSpec((tokens, depth), lambda step: (0, 0))
-    part = lambda index: pl.BlockSpec((depth, tile), lambda step: (0, index * count + step))
+    whole = pl.BlockSpec((tokens, depth), lambda step, share: (0, 0))
+    part = lambda index: pl.BlockSpec(
+        (depth, tile), lambda step, share: (0, (index * shares + share[0]) * count + step)
+    )
     return pl.pallas_call(
         feed_kernel,
-        grid=(count,),
-        in_specs=[whole, whole, part(0), part(1), part(2)],
-        out_specs=[pl.BlockSpec((tokens, tile), lambda step: (0, step))] * 3,
+        grid_spec=pltpu.PrefetchScalarGridSpec(
+            num_scalar_prefetch=1,
+            grid=(count,),
+            in_specs=[whole, whole, part(0), part(1), part(2)],
+            out_specs=[pl.BlockSpec((tokens, tile), lambda step, share: (0, step))] * 3,
+        ),
         out_shape=[jax.ShapeDtypeStruct((tokens, width), HALF_TYPE)] * 3,
         compiler_params=pltpu.CompilerParams(vmem_limit_bytes=KERNEL_MEMORY),
-        cost_estimate=hint(),
-    )(normed, ffn_grad, gathered, gathered, gathered)
-
-
-def across_kernel(count, *refs):
+        cost_estimate=cost(6 * tokens * depth * width, normed, ffn_grad, gathered),
+    )(jnp.full((1,), share, jnp.int32), normed, ffn_grad, gathered, gathered, gathered)
+
+
+def across_kernel(count, share, *refs):
     total = kernel_dot(refs[0][...], refs[count][...], NT)
     for index in range(1, count):
         total = total + kernel_dot(refs[index][...], refs[count + index][...], NT)
-    for more in refs[2 * count : -1]:
-        total = total + more[...]
     refs[-1][...] = total.astype(refs[-1].dtype)
 
 
-def across_part(sides, places, gathered, earlier, kind):
+def across_part(sides, places, gathered, kind, shares=1, share=0):
     tokens, width = sides[0].shape
     depth = gathered.shape[0]
     if width % LANES:
         total = sum(
-            times_transposed(side, gathered[:, place * width : (place + 1) * width])
+            times_transposed(
+                side,
+                lax.dynamic_slice_in_dim(gathered, (place * shares + share) * width, width, 1),
+            )
             for side, place in zip(sides, places, strict=True)
         )
-        return sum(earlier, total).astype(kind)
+        return total.astype(kind)
     tile = tile_of(depth, 512)
-    block = pl.BlockSpec((tokens, tile), lambda step: (0, step))
-    rows = lambda place: pl.BlockSpec((tile, width), lambda step: (step, place))
+    rows = lambda place: pl.BlockSpec(
+        (tile, width), lambda step, share: (step, place * shares + share[0])
+    )
     return pl.pallas_call(
         functools.partial(across_kernel, len(sides)),
-        grid=(depth // tile,),
-        in_specs=[pl.BlockSpec((tokens, width), lambda step: (0, 0))] * len(sides)
-        + [rows(place) for place in places]
-        + [block] * len(earlier),
-        out_specs=block,
+        grid_spec=pltpu.PrefetchScalarGridSpec(
+            num_scalar_prefetch=1,
+            grid=(depth // tile,),
+            in_specs=[pl.BlockSpec((tokens, width), lambda step, share: (0, 0))] * len(sides)
+            + [rows(place) for place in places],
+            out_specs=pl.BlockSpec((tokens, tile), lambda step, share: (0, step)),
+        ),
         out_shape=jax.ShapeDtypeStruct((tokens, depth), kind),
         compiler_params=pltpu.CompilerParams(vmem_limit_bytes=KERNEL_MEMORY),
-        cost_estimate=hint(),
-    )(*sides, *[gathered] * len(sides), *earlier)
+        cost_estimate=cost(2 * len(sides) * tokens * depth * width, *sides),
+    )(jnp.full((1,), share, jnp.int32), *sides, *[gathered] * len(sides))
 
 
 def piece_kernel(places, left_side, right_side, *refs):
@@ -389,17 +402,19 @@
     refs[-1][...] = total.astype(HALF_TYPE)
 
 
-def piece_product(blocks, x_at, core_at, right_side, earlier):
-    z_size, _, _, rows, tokens = blocks.shape
+def piece_product(blocks, x_at, core_at, right_side, earlier, every_x=False):
+    z_size, x_count, _, rows, tokens = blocks.shape
+    x_count = x_count if every_x else 1
     width = right_side.shape[1]
     tile = tile_of(width, 1280)
     if tile is None or rows % 16:
         left_side = lax.dynamic_slice(
-            blocks, (0, x_at, core_at, 0, 0), (z_size, 1, 1, rows, tokens)
+            blocks, (0, x_at, core_at, 0, 0), (z_size, x_count, 1, rows, tokens)
         )
         total = product(left_side.reshape(-1, tokens), right_side)
         return sum([more.astype(FULL_TYPE) for more in earlier], total).astype(HALF_TYPE)
-    block = pl.BlockSpec((z_size * rows, tile), lambda step, places: (0, step))
+    height = z_size * x_count * rows
+    block = pl.BlockSpec((height, tile), lambda step, places: (0, step))
     return pl.pallas_call(
         piece_kernel,
         grid_spec=pltpu.PrefetchScalarGridSpec(
@@ -407,7 +422,7 @@
             grid=(width // tile,),
             in_specs=[
                 pl.BlockSpec(
-                    (z_size, 1, 1, rows, tokens),
+                    (z_size, x_count, 1, rows, tokens),
                     lambda step, places: (0, places[0], places[1], 0, 0),
                 ),
                 pl.BlockSpec((tokens, tile), lambda step, places: (0, step)),
@@ -415,9 +430,11 @@
             + [block] * len(earlier),
             out_specs=block,
         ),
-        out_shape=jax.ShapeDtypeStruct((z_size * rows, width), HALF_TYPE),
+        out_shape=jax.ShapeDtypeStruct((height, width), HALF_TYPE),
         compiler_params=pltpu.CompilerParams(vmem_limit_bytes=KERNEL_MEMORY),
-        cost_estimate=hint(),
+        cost_estimate=cost(
+            2 * height * tokens * width, right_side, right_side, right_side, *earlier
+        ),
     )(jnp.stack([x_at, core_at]).astype(jnp.int32), blocks, right_side, *earlier)
 
 
@@ -478,22 +495,44 @@
         )
         return found.astype(FULL_TYPE)
 
-    def over_z_direct(self, values, *earlier):
-        blocks = values.reshape((Z_SIZE, -1, values.shape[1]))
+    def by_core(self, halves, axis):
+        first = self.core == 0
+        keep = jnp.where(first, halves[0], halves[1])
+        came = self.move(jnp.where(first, halves[1], halves[0]), dc=1)
+        return jnp.concatenate(
+            [jnp.where(first, keep, came), jnp.where(first, came, keep)], axis=axis
+        )
+
+    def begun(self, values):
+        return self.move(values[:16, :LANES], dc=1)
+
+    def with_other(self, values):
+        return jnp.concatenate([values, self.move(values, dc=1)], axis=0)
+
+    def own_half(self, values, *earlier):
+        count = values.shape[0] // CORES
+        came = after(self.move(values[count:], dc=1), *earlier)
+        return values[:count].astype(FULL_TYPE) + came.astype(FULL_TYPE)
+
+    def x_last(self, values):
+        blocks = values.reshape((self.x_size, -1, values.shape[1]))
 
         def block(ahead):
             return lax.dynamic_index_in_dim(
-                blocks, lax.rem(self.z + ahead, Z_SIZE), 0, keepdims=False
+                blocks, lax.rem(self.x + ahead, self.x_size), 0, keepdims=False
             )
 
-        total = block(0).astype(FULL_TYPE)
-        for ahead in range(1, Z_SIZE):
-            came = after(self.move(block(ahead), dz=ahead), *earlier)
-            total = total + came.astype(FULL_TYPE)
+        total = block(self.x_size - 1)
+        for step in range(1, self.x_size):
+            came = self.move(total.astype(HALF_TYPE), dx=1)
+            total = came.astype(FULL_TYPE) + block(self.x_size - 1 - step)
         return total
 
 
 def after(values, *earlier):
+    if not earlier:
+        return values
+    values = lax.optimization_barrier((values, earlier))[0]
     return lax.optimization_barrier((values, earlier))[0]
 
 
@@ -516,17 +555,18 @@
         self.row = row
         self.terms = terms
 
-    def over_cores(self, dx):
-        other = self.row.move(self.terms(dx, 1, ()), dc=1)
-        return self.terms(dx, 0, (other,))
+    def share(self, *earlier):
+        terms = after(self.terms(self.row.x_size - 1, 1, ()), *earlier)
+        self.shared = self.row.move(terms, dc=1)
+        return terms
 
     def prepare(self):
-        self.total = self.over_cores(self.row.x_size - 1)
+        self.total = self.terms(self.row.x_size - 1, 0, (self.shared,))
         return self.total
 
     def send(self, *earlier, last=True):
         sent, self.came = self.row.x_link.send(self.total, *earlier, last=last)
-        return sent
+        return self.row.begun(sent)
 
     def hold(self):
         terms = self.terms(0, 1, ())
@@ -543,19 +583,59 @@
         return total
 
 
+class WideSum:
+    def __init__(self, row, terms):
+        self.row = row
+        self.terms = terms
+
+    def prepare(self):
+        self.total = self.terms(self.row.x_size - 1, 0, ())
+        return self.total
+
+    def send(self, *earlier):
+        sent, self.came = self.row.x_link.send(self.total, *earlier)
+        return self.row.begun(sent)
+
+    def finish(self, *earlier):
+        came = after(self.came, *earlier)
+        for dx in range(self.row.x_size - 2, -1, -1):
+            total = self.terms(dx, 0, (came,))
+            if dx:
+                came = self.row.move(total, dx=1)
+        return total
+
+
 class Terms:
-    def __init__(self, row, across, right_side):
+    def __init__(self, row, across, right_side, cores=CORES):
         self.row = row
-        self.blocks = across.reshape((Z_SIZE, row.x_size, CORES, -1, across.shape[1]))
+        self.cores = cores
+        self.blocks = across.reshape((Z_SIZE, row.x_size, cores, -1, across.shape[1]))
         self.right_side = right_side
 
     def __call__(self, dx, dc, earlier):
         x_at = lax.rem(self.row.x + dx, self.row.x_size)
-        core_at = lax.rem(self.row.core + dc, CORES)
+        core_at = lax.rem(self.row.core + dc, CORES) if self.cores > 1 else jnp.int32(0)
         return piece_product(self.blocks, x_at, core_at, self.right_side, earlier)
 
     def wait(self, *earlier):
         self.right_side = after(self.right_side, *earlier)
+
+    def every_x(self, dc, earlier):
+        core_at = lax.rem(self.row.core + dc, CORES)
+        return piece_product(
+            self.blocks, jnp.int32(0), core_at, self.right_side, earlier, every_x=True
+        )
+
+
+def terms_and_taken(terms, row, array, width):
+    total = terms.right_side.shape[1]
+
+    def both(dx, dc, earlier):
+        more = row.quarter(array, dx, dc).astype(HALF_TYPE)
+        more = jnp.pad(more, ((0, 0), (width, total - width - array.shape[1])))
+        return terms(dx, dc, (*earlier, more))
+
+    return both
 
 
 def taken_terms(row, rows_of):
@@ -773,6 +853,7 @@
         + [jnp.zeros((shard_rows, spare), HALF_TYPE)],
         axis=1,
     )
+    second_width = (ffn_width - first_width) // CORES
     packed_two = jnp.concatenate([weight[:, first_width:] for weight in ffn_weights], axis=1)
     gathered_one = lax.all_gather(packed_one, "row", axis=0, tiled=True)
     gathered_two = lax.all_gather(packed_two, "row", axis=0, tiled=True)
@@ -859,69 +940,87 @@
     scale_two = rms_scale(residual)
     normed_two = (residual * scale_two * gain_two).astype(HALF_TYPE)
     ffn_grad_across = ffn_grad.T
+    ffn_grad_pair = row.with_other(ffn_grad)
     normed_two_across = normed_two.T
     normed_one_across = normed_one.T
     activated, grad_gate, grad_up = feed_part(normed_two, ffn_grad, gathered_one, first_width)
     down_sum = Sum(row, Terms(row, ffn_grad_across, activated))
-    both_sum = Sum(
-        row, Terms(row, normed_two_across, jnp.concatenate([grad_gate, grad_up], axis=1))
-    )
+    both_terms = Terms(
+        row, normed_two_across, jnp.concatenate([grad_gate, grad_up], axis=1)
+    )
+    down_sum.share()
+    both_shared = both_terms.every_x(1, ())
     down_sum.prepare()
     down_sum.send()
-    both_sum.prepare()
-    held = (down_sum.hold(), both_sum.hold())
-    forward_one = across_part([activated], [2], gathered_one, [], FULL_TYPE)
-    backward_one = across_part([grad_gate, grad_up], [0, 1], gathered_one, [], FULL_TYPE)
-    both_sent = both_sum.send(held)
-    down_one = down_sum.finish(both_sent, forward_one, backward_one)
-    gathered_two = after(gathered_two, forward_one, backward_one, down_one)
+    both_total = both_terms.every_x(0, (row.move(both_shared, dc=1),))
+    both_found = row.over_z(both_total)
+    held = down_sum.hold()
+    forward_one = across_part([activated], [2], gathered_one, FULL_TYPE)
+    backward_one = across_part([grad_gate, grad_up], [0, 1], gathered_one, FULL_TYPE)
+    normed_pair = row.with_other(normed_two)
+    normed_pair_across = normed_pair.T
+    ffn_grad_pair_across = ffn_grad_pair.T
+    down_one = down_sum.finish(
+        both_total, forward_one, backward_one, normed_pair_across, ffn_grad_pair_across
+    )
+    down_one_grad = row.over_z(down_one)
+    gathered_two = after(gathered_two, down_one)
 
     activated, grad_gate, grad_up = feed_part(
-        normed_two, ffn_grad, gathered_two, ffn_width - first_width
-    )
-    down_terms = Terms(row, ffn_grad_across, activated)
-    gate_terms = Terms(row, normed_two_across, grad_gate)
-    up_terms = Terms(row, normed_two_across, grad_up)
-    down_sum = Sum(row, down_terms)
-    gate_sum = Sum(row, gate_terms)
-    up_sum = Sum(row, up_terms)
+        normed_pair, ffn_grad_pair, gathered_two, second_width, CORES, row.core
+    )
+    down_sum = WideSum(row, Terms(row, ffn_grad_pair_across, activated, 1))
+    gate_sum = WideSum(row, Terms(row, normed_pair_across, grad_gate, 1))
+    up_sum = WideSum(row, Terms(row, normed_pair_across, grad_up, 1))
     down_sum.prepare()
-    gate_total = gate_sum.prepare()
-    down_sent = down_sum.send(gate_total)
-
-    one_grads = row.over_z(jnp.concatenate([both_sum.finish(down_sent), down_one], axis=1))
+    down_sent = down_sum.send()
+
     grad_gate, grad_up = after((grad_gate, grad_up), down_sent)
     backward_two = across_part(
-        [grad_gate, grad_up], [0, 1], gathered_two, [backward_one], HALF_TYPE
-    )
-    up_terms.wait(backward_two)
+        [grad_gate, grad_up], [0, 1], gathered_two, HALF_TYPE, CORES, row.core
+    )
+    pair = col_send(row.own_half(backward_two) + backward_one, col_count)
+    y_sent = row.begun(pair[0])
+    gate_sum.terms.wait(y_sent)
+    gate_total = gate_sum.prepare()
+    up_sum.terms.wait(gate_total)
     up_total = up_sum.prepare()
-    grad_normed_two = col_send(backward_two, col_count)
     activated = after(activated, up_total)
-    forward_two = across_part([activated], [2], gathered_two, [forward_one], HALF_TYPE)
-    down_terms.wait(forward_two)
-    gate_terms.wait(forward_two)
-    held = (down_sum.hold(), gate_sum.hold())
-    gate_sent = gate_sum.send(up_total, held)
-
-    down_two = row.over_z(down_sum.finish(gate_sent))
-    grad_normed_two = col_sum(grad_normed_two, gate_sent)
+    forward_two = across_part([activated], [2], gathered_two, HALF_TYPE, CORES, row.core)
+    grad_normed_two = col_sum(pair, forward_two)
+    gate_sent = gate_sum.send(grad_normed_two)
+
+    down_total = down_sum.finish(gate_sent)
+    down_two = row.over_z(after(down_total, both_found))
+    one_grads = row.x_last(after(both_found, down_total))
+    grad_normed_two = after(grad_normed_two, down_total)
     through_two, gain_two_grad = rms_backward(grad_normed_two, residual, scale_two, gain_two)
     grad_residual = upstream + through_two
     branch_grad = (RESIDUAL_SCALE * grad_residual).astype(HALF_TYPE)
     out_sum = Sum(row, Terms(row, branch_grad.T, attended))
+    shared = out_sum.share()
     out_total = out_sum.prepare()
-    branch_grad = after(branch_grad, out_total)
+    out_sum.terms.wait(out_total)
+    held = out_sum.hold()
+    branch_grad = after(branch_grad, shared)
     grad_attended = product(branch_grad, out_all).astype(HALF_TYPE)
+    feed_forward = col_scatter(
+        row.own_half(after(forward_two, down_total)) + forward_one, col_count
+    )
+    residual_part = lax.dynamic_slice_in_dim(residual, col_start, width_share, 1)
+    output_rows = residual_part + RESIDUAL_SCALE * feed_forward
+    output_pad = product(row_matrix, output_rows.astype(HALF_TYPE)).astype(HALF_TYPE)
 
     grad_nope, grad_rope, grad_joint_full, grad_key = attention_backward(
         places, key_rope, query_nope, rotated, joint_full, grad_attended, log_totals, heads
     )
-    up_sent = up_sum.send(grad_joint_full)
+    up_sent = up_sum.send(grad_joint_full, held, output_pad, one_grads)
+
+    gate_total = gate_sum.finish(up_sent)
+    gate_two = row.over_z(gate_total)
     grad_nope, grad_rope, grad_joint_full = after(
-        (grad_nope, grad_rope, grad_joint_full), up_sent
-    )
-    gate_two = row.over_z(gate_sum.finish(up_sent))
+        (grad_nope, grad_rope, grad_joint_full), gate_total
+    )
     query_up_grad = jnp.concatenate(
         [contract_rows(query_normed, grad_nope), contract_rows(query_normed, grad_rope)], axis=1
     )
@@ -933,10 +1032,6 @@
         ],
         axis=1,
     )
-    up_terms.wait(grad_joint_full)
-    held = up_sum.hold()
-    heads_sum = Sum(row, taken_terms(row, lambda take: take(folded_grads)))
-    heads_total = heads_sum.prepare()
     latents = col_send(
         jnp.concatenate(
             [
@@ -949,6 +1044,9 @@
         ),
         col_count,
     )
+    heads_sum = Sum(row, taken_terms(row, lambda take: take(folded_grads)))
+    heads_sum.share()
+    heads_sum.hold()
     latents = col_sum(latents)
     grad_query_normed = latents[:, :Q_RANK]
     grad_compressed = latents[:, Q_RANK : Q_RANK + KV_RANK]
@@ -975,44 +1073,62 @@
         row_count,
         shard_rows,
     )
-    downs_sum = Sum(
-        row,
-        taken_terms(
-            row,
-            lambda take: jnp.concatenate(
-                [product(take(normed_one_across), grad_latents), take(gains_grad)], axis=1
-            ),
-        ),
-    )
-    downs_total = downs_sum.prepare()
-    out_sent = out_sum.send(heads_total, held, downs_total, last=False)
+    latent_width = grad_latents.shape[1] // col_count
+    latent_part = lax.dynamic_slice_in_dim(
+        grad_latents, col_index * latent_width, latent_width, 1
+    )
+    filled = -(latent_width + GAIN_LANES) % LANES + GAIN_LANES
+    downs_terms = Terms(
+        row, normed_one_across, jnp.pad(latent_part, ((0, 0), (0, filled)))
+    )
+    downs_sum = Sum(row, terms_and_taken(downs_terms, row, gains_grad, latent_width))
+    heads_total = heads_sum.prepare()
+    out_sent = out_sum.send(heads_total, last=False)
     heads_sent = heads_sum.send(last=False)
+
+    up_total = up_sum.finish(out_sent)
+    up_two = row.over_z(up_total)
+    downs_terms.wait(up_total, heads_sent)
+    downs_sum.share()
+    downs_sum.hold()
+    downs_sum.prepare()
     downs_sent = downs_sum.send(last=False)
-
-    up_two = row.over_z(up_sum.finish(out_sent))
     returned = lax.all_to_all(
-        after(grad_inputs, out_sent), "row", split_axis=0, concat_axis=0, tiled=True
-    )
+        after(grad_inputs, downs_sent), "row", split_axis=0, concat_axis=0, tiled=True
+    )
+    out_total = out_sum.finish(up_total)
     grad_tokens = contract_rows(send_matrix, returned).astype(HALF_TYPE)
-    feed_forward = col_scatter(after(forward_two, out_sent), col_count)
-    residual_part = lax.dynamic_slice_in_dim(residual, col_start, width_share, 1)
-    output_rows = residual_part + RESIDUAL_SCALE * feed_forward
-    output_pad = product(row_matrix, output_rows.astype(HALF_TYPE)).astype(HALF_TYPE)
-    out_sum.hold()
-    heads_sum.hold()
-    downs_sum.hold()
-    out_total = out_sum.finish(heads_sent, downs_sent)
-    heads_total = heads_sum.finish(downs_sent)
-    downs_total = downs_sum.finish()
-    out_grad = row.over_z_direct(out_total, downs_total)
-    heads_grad = row.over_z_direct(heads_total, downs_total)
-    downs_grad = row.over_z_direct(downs_total)
+    heads_total = heads_sum.finish(out_total, downs_sent)
+    downs_total = downs_sum.finish(heads_total)
+    last_grad = row.over_z(jnp.concatenate([out_total, heads_total, downs_total], axis=1))
     gate_grad, up_grad, down_grad = [
         jnp.concatenate(
-            [one_grads[:, index * first_width : (index + 1) * first_width], two], axis=1
+            [
+                one,
+                row.by_core(
+                    [two[:shard_rows].astype(HALF_TYPE), two[shard_rows:].astype(HALF_TYPE)],
+                    axis=1,
+                ).astype(FULL_TYPE),
+            ],
+            axis=1,
         )
-        for index, two in enumerate((gate_two, up_two, down_two))
+        for one, two in (
+            (one_grads[:, :first_width], gate_two),
+            (one_grads[:, first_width:], up_two),
+            (down_one_grad, down_two),
+        )
     ]
+    step_rates = learning_rates()
+    updated = {
+        slot: adam_update(params[slot], grad, firsts[slot], seconds[slot], step_rates[slot])
+        for slot, grad in ((5, gate_grad), (6, up_grad), (7, down_grad))
+    }
+    out_grad = last_grad[:, : out_total.shape[1]]
+    heads_grad = last_grad[:, out_total.shape[1] : -downs_total.shape[1]]
+    downs_part = last_grad[:, -downs_total.shape[1] :]
+    downs_grad = col_gather(downs_part[:, :latent_width].astype(HALF_TYPE), col_count)
+    downs_grad = downs_grad.astype(FULL_TYPE)
+    gains_found = downs_part[:, latent_width : latent_width + GAIN_LANES]
     query_fold = taken[3].shape[1]
     reduced = (
         downs_grad[:, :Q_RANK],
@@ -1025,13 +1141,12 @@
         gate_grad,
         up_grad,
         down_grad,
-        unfold_gains(downs_grad[:, Q_RANK + KV_RANK + ROPE :], 1, gain_count),
-    )
-    step_rates = learning_rates()
+        unfold_gains(gains_found, 1, gain_count),
+    )
     seconds_next = []
     weights_next = []
     for slot_index in range(9):
-        second_new, weight_new = adam_update(
+        second_new, weight_new = updated.get(slot_index) or adam_update(
             params[slot_index],
             reduced[slot_index],
             firsts[slot_index],

time: 922 us -> 911 us (0.988)
  starting transfers between devices: 62.2 us -> 43.4 us
  Pallas kernels: 237 us -> 220 us
  other arithmetic: 95.2 us -> 111 us
  waiting for transfers between devices: 353 us -> 363 us
    ppermute x33 -> x31, waiting for transfers between devices: 142 us -> 87.3 us  [move(): return lax.ppermute(values, 'row', pairs)]
    all_to_all x1, waiting for transfers between devices: 0.01 us -> 27.6 us  [body(): lax.all_to_all(after(grad_inputs, downs_sent), 'row', split_axis=0, conca...]
    ppermute x3, waiting for transfers between devices: 40.2 us -> 65.8 us  [col_send(): return (half, lax.ppermute(half, 'col', [(0, 1), (1, 0)]))]
    ppermute x33 -> x31, starting transfers between devices: 36.8 us -> 12.9 us  [move(): return lax.ppermute(values, 'row', pairs)]
    reduce_scatter x4 -> x6, waiting for transfers between devices: 0.03 us -> 19.7 us  [over_z(): lax.psum_scatter(values, 'row', scatter_dimension=0, axis_index_groups=li...]
    transpose x0 -> x2, local copies, waits for them, and re-layouts: none -> 12.6 us  [the longest x1 6.34 us: body(): ffn_grad_pair_across = ffn_grad_pair.T]
    pallas_call x24 -> x20, Pallas kernels: 121 us -> 109 us  [piece_product(): pl.pallas_call(piece_kernel, grid_spec=pltpu.PrefetchScalarGridSpec(num_s...]
    transpose x0 -> x2, other arithmetic: none -> 9.64 us  [the longest x1 4.99 us: body(): normed_pair_across = normed_pair.T]
  transfers between devices with their start and end apart: 48 -> 49, of which waited for: 17 -> 23; matrix products, arithmetic and copies ran while one was open for 20% -> 23% of each run, Pallas kernels for 25% -> 24%
where the time goes in v3:
time: 911 us; the launch traced here: 901 us
  waiting for transfers between devices  363 us (40%)
  Pallas kernels  220 us (24%)
  other arithmetic  111 us (12%)
  local copies, waits for them, and re-layouts  91 us (10%)
  matrix products  55.2 us (6%)
  starting transfers between devices  43.4 us (5%)
  between operations  17.5 us (2%)
    all_gather x1, waiting for transfers between devices, body(): gathered_one = lax.all_gather(packed_one, 'row', axis=0, tiled=True)  110 us
    pallas_call x20, Pallas kernels, piece_product(): pl.pallas_call(piece_kernel, grid_spec=pltpu.PrefetchScalarGridSpec(num_s...  109 us
    ppermute x31, waiting for transfers between devices, move(): return lax.ppermute(values, 'row', pairs)  87.3 us
    ppermute x3, waiting for transfers between devices, col_send(): return (half, lax.ppermute(half, 'col', [(0, 1), (1, 0)]))  65.8 us
    pallas_call x4, Pallas kernels, across_part(): pl.pallas_call(functools.partial(across_kernel, len(sides)), grid_spec=pl...  40.2 us
    all_to_all x1, waiting for transfers between devices, body(): lax.all_to_all(sorted_tokens, 'row', split_axis=0, concat_axis=0, tiled=T...  35.5 us
    pallas_call x2, Pallas kernels, feed_part(): pl.pallas_call(feed_kernel, grid_spec=pltpu.PrefetchScalarGridSpec(num_sc...  35.4 us
    all_to_all x1, waiting for transfers between devices, body(): lax.all_to_all(after(grad_inputs, downs_sent), 'row', split_axis=0, conca...  27.6 us
  transfers between devices with their start and end apart: 49, of which 23 were waited for; matrix products, arithmetic and copies ran while one was open for 23% of the time, Pallas kernels for 24%

profile of v3, /device:TPU:0, one launch (start us, length us, event | category | flops | bytes accessed | tf_op | source)
XLA Modules:
  0.0 900.5 jit_solution(4256737619936574769)
XLA Ops:
  31.1 7.4 all-to-all-start.1
  40.9 35.5 %all-to-all-done.1 = bf16[16,24,1280]{2,1,0:T(8,128)(2,1)} async-done(((bf16[16,24,1280]{2,1,0:T(8,128)(2,1)}), bf16[16,24,1280]{2,1,0:T(8,128)(2,1)}, u32[]{:S(2)}, u32[]{:S(2)}) %all-to-all-start.1) | async-done | bytes 983072 | tf_op jit(solution)/shard_map/all_to_all | solution.py:887
  93.5 11.5 %collective-permute-done = bf16[384,1280]{1,0:T(8,128)(2,1)} collective-permute-done((bf16[384,1280]{1,0:T(8,128)(2,1)}, bf16[384,1280]{1,0:T(8,128)(2,1)}, u32[]{:S(2)}, u32[]{:S(2)}) %collective-permute-start) | collective-permute-done | bytes 983072 | tf_op jit(solution)/shard_map/ppermute | solution.py:663
  107.9 109.9 %all-gather.3.cloned.1.call-done.gate.up.down.refs_1_.refs_2_.refs_3_ = bf16[2560,6784]{1,0:T(8,128)(2,1)} async-done(((bf16[160,6784]{1,0:T(8,128)(2,1)}), bf16[2560,6784]{1,0:T(8,128)(2,1)}) %all-gather.3.cloned.1.call-update) | async-done | bytes 34734096 | tf_op jit(solution)/shard_map/all_gather | solution.py:858
  236.5 14.1 %shard_map.518 = (bf16[384,1280]{1,0:T(8,128)(2,1)S(1)}, bf16[384,640]{1,0:T(8,128)(2,1)S(1)}, f32[5,4,384]{2,1,0:T(4,128)S(1)}) custom-call(s32[384,1]{1,0:T(8,128)S(1)} %broadcast_in_dim.46.row_here, s32[1,384]{1,0:T(1,128)S(1)} %broadcast_in_dim.39.row_across, s32[1,384]{1,0:T(1,128)S(1)} %broadcast_in_dim.41.first_across, f32[384,128]{1,0:T(8,128)S(1)} %copy.229.cosine, ...), custom_call_target="tpu_custom_call" | custom-call | flops 2949120000 | bytes 3932160 | tf_op jit(solution)/shard_map/pallas_call | solution.py:258
  250.7 8.9 fusion.4
  265.9 39.0 %collective-permute-done.1 = bf16[384,2560]{1,0:T(8,128)(2,1)} collective-permute-done((bf16[384,2560]{1,0:T(8,128)(2,1)}, bf16[384,2560]{1,0:T(8,128)(2,1)}, u32[]{:S(2)}, u32[]{:S(2)}) %collective-permute-start.1) | collective-permute-done | bytes 1966112 | tf_op jit(solution)/shard_map/ppermute | solution.py:674
  316.6 15.0 %shard_map.519 = (bf16[384,1152]{1,0:T(8,128)(2,1)}, bf16[384,1152]{1,0:T(8,128)(2,1)}, bf16[384,1152]{1,0:T(8,128)(2,1)}) custom-call(s32[1]{0:T(128)} %constant.201.clone.1.share, bf16[384,2560]{1,0:T(8,128)(2,1)} %multiply_convert_fusion.1.normed, bf16[384,2560]{1,0:T(8,128)(2,1)} %get-tuple-element.233.ffn_grad, ...), custom_call_target="tpu_custom_call" | custom-call | flops 6794772480 | bytes 38666240 | tf_op jit(solution)/shard_map/pallas_call | solution.py:345
  334.4 7.6 shard_map.523
  343.1 11.4 %collective-permute-done.8.refs_0_ = bf16[1280,2304]{1,0:T(8,128)(2,1)} collective-permute-done((bf16[1280,2304]{1,0:T(8,128)(2,1)}, bf16[1280,2304]{1,0:T(8,128)(2,1)}, u32[]{:S(2)}, u32[]{:S(2)}) %collective-permute-start.8) | collective-permute-done | bytes 5898272 | tf_op jit(solution)/shard_map/ppermute | solution.py:461
  354.5 8.4 shard_map.524
  397.4 7.7 shard_map.525
  405.2 10.6 %shard_map.526 = f32[384,2560]{1,0:T(8,128)} custom-call(s32[1]{0:T(128)} %constant.201.clone.1.share, bf16[384,1152]{1,0:T(8,128)(2,1)} %get-tuple-element.106.refs_0_, bf16[384,1152]{1,0:T(8,128)(2,1)} %get-tuple-element.107.refs_1_, bf16[2560,6784]{1,0:T(8,128)(2,1)} %all-gather.3.cloned.1.call-done.gate.up.down.refs_1_.refs_2_.refs_3_, ...), custom_call_target="tpu_custom_call" | custom-call | flops 4529848320 | bytes 1769472 | tf_op jit(solution)/shard_map/pallas_call | solution.py:382
  425.8 20.5 %shard_map.528 = (bf16[768,1024]{1,0:T(8,128)(2,1)}, bf16[768,1024]{1,0:T(8,128)(2,1)}, bf16[768,1024]{1,0:T(8,128)(2,1)}) custom-call(s32[1]{0:T(128)} %bitcast.42.share, bf16[768,2560]{1,0:T(8,128)(2,1)} %get-tuple-element.225.normed, bf16[768,2560]{1,0:T(8,128)(2,1)} %get-tuple-element.223.ffn_grad, ...), custom_call_target="tpu_custom_call" | custom-call | flops 12079595520 | bytes 39321600 | tf_op jit(solution)/shard_map/pallas_call | solution.py:345
  446.3 6.4 shard_map.529
  454.5 13.1 %shard_map.530 = bf16[768,2560]{1,0:T(8,128)(2,1)} custom-call(s32[1]{0:T(128)} %bitcast.42.share, bf16[768,1024]{1,0:T(8,128)(2,1)} %get-tuple-element.122.refs_0_.right_side, bf16[768,1024]{1,0:T(8,128)(2,1)} %get-tuple-element.124.refs_1_.right_side, bf16[2560,6144]{1,0:T(8,128)(2,1)} %all-gather.5.cloned.1.call-done.gate.up.down.refs_2_.refs_3_.refs_1_, ...), custom_call_target="tpu_custom_call" | custom-call | flops 8053063680 | bytes 3145728 | tf_op jit(solution)/shard_map/pallas_call | solution.py:382
  496.3 8.8 shard_map.533
  505.1 15.9 %collective-permute-done.13 = bf16[384,2560]{1,0:T(8,128)(2,1)} collective-permute-done((bf16[384,2560]{1,0:T(8,128)(2,1)S(1)}, bf16[384,2560]{1,0:T(8,128)(2,1)}, u32[]{:S(2)}, u32[]{:S(2)}) %collective-permute-start.13) | collective-permute-done | bytes 1966112 | tf_op jit(solution)/shard_map/ppermute | solution.py:674
  525.0 11.0 %collective-permute-done.12.refs_0_ = bf16[1280,1024]{1,0:T(8,128)(2,1)} collective-permute-done((bf16[1280,1024]{1,0:T(8,128)(2,1)}, bf16[1280,1024]{1,0:T(8,128)(2,1)}, u32[]{:S(2)}, u32[]{:S(2)}) %collective-permute-start.12) | collective-permute-done | bytes 2621472 | tf_op jit(solution)/shard_map/ppermute | solution.py:461
  537.9 7.2 shard_map.534
  583.6 20.9 %shard_map.536 = (bf16[384,1280]{1,0:T(8,128)(2,1)S(1)}, bf16[384,640]{1,0:T(8,128)(2,1)S(1)}, bf16[384,2560]{1,0:T(8,128)(2,1)S(1)}, f32[384,32]{1,0:T(8,128)S(1)}) custom-call(s32[384,1]{1,0:T(8,128)S(1)} %copy-done.6, s32[1,384]{1,0:T(1,128)S(1)} %copy-done.10, s32[1,384]{1,0:T(1,128)S(1)} %copy-done.12, f32[384,128]{1,0:T(8,128)S(1)} %copy.229.cosine, ...), custom_call_target="tpu_custom_call" | custom-call | flops 5898240000 | bytes 5898240 | tf_op jit(solution)/shard_map/pallas_call | solution.py:278
  628.4 7.3 shard_map.539
  656.2 11.0 %collective-permute-done.21 = bf16[384,1056]{0,1:T(8,128)(2,1)} collective-permute-done((bf16[384,1056]{0,1:T(8,128)(2,1)}, bf16[384,1056]{0,1:T(8,128)(2,1)}, u32[]{:S(2)}, u32[]{:S(2)}) %collective-permute-start.21) | collective-permute-done | bytes 811040 | tf_op jit(solution)/shard_map/ppermute | solution.py:674
  674.8 12.8 %collective-permute-done.22.refs_0_ = bf16[1280,1024]{1,0:T(8,128)(2,1)} collective-permute-done((bf16[1280,1024]{1,0:T(8,128)(2,1)}, bf16[1280,1024]{1,0:T(8,128)(2,1)}, u32[]{:S(2)}, u32[]{:S(2)}) %collective-permute-start.22) | collective-permute-done | bytes 2621472 | tf_op jit(solution)/shard_map/ppermute | solution.py:461
  689.5 7.2 shard_map.540
  733.0 8.4 collective-permute-done.29.refs_1_
  749.2 16.9 %collective-permute-done.31 = bf16[640,896]{1,0:T(8,128)(2,1)} collective-permute-done((bf16[640,896]{1,0:T(8,128)(2,1)S(1)}, bf16[640,896]{1,0:T(8,128)(2,1)}, u32[]{:S(2)}, u32[]{:S(2)}) %collective-permute-start.31) | collective-permute-done | bytes 1146912 | tf_op jit(solution)/shard_map/ppermute | solution.py:461
  768.1 14.7 %collective-permute-done.33.refs_1_ = bf16[640,640]{1,0:T(8,128)(2,1)} collective-permute-done((bf16[640,640]{1,0:T(8,128)(2,1)}, bf16[640,640]{1,0:T(8,128)(2,1)}, u32[]{:S(2)}, u32[]{:S(2)}) %collective-permute-start.33) | collective-permute-done | bytes 819232 | tf_op jit(solution)/shard_map/ppermute | solution.py:461
  795.1 9.7 %all-to-all-start.2 = ((bf16[16,24,1280]{2,1,0:T(8,128)(2,1)}), bf16[16,24,1280]{2,1,0:T(8,128)(2,1)}, u32[]{:S(2)}, u32[]{:S(2)}) async-start(bf16[16,24,1280]{2,1,0:T(8,128)(2,1)} %bitcast.80), calls=%async_computation.3 | async-start | bytes 1966080 | tf_op jit(solution)/shard_map/all_to_all | solution.py:1096
  815.2 27.6 %all-to-all-done.2 = bf16[16,24,1280]{2,1,0:T(8,128)(2,1)} async-done(((bf16[16,24,1280]{2,1,0:T(8,128)(2,1)}), bf16[16,24,1280]{2,1,0:T(8,128)(2,1)}, u32[]{:S(2)}, u32[]{:S(2)}) %all-to-all-start.2) | async-done | bytes 983072 | tf_op jit(solution)/shard_map/all_to_all | solution.py:1096
  849.8 7.5 multiply_subtract_fusion.1
  857.3 19.7 %reduce-scatter.9.cloned.1.call-done = bf16[160,2816]{1,0:T(8,128)(2,1)} async-done(((bf16[640,2816]{1,0:T(8,128)(2,1)}), bf16[160,2816]{1,0:T(8,128)(2,1)}) %reduce-scatter.9.cloned.1.call-update) | async-done | bytes 901136 | tf_op jit(solution)/shard_map/reduce_scatter | solution.py:493
  (633 shorter events, 349.3 us)
Async XLA Ops:
  7.2 210.5 %all-gather.3.cloned.1.call-start = ((), (), s32[]{:S(2)}) async-start(), calls=%async_computation.9 | async-start | bytes 36904960 | tf_op jit(solution)/shard_map/all_gather | solution.py:858
  25.4 400.4 %all-gather.5.cloned.1.call-start = ((), (), s32[]{:S(2)}) async-start(), calls=%async_computation.10 | async-start | bytes 33423360 | tf_op jit(solution)/shard_map/all_gather | solution.py:859
  31.1 45.2 %all-to-all-start.1 = ((bf16[16,24,1280]{2,1,0:T(8,128)(2,1)}), bf16[16,24,1280]{2,1,0:T(8,128)(2,1)}, u32[]{:S(2)}, u32[]{:S(2)}) async-start(bf16[16,24,1280]{2,1,0:T(8,128)(2,1)} %bitcast), calls=%async_computation.1 | async-start | bytes 1966080 | tf_op jit(solution)/shard_map/all_to_all | solution.py:887
  79.8 465.3 %reduce-scatter.7.cloned.1.call-start = ((), (), s32[]{:S(2)}) async-start(), calls=%async_computation.11 | async-start | bytes 7372800 | tf_op jit(solution)/shard_map/reduce_scatter | solution.py:493
  80.1 25.0 %collective-permute-start = (bf16[384,1280]{1,0:T(8,128)(2,1)}, bf16[384,1280]{1,0:T(8,128)(2,1)}, u32[]{:S(2)}, u32[]{:S(2)}) collective-permute-start(bf16[384,1280]{1,0:T(8,128)(2,1)} %bitcast.1), channel_id=1, source_target_pairs={{0,1},{1,0},{2,3},{3,2},{4,5},{5,4},{6,7},{7,6},{8,9},{9,8},{10,11... | collective-permute-start | bytes 2949128 | tf_op jit(solution)/shard_map/ppermute | solution.py:663
  92.0 169.7 %collective-permute-start.3 = (bf16[384,1280]{1,0:T(8,128)(2,1)}, bf16[384,1280]{1,0:T(8,128)(2,1)}, u32[]{:S(2)}, u32[]{:S(2)}) collective-permute-start(bf16[384,1280]{1,0:T(8,128)(2,1)} %convolution_convert_fusion.4), channel_id=1, source_target_pairs={{0,1},{1,0},{2,3},{3,2},{4,5},{5,4},{6,7},{7,6},{8,9},{9,8},{10,11... | collective-permute-start | bytes 2949128 | tf_op jit(solution)/shard_map/ppermute | solution.py:663
  259.6 45.3 %collective-permute-start.1 = (bf16[384,2560]{1,0:T(8,128)(2,1)}, bf16[384,2560]{1,0:T(8,128)(2,1)}, u32[]{:S(2)}, u32[]{:S(2)}) collective-permute-start(bf16[384,2560]{1,0:T(8,128)(2,1)} %fusion.4), channel_id=1, source_target_pairs={{0,1},{1,0},{2,3},{3,2},{4,5},{5,4},{6,7},{7,6},{8,9},{9,8},{10,11... | collective-permute-start | bytes 5898248 | tf_op jit(solution)/shard_map/ppermute | solution.py:674
  342.6 43.9 %collective-permute-start.4 = (bf16[384,2560]{1,0:T(8,128)(2,1)S(1)}, bf16[384,2560]{1,0:T(8,128)(2,1)}, u32[]{:S(2)}, u32[]{:S(2)}) collective-permute-start(bf16[384,2560]{1,0:T(8,128)(2,1)S(1)} %copy-done.22), channel_id=1, source_target_pairs={{0,2},{2,0},{4,6},{6,4},{8,10},{10,8},{12,14},{14,12},{16,18},{18,... | collective-permute-start | bytes 5898248 | tf_op jit(solution)/shard_map/ppermute | solution.py:461
  362.9 441.9 %reduce-scatter.17.cloned.1.call-start = ((), (), s32[]{:S(2)}) async-start(), calls=%async_computation.16 | async-start | bytes 3276800 | tf_op jit(solution)/shard_map/reduce_scatter | solution.py:493
  372.0 43.8 %collective-permute-start.2 = (bf16[384,2560]{1,0:T(8,128)(2,1)}, bf16[384,2560]{1,0:T(8,128)(2,1)}, u32[]{:S(2)}, u32[]{:S(2)}) collective-permute-start(bf16[384,2560]{1,0:T(8,128)(2,1)} %multiply_convert_fusion.1.normed), channel_id=1, source_target_pairs={{0,2},{2,0},{4,6},{6,4},{8,10},{10,8},{12,14},{14,12},{16,18},{18,... | collective-permute-start | bytes 5898248 | tf_op jit(solution)/shard_map/ppermute | solution.py:461
  379.0 41.7 %collective-permute-start.5 = (bf16[640,1152]{1,0:T(8,128)(2,1)}, bf16[640,1152]{1,0:T(8,128)(2,1)}, u32[]{:S(2)}, u32[]{:S(2)}) collective-permute-start(bf16[640,1152]{1,0:T(8,128)(2,1)} %shard_map.520), channel_id=1, source_target_pairs={{0,2},{2,0},{4,6},{6,4},{8,10},{10,8},{12,14},{14,12},{16,18},{18,... | collective-permute-start | bytes 4423688 | tf_op jit(solution)/shard_map/ppermute | solution.py:461
  383.6 37.2 %collective-permute-start.7 = (bf16[640,1152]{1,0:T(8,128)(2,1)}, bf16[640,1152]{1,0:T(8,128)(2,1)}, u32[]{:S(2)}, u32[]{:S(2)}) collective-permute-start(bf16[640,1152]{1,0:T(8,128)(2,1)} %shard_map.522), channel_id=1, source_target_pairs={{0,4},{2,6},{4,0},{6,2},{8,12},{10,14},{12,8},{14,10},{16,20},{18,... | collective-permute-start | bytes 4423688 | tf_op jit(solution)/shard_map/ppermute | solution.py:461
  475.9 45.2 %collective-permute-start.13 = (bf16[384,2560]{1,0:T(8,128)(2,1)S(1)}, bf16[384,2560]{1,0:T(8,128)(2,1)}, u32[]{:S(2)}, u32[]{:S(2)}) collective-permute-start(bf16[384,2560]{1,0:T(8,128)(2,1)S(1)} %add_convert_fusion.1), channel_id=1, source_target_pairs={{0,1},{1,0},{2,3},{3,2},{4,5},{5,4},{6,7},{7,6},{8,9},{9,8},{10,11... | collective-permute-start | bytes 5898248 | tf_op jit(solution)/shard_map/ppermute | solution.py:674
  476.9 59.1 %collective-permute-start.12 = (bf16[1280,1024]{1,0:T(8,128)(2,1)}, bf16[1280,1024]{1,0:T(8,128)(2,1)}, u32[]{:S(2)}, u32[]{:S(2)}) collective-permute-start(bf16[1280,1024]{1,0:T(8,128)(2,1)} %shard_map.529), channel_id=1, source_target_pairs={{0,4},{2,6},{4,0},{6,2},{8,12},{10,14},{12,8},{14,10},{16,20},{18,... | collective-permute-start | bytes 7864328 | tf_op jit(solution)/shard_map/ppermute | solution.py:461
  548.4 259.5 %reduce-scatter.15.cloned.1.call-start = ((), (), s32[]{:S(2)}) async-start(), calls=%async_computation.15 | async-start | bytes 1843200 | tf_op jit(solution)/shard_map/reduce_scatter | solution.py:493
  549.0 264.3 %reduce-scatter.11.cloned.1.call-start = ((), (), s32[]{:S(2)}) async-start(), calls=%async_computation.13 | async-start | bytes 3276800 | tf_op jit(solution)/shard_map/reduce_scatter | solution.py:493
  549.0 77.5 %collective-permute-start.17 = (bf16[1280,1024]{1,0:T(8,128)(2,1)}, bf16[1280,1024]{1,0:T(8,128)(2,1)}, u32[]{:S(2)}, u32[]{:S(2)}) collective-permute-start(bf16[1280,1024]{1,0:T(8,128)(2,1)} %shard_map.531), channel_id=1, source_target_pairs={{0,4},{2,6},{4,0},{6,2},{8,12},{10,14},{12,8},{14,10},{16,20},{18,... | collective-permute-start | bytes 7864328 | tf_op jit(solution)/shard_map/ppermute | solution.py:461
  569.4 36.1 %collective-permute-start.18 = (bf16[640,1280]{1,0:T(8,128)(2,1)}, bf16[640,1280]{1,0:T(8,128)(2,1)}, u32[]{:S(2)}, u32[]{:S(2)}) collective-permute-start(bf16[640,1280]{1,0:T(8,128)(2,1)} %shard_map.535), channel_id=1, source_target_pairs={{0,2},{2,0},{4,6},{6,4},{8,10},{10,8},{12,14},{14,12},{16,18},{18,... | collective-permute-start | bytes 4915208 | tf_op jit(solution)/shard_map/ppermute | solution.py:461
  578.5 36.0 %collective-permute-start.16 = (bf16[384,1280]{1,0:T(8,128)(2,1)}, bf16[384,1280]{1,0:T(8,128)(2,1)}, u32[]{:S(2)}, u32[]{:S(2)}) collective-permute-start(bf16[384,1280]{1,0:T(8,128)(2,1)} %broadcast_select_fusion), channel_id=1, source_target_pairs={{0,1},{1,0},{2,3},{3,2},{4,5},{5,4},{6,7},{7,6},{8,9},{9,8},{10,11... | collective-permute-start | bytes 2949128 | tf_op jit(solution)/shard_map/ppermute | solution.py:656
  581.9 42.3 %collective-permute-start.19 = (bf16[160,2304]{1,0:T(8,128)(2,1)}, bf16[160,2304]{1,0:T(8,128)(2,1)}, u32[]{:S(2)}, u32[]{:S(2)}) collective-permute-start(bf16[160,2304]{1,0:T(8,128)(2,1)} %fusion.41), channel_id=1, source_target_pairs={{0,4},{2,6},{4,0},{6,2},{8,12},{10,14},{12,8},{14,10},{16,20},{18,... | collective-permute-start | bytes 2211848 | tf_op jit(solution)/shard_map/ppermute | solution.py:461
  628.0 59.7 %collective-permute-start.22 = (bf16[1280,1024]{1,0:T(8,128)(2,1)}, bf16[1280,1024]{1,0:T(8,128)(2,1)}, u32[]{:S(2)}, u32[]{:S(2)}) collective-permute-start(bf16[1280,1024]{1,0:T(8,128)(2,1)} %shard_map.532), channel_id=1, source_target_pairs={{0,4},{2,6},{4,0},{6,2},{8,12},{10,14},{12,8},{14,10},{16,20},{18,... | collective-permute-start | bytes 7864328 | tf_op jit(solution)/shard_map/ppermute | solution.py:461
  640.6 205.3 %reduce-scatter.13.cloned.1.call-start = ((), (), s32[]{:S(2)}) async-start(), calls=%async_computation.14 | async-start | bytes 3276800 | tf_op jit(solution)/shard_map/reduce_scatter | solution.py:493
  646.7 20.5 %collective-permute-start.21 = (bf16[384,1056]{0,1:T(8,128)(2,1)}, bf16[384,1056]{0,1:T(8,128)(2,1)}, u32[]{:S(2)}, u32[]{:S(2)}) collective-permute-start(bf16[384,1056]{0,1:T(8,128)(2,1)} %copy.240), channel_id=1, source_target_pairs={{0,1},{1,0},{2,3},{3,2},{4,5},{5,4},{6,7},{7,6},{8,9},{9,8},{10,11... | collective-permute-start | bytes 2433032 | tf_op jit(solution)/shard_map/ppermute | solution.py:674
  655.7 87.7 %collective-permute-start.28 = (bf16[640,1280]{1,0:T(8,128)(2,1)}, bf16[640,1280]{1,0:T(8,128)(2,1)}, u32[]{:S(2)}, u32[]{:S(2)}) collective-permute-start(bf16[640,1280]{1,0:T(8,128)(2,1)} %shard_map.538), channel_id=1, source_target_pairs={{0,2},{2,0},{4,6},{6,4},{8,10},{10,8},{12,14},{14,12},{16,18},{18,... | collective-permute-start | bytes 4915208 | tf_op jit(solution)/shard_map/ppermute | solution.py:461
  696.7 180.3 %reduce-scatter.9.cloned.1.call-start = ((), (), s32[]{:S(2)}) async-start(), calls=%async_computation.12 | async-start | bytes 4505600 | tf_op jit(solution)/shard_map/reduce_scatter | solution.py:493
  702.5 39.0 %collective-permute-start.29 = (bf16[640,1280]{1,0:T(8,128)(2,1)}, bf16[640,1280]{1,0:T(8,128)(2,1)}, u32[]{:S(2)}, u32[]{:S(2)}) collective-permute-start(bf16[640,1280]{1,0:T(8,128)(2,1)} %shard_map.537), channel_id=1, source_target_pairs={{0,4},{2,6},{4,0},{6,2},{8,12},{10,14},{12,8},{14,10},{16,20},{18,... | collective-permute-start | bytes 4915208 | tf_op jit(solution)/shard_map/ppermute | solution.py:461
  721.1 45.0 %collective-permute-start.31 = (bf16[640,896]{1,0:T(8,128)(2,1)S(1)}, bf16[640,896]{1,0:T(8,128)(2,1)}, u32[]{:S(2)}, u32[]{:S(2)}) collective-permute-start(bf16[640,896]{1,0:T(8,128)(2,1)S(1)} %copy-done.79), channel_id=1, source_target_pairs={{0,4},{2,6},{4,0},{6,2},{8,12},{10,14},{12,8},{14,10},{16,20},{18,... | collective-permute-start | bytes 3440648 | tf_op jit(solution)/shard_map/ppermute | solution.py:461
  722.8 43.3 %collective-permute-start.30 = (bf16[640,896]{1,0:T(8,128)(2,1)}, bf16[640,896]{1,0:T(8,128)(2,1)}, u32[]{:S(2)}, u32[]{:S(2)}) collective-permute-start(bf16[640,896]{1,0:T(8,128)(2,1)} %bitcast.83), channel_id=1, source_target_pairs={{0,2},{2,0},{4,6},{6,4},{8,10},{10,8},{12,14},{14,12},{16,18},{18,... | collective-permute-start | bytes 3440648 | tf_op jit(solution)/shard_map/ppermute | solution.py:461
  729.0 53.8 %collective-permute-start.33 = (bf16[640,640]{1,0:T(8,128)(2,1)}, bf16[640,640]{1,0:T(8,128)(2,1)}, u32[]{:S(2)}, u32[]{:S(2)}) collective-permute-start(bf16[640,640]{1,0:T(8,128)(2,1)} %shard_map.542), channel_id=1, source_target_pairs={{0,4},{2,6},{4,0},{6,2},{8,12},{10,14},{12,8},{14,10},{16,20},{18,... | collective-permute-start | bytes 2457608 | tf_op jit(solution)/shard_map/ppermute | solution.py:461
  741.5 41.4 %collective-permute-start.32 = (bf16[640,640]{1,0:T(8,128)(2,1)}, bf16[640,640]{1,0:T(8,128)(2,1)}, u32[]{:S(2)}, u32[]{:S(2)}) collective-permute-start(bf16[640,640]{1,0:T(8,128)(2,1)} %shard_map.544), channel_id=1, source_target_pairs={{0,2},{2,0},{4,6},{6,4},{8,10},{10,8},{12,14},{14,12},{16,18},{18,... | collective-permute-start | bytes 2457608 | tf_op jit(solution)/shard_map/ppermute | solution.py:461
  795.1 47.7 %all-to-all-start.2 = ((bf16[16,24,1280]{2,1,0:T(8,128)(2,1)}), bf16[16,24,1280]{2,1,0:T(8,128)(2,1)}, u32[]{:S(2)}, u32[]{:S(2)}) async-start(bf16[16,24,1280]{2,1,0:T(8,128)(2,1)} %bitcast.80), calls=%async_computation.3 | async-start | bytes 1966080 | tf_op jit(solution)/shard_map/all_to_all | solution.py:1096
  814.4 32.7 %collective-permute-start.35 = (bf16[160,1024]{1,0:T(8,128)(2,1)S(1)}, bf16[160,1024]{1,0:T(8,128)(2,1)S(1)}, u32[]{:S(2)}, u32[]{:S(2)}) collective-permute-start(bf16[160,1024]{1,0:T(8,128)(2,1)S(1)} %broadcast_select_fusion.15), channel_id=1, source_target_pairs={{0,2},{2,0},{4,6},{6,4},{8,10},{10,8},{12,14},{14,12},{16,18},{18,... | collective-permute-start | bytes 983048 | tf_op jit(solution)/shard_map/ppermute | solution.py:461
  (156 other events, 1823.8 us)
Sparse Core Ops, SparseCore 0:
  25.5 192.2 all-gather.2
  219.9 163.2 all-gather.4
  385.5 104.6 reduce-scatter.6
  548.5 55.7 reduce-scatter.16
  607.0 33.4 reduce-scatter.14
  642.7 54.5 reduce-scatter.10
  699.8 52.8 reduce-scatter.12
  790.2 86.7 reduce-scatter.8
